TPU v7x, 32 devices: a whole 2x2x4 slice. The times are simulated.
32 devices in a mesh: pa: 4 (over y, core), pb: 8 (over z, x).
Axes of the slice: x: 2, y: 2, z: 4, core: 2. Of those that a mesh axis runs over, the one named last changes fastest.
Arguments:
- velocity: float32 [3, 2048, 32, 1024], P(None, ('pa', 'pb')), may hold values from -6 to 6
- fluid: float32 [2048, 32, 1024], P(('pa', 'pb')), may hold values from 0.25 to 1
- block_place: int32 [2048], P(('pa', 'pb')), may hold values from 0 to 63, as said below
Outputs:
- velocity_next: float32 [3, 2048, 32, 1024], P(None, ('pa', 'pb'))
- pressure: float32 [2048, 32, 1024], P(('pa', 'pb'))
Inputs may be any that keep to these rules, and one draw needn't show every extreme that they name: `block_place`: within each device's 64 consecutive slots every tile position appears exactly once.
All inputs are finite; a program needn't handle non-finite values.
Results may differ from a plain program's by a relative error of at most 0.0015.
Values sent between devices are 32-bit elements; how exact they have to be, the bound alone decides.
No kernel may reach another device: no remote copies, remote signals or barrier semaphores. Data moves between devices by JAX's collectives and lax.ppermute only.
A program may use at most 448 MiB of HBM per device.

v0:
```python
import jax
import jax.numpy as jnp
from jax import lax
from jax.sharding import PartitionSpec as P

NX = 2048
NY = 1024
NZ = 32
B = 32


step_size = 0.25
viscosity = 0.1
highest = lax.Precision.HIGHEST


def extended(array, sides, width):
    for axis, dim in sides:
        peers, length = (lax.axis_size(axis), array.shape[dim])
        up = [(i, (i + 1) % peers) for i in range(peers - 1)]
        down = [(j, i) for i, j in up]
        last = lax.slice_in_dim(array, length - width, length, axis=dim)
        first = lax.slice_in_dim(array, 0, width, axis=dim)
        before = lax.ppermute(last, axis, up)
        after = lax.ppermute(first, axis, down)
        array = jnp.concatenate([before, array, after], axis=dim)
    return array


def advance_one(center, flow_center, lower_side, upper_side, fraction):
    diffusion = (
        lower_side[0]
        + upper_side[0]
        + lower_side[1]
        + upper_side[1]
        + lower_side[2]
        + upper_side[2]
        - 6.0 * center
    )
    transport = (
        flow_center[0] * (upper_side[0] - lower_side[0])
        + flow_center[1] * (upper_side[1] - lower_side[1])
        + flow_center[2] * (upper_side[2] - lower_side[2])
    )
    return fraction * (center + step_size * (viscosity * diffusion - 0.5 * transport))


def wall_mask(layer_count):
    layer_ids = jnp.arange(layer_count)
    open_top = jnp.where(layer_ids < layer_count - 1, 1.0, 0.0).astype(jnp.float32)
    ones_layer = jnp.ones((layer_count,), jnp.float32)
    return jnp.stack([ones_layer, ones_layer, open_top])[:, :, None, None]


def eigen_of(mode_ids, length):
    half_angle = jnp.pi * (mode_ids + 1).astype(jnp.float32) / (2.0 * (length + 1))
    return 4.0 * jnp.sin(half_angle) * jnp.sin(half_angle)


def solve_columns(source, eigen_sum):
    layer_count = source.shape[0]
    first_pivot = eigen_sum + 1.0
    first_ratio = -1.0 / first_pivot
    first_value = source[0] / first_pivot
    top_flags = jnp.arange(1, layer_count) == layer_count - 1

    def eliminate(state_pair, element):
        prior_ratio, prior_value = state_pair
        layer_source, is_top = element
        pivot_value = eigen_sum + jnp.where(is_top, 1.0, 2.0) + prior_ratio
        new_ratio = -1.0 / pivot_value
        new_value = (layer_source + prior_value) / pivot_value
        return ((new_ratio, new_value), (new_ratio, new_value))

    unused_state, (ratios, reduced_all) = lax.scan(
        eliminate, (first_ratio, first_value), (source[1:], top_flags)
    )
    ratios = jnp.concatenate([first_ratio[None], ratios], axis=0)
    reduced_all = jnp.concatenate([first_value[None], reduced_all], axis=0)

    def substitute(following, element):
        layer_ratio, layer_value = element
        solved_layer = layer_value - layer_ratio * following
        return (solved_layer, solved_layer)

    top_layer = reduced_all[-1]
    unused_last, lower_layers = lax.scan(
        substitute, top_layer, (ratios[:-1], reduced_all[:-1]), reverse=True
    )
    return jnp.concatenate([lower_layers, top_layer[None]], axis=0)


def sine_table(first_ids, second_ids, length):
    product = jnp.mod((first_ids + 1) * (second_ids + 1), 2 * (length + 1))
    return jnp.sin(jnp.pi * product.astype(jnp.float32) / (length + 1))


def parity_tables(length):
    half_ids = jnp.arange(length // 2, dtype=jnp.int32)
    even_table = sine_table(half_ids[:, None], 2 * half_ids[None, :], length)
    odd_table = sine_table(half_ids[:, None], 2 * half_ids[None, :] + 1, length)
    return (even_table, odd_table)


def fold_forward(values, even_table, odd_table):
    half = values.shape[-1] // 2
    lower_half = values[..., :half]
    upper_half = values[..., half:][..., ::-1]
    summed = lower_half + upper_half
    differed = lower_half - upper_half
    even_part = jnp.einsum("...x,xm->...m", summed, even_table, precision=highest)
    odd_part = jnp.einsum("...x,xm->...m", differed, odd_table, precision=highest)
    return jnp.stack([even_part, odd_part], axis=-1).reshape(values.shape)


def fold_backward(values, even_table, odd_table):
    half = values.shape[-1] // 2
    pairs = values.reshape(values.shape[:-1] + (half, 2))
    even_part = jnp.einsum("...m,xm->...x", pairs[..., 0], even_table, precision=highest)
    odd_part = jnp.einsum("...m,xm->...x", pairs[..., 1], odd_table, precision=highest)
    return jnp.concatenate([even_part + odd_part, (even_part - odd_part)[..., ::-1]], axis=-1)


def to_tile(blocks, placing, row_span, col_span):
    channels = blocks.shape[0]
    slot_count = placing.shape[0]
    slot_ids = jnp.arange(slot_count, dtype=jnp.int32)
    matches = placing[None, :] == slot_ids[:, None]
    inverse = jnp.sum(jnp.where(matches, slot_ids[None, :], 0), axis=1)
    ordered = jnp.take(blocks, inverse, axis=1)
    shaped = ordered.reshape(channels, NZ // B, row_span // B, col_span // B, B, B, B)
    return shaped.transpose(0, 1, 4, 2, 5, 3, 6).reshape(channels, NZ, row_span, col_span)


def from_tile(field, placing):
    channels, layer_count, row_span, col_span = field.shape
    shaped = field.reshape(channels, layer_count // B, B, row_span // B, B, col_span // B, B)
    ordered = shaped.transpose(0, 1, 3, 5, 2, 4, 6).reshape(channels, -1, B, B * B)
    return jnp.take(ordered, placing, axis=1)


def layer_below(field):
    return jnp.concatenate([jnp.zeros_like(field[:1]), field[:-1]], axis=0)


def layer_above(field):
    return jnp.concatenate([field[1:], jnp.zeros_like(field[:1])], axis=0)


def shards(velocity, fluid, block_place):
    pa_size = lax.axis_size("pa")
    pb_size = lax.axis_size("pb")
    group_count = pa_size * pb_size
    row_span = NY // pa_size
    col_span = NX // pb_size
    mode_span = NX // group_count
    row_piece = NY // group_count
    flow = to_tile(velocity, block_place, row_span, col_span)
    fraction = to_tile(fluid[None], block_place, row_span, col_span)
    stacked = jnp.concatenate([flow, fraction], axis=0)
    widened = extended(stacked, (("pa", 2), ("pb", 3)), 2)
    moving = widened[:3]

    def window(field, y_start, x_start):
        return field[:, y_start : y_start + row_span + 1, x_start : x_start + col_span + 1]

    fraction_region = window(widened[3], 1, 1)
    centers = [window(moving[component], 1, 1) for component in range(3)]
    updated = []
    for component in range(3):
        lower_side = (
            window(moving[component], 1, 0),
            window(moving[component], 0, 1),
            layer_below(centers[component]),
        )
        upper_side = (
            window(moving[component], 1, 2),
            window(moving[component], 2, 1),
            layer_above(centers[component]),
        )
        updated.append(
            advance_one(centers[component], centers, lower_side, upper_side, fraction_region)
        )
    provisional = jnp.stack(updated) * wall_mask(NZ)
    flux_x = provisional[0, :, 1:, 1:] - provisional[0, :, 1:, :-1]
    flux_y = provisional[1, :, 1:, 1:] - provisional[1, :, :-1, 1:]
    vertical = provisional[2, :, 1:, 1:]
    divergence = flux_x + flux_y + (vertical - layer_below(vertical))
    interior = provisional[:, :, 1:, 1:]
    columns = lax.all_to_all(divergence, "pb", split_axis=1, concat_axis=2, tiled=True)
    y_ids = jnp.arange(NY, dtype=jnp.int32)
    x_even, x_odd = parity_tables(NX)
    y_even, y_odd = parity_tables(NY)
    modes_flat = fold_forward(columns, x_even, x_odd)
    modes_x = modes_flat.reshape(NZ, row_piece, group_count, mode_span).transpose(0, 2, 3, 1)
    packed = modes_x.reshape(NZ, group_count, mode_span * row_piece)
    moved = lax.all_to_all(packed, ("pa", "pb"), split_axis=1, concat_axis=1, tiled=True).reshape(
        NZ, group_count, mode_span, row_piece
    )
    lines = moved.transpose(0, 2, 1, 3).reshape(NZ, mode_span, NY)
    modes = fold_forward(lines, y_even, y_odd)
    group = lax.axis_index("pa") * pb_size + lax.axis_index("pb")
    mode_ids = group * mode_span + jnp.arange(mode_span, dtype=jnp.int32)
    eigen_sum = eigen_of(mode_ids, NX)[:, None] + eigen_of(y_ids, NY)[None, :]
    scale = 4.0 / ((NX + 1) * (NY + 1))
    solved = solve_columns(-modes * scale, eigen_sum)
    rim_ids = (jnp.arange(group_count, dtype=jnp.int32) + 1) * row_piece
    rim_table = jnp.where(
        rim_ids[None, :] < NY, sine_table(y_ids[:, None], rim_ids[None, :], NY), 0.0
    )
    back_lines = fold_backward(solved, y_even, y_odd)
    main_back = back_lines.reshape(NZ, mode_span, group_count, row_piece).transpose(0, 2, 1, 3)
    main_back = main_back.reshape(NZ, group_count, mode_span * row_piece)
    rim_back = jnp.einsum("zkj,jg->zgk", solved, rim_table, precision=highest)
    main_home, rim_home = (
        lax.all_to_all(main_back, ("pa", "pb"), split_axis=1, concat_axis=1, tiled=True),
        lax.all_to_all(rim_back, ("pa", "pb"), split_axis=1, concat_axis=1, tiled=True),
    )
    main_home = main_home.reshape(NZ, group_count, mode_span, row_piece)
    rim_home = rim_home.reshape(NZ, NX)
    home_lines = main_home.transpose(0, 3, 1, 2).reshape(NZ, row_piece, NX)
    pressure_rows = fold_backward(home_lines, x_even, x_odd)
    pressure_rim = fold_backward(rim_home, x_even, x_odd)
    x_edges = jnp.concatenate(
        [pressure_rows[:, :, col_span::col_span], jnp.zeros((NZ, row_piece, 1), jnp.float32)],
        axis=2,
    )
    pressure_tile, x_rim, y_rims = (
        lax.all_to_all(pressure_rows, "pb", split_axis=2, concat_axis=1, tiled=True),
        lax.all_to_all(x_edges, "pb", split_axis=2, concat_axis=1, tiled=True),
        lax.all_to_all(pressure_rim[:, None, :], "pb", split_axis=2, concat_axis=1, tiled=True),
    )
    y_rim = y_rims[:, -1, :]
    next_x = jnp.concatenate([pressure_tile[:, :, 1:], x_rim], axis=2)
    next_y = jnp.concatenate([pressure_tile[:, 1:, :], y_rim[:, None, :]], axis=1)
    next_z = layer_above(pressure_tile)
    gradient = jnp.stack(
        [next_x - pressure_tile, next_y - pressure_tile, next_z - pressure_tile]
    ) * wall_mask(NZ)
    velocity_grid = interior - gradient
    return (from_tile(velocity_grid, block_place), from_tile(pressure_tile[None], block_place)[0])


def solution(mesh):
    return jax.shard_map(
        shards,
        mesh=mesh,
        in_specs=(P(None, ("pa", "pb"), None, None), P(("pa", "pb"), None, None), P(("pa", "pb"))),
        out_specs=(P(None, ("pa", "pb"), None, None), P(("pa", "pb"), None, None)),
        check_vma=False,
    )
```

profile of v0, /device:TPU:0, one launch (start us, length us, event | category | flops | bytes accessed | tf_op | source)
XLA Modules:
  0.0 3132.9 jit_solution(9045579455979406268)
XLA Ops:
  40.4 62.6 %reshape.317 = f32[3,1,8,8,32,32,32]{6,5,4,0,3,2,1:T(8,128)} reshape(f32[3,64,32,1024]{3,2,0,1:T(8,128)} %select_bitcast_fusion.1) | data formatting | bytes 50331648 | tf_op jit(solution)/shard_map/reshape | solution.py:131
  103.0 109.8 %copy.292 = f32[3,1,8,8,32,32,32]{6,3,5,2,4,0,1:T(8,128)} copy(f32[3,1,8,8,32,32,32]{6,5,4,0,3,2,1:T(8,128)} %reshape.317) | data formatting | bytes 50331648 | tf_op jit(solution)/shard_map/reshape | solution.py:131
  212.9 67.4 %reshape.318 = f32[3,32,256,256]{3,2,1,0:T(8,128)} reshape(f32[3,1,32,8,32,8,32]{6,5,4,3,2,0,1:T(8,128)} %bitcast.232) | data formatting | bytes 50331648 | tf_op jit(solution)/shard_map/reshape | solution.py:132
  335.9 38.4 %copy.294 = f32[1,1,8,8,32,32,32]{6,3,5,2,4,1,0:T(8,128)} copy(f32[1,1,8,8,32,32,32]{6,5,4,3,2,1,0:T(8,128)} %reshape.319) | data formatting | bytes 16777216 | tf_op jit(solution)/shard_map/reshape | solution.py:131
  506.5 47.3 %pad_maximum_fusion = f32[4,32,260,260]{3,2,1,0:T(8,128)} fusion(f32[4,32,260,2]{3,2,1,0:T(8,128)} %copy.224, f32[4,32,2,256]{3,2,1,0:T(2,128)S(1)} %collective-permute-done.1, f32[4,32,256,256]{3,2,1,0:T(8,128)} %constant_dynamic-update-slice_fusion, f32[4,32,2,256]{3,2,1,0:T(2,128)S(1)} %collective-permute-done, f32[4,32,260,2]{3,2,1,0:T(8,128)} %copy.223), kind=kLoop, calls=%fused_computation.17 | loop fusion | flops 34611200 | bytes 69222400 | tf_op jit(solution)/shard_map/concatenate | solution.py:26
  553.9 34.3 %slice_bitcast_fusion.3 = (f32[32,260,260]{2,1,0:T(8,128)}, f32[32,260,260]{2,1,0:T(8,128)}, f32[32,260,260]{2,1,0:T(8,128)}, f32[32,260,260]{2,1,0:T(8,128)}) fusion(f32[4,32,260,260]{3,2,1,0:T(8,128)} %pad_maximum_fusion), kind=kLoop, calls=%fused_computation.29 | loop fusion | bytes 69222400 | tf_op jit(solution)/shard_map/squeeze | solution.py:167
  647.7 56.2 %multiply_bitcast_fusion.2 = f32[1,32,257,257]{3,2,1,0:T(8,128)} fusion(f32[31,257,257]{2,1,0:T(8,128)} %get-tuple-element.290, f32[31,257,257]{2,1,0:T(8,128)} %get-tuple-element.289, f32[32,260,260]{2,1,0:T(8,128)} %get-tuple-element.280, f32[32,260,260]{2,1,0:T(8,128)S(1)} %bitcast.243, f32[32,260,260]{2,1,0:T(8,128)} %get-tuple-element.279, ...), kind=kLoop, calls=%fused_computation.32 | loop fusion | flops 44384928 | bytes 92468600 | tf_op jit(solution)/shard_map/stack | solution.py:184
  703.9 55.6 %multiply_bitcast_fusion.1 = f32[1,32,257,257]{3,2,1,0:T(8,128)} fusion(f32[31,257,257]{2,1,0:T(8,128)} %get-tuple-element.292, f32[31,257,257]{2,1,0:T(8,128)} %get-tuple-element.291, f32[32,260,260]{2,1,0:T(8,128)} %get-tuple-element.279, f32[32,260,260]{2,1,0:T(8,128)S(1)} %bitcast.243, f32[32,260,260]{2,1,0:T(8,128)} %get-tuple-element.280, ...), kind=kLoop, calls=%fused_computation.31 | loop fusion | flops 44384928 | bytes 92468600 | tf_op jit(solution)/shard_map/stack | solution.py:184
  759.6 32.5 %multiply_bitcast_fusion = f32[1,32,257,257]{3,2,1,0:T(8,128)} fusion(f32[31,257,257]{2,1,0:T(8,128)} %get-tuple-element.294, f32[31,257,257]{2,1,0:T(8,128)} %get-tuple-element.293, f32[32,260,260]{2,1,0:T(8,128)S(1)} %bitcast.243, f32[32,260,260]{2,1,0:T(8,128)} %get-tuple-element.279, f32[32,260,260]{2,1,0:T(8,128)} %get-tuple-element.280, ...), kind=kLoop, calls=%fused_computation.30 | loop fusion | flops 44384928 | bytes 92468600 | tf_op jit(solution)/shard_map/stack | solution.py:184
  792.1 28.8 maximum_multiply_fusion
  864.5 181.8 %all-to-all-done = f32[32,256,256]{2,0,1:T(8,128)} async-done(((f32[32,256,256]{2,0,1:T(8,128)}), f32[32,256,256]{2,0,1:T(8,128)}, u32[]{:S(2)}, u32[]{:S(2)}) %all-to-all-start) | async-done | bytes 8388640 | tf_op jit(solution)/shard_map/all_to_all | solution.py:190
  1079.3 34.8 %fusion.62 = f32[32,32,1024,1]{2,1,0,3:T(8,128)S(1)} fusion(f32[32,32,1024]{2,1,0:T(8,128)} %rev.15, f32[32,32,2048]{2,1,0:T(8,128)} %all_to_all.60, s32[1024]{0:T(1024)S(1)} %fusion.162, s32[1024]{0:T(1024)S(1)} %get-tuple-element.317), kind=kOutput, calls=%fused_computation.101 | convolution fusion | flops 12895387648 | bytes 12591104 | tf_op jit(solution)/shard_map/...x,xm->...m/dot_general | solution.py:111
  1114.1 33.2 %fusion.67 = f32[32,32,1024,1]{2,1,0,3:T(8,128)S(1)} fusion(f32[32,32,1024]{2,1,0:T(8,128)S(1)} %copy-done.7, f32[32,32,2048]{2,1,0:T(8,128)} %all_to_all.60, s32[1024]{0:T(1024)S(1)} %get-tuple-element.316, s32[1024]{0:T(1024)S(1)} %get-tuple-element.317), kind=kOutput, calls=%fused_computation.102 | convolution fusion | flops 12895387648 | bytes 12591104 | tf_op jit(solution)/shard_map/...x,xm->...m/dot_general | solution.py:112
  1151.5 26.4 copy.228
  1178.0 31.8 %copy.272 = f32[32,32,64,32]{3,2,0,1:T(8,128)} copy(f32[32,32,64,32]{3,0,2,1:T(8,128)} %bitcast.254) | data formatting | bytes 16777216 | tf_op jit(solution)/shard_map/reshape | solution.py:196
  1209.7 25.3 reshape.388
  1240.7 185.7 %all-to-all-done.1 = f32[32,32,2048]{2,0,1:T(8,128)} async-done(((f32[32,32,2048]{2,0,1:T(8,128)}), f32[32,32,2048]{2,0,1:T(8,128)}, u32[]{:S(2)}, u32[]{:S(2)}) %all-to-all-start.1) | async-done | bytes 8388640 | tf_op jit(solution)/shard_map/all_to_all | solution.py:197
  1491.3 63.9 %rev.16 = f32[32,64,512]{1,2,0:T(8,128)} reverse(f32[32,64,512]{1,2,0:T(8,128)} %slice.315), dimensions={2} | reverse | bytes 8388608 | tf_op jit(solution)/shard_map/rev | solution.py:108
  1652.1 99.6 %while.34 = (s32[]{:T(128)}, f32[64,1024]{1,0:T(8,128)S(1)}, f32[64,1024]{1,0:T(8,128)S(1)}, f32[31,64,1024]{2,1,0:T(8,128)}, f32[31,64,1024]{2,1,0:T(8,128)}, /...) while((s32[]{:T(128)}, f32[64,1024]{1,0:T(8,128)S(1)}, ...), condition=%wide.region_2.5_spmd.clone, body=%wide.region_1.0_spmd.clone.sunk | while | flops 393219 | bytes 1840520 | solution.py:75
  1769.9 59.7 %while.33 = (s32[]{:T(128)}, f32[64,1024]{1,0:T(8,128)S(1)}, f32[31,64,1024]{2,1,0:T(8,128)}, f32[31,64,1024]{2,1,0:T(8,128)}, f32[31,64,1024]{2,1,0:T(8,128)}, /*index=5*/s32[]{:T(128)}, s32[]{:T(128)}) while((s32[]{:T(128)}, f32[64,1024]{1,0:T(8,128)S(1)}, f32[31,64,1024]{2,1,0:T(8,128)}, f32[31,64,1024]{2,1,0:T(8,128)}, ...), condition=%wide.region_4.7_spmd, body=%wide.region_3.6_spmd.sunk | while | flops 131075 | bytes 1310813 | solution.py:87
  1980.1 25.3 reshape.389
  2100.8 96.6 %all-to-all-done.2 = f32[32,32,2048]{2,0,1:T(8,128)} async-done(((f32[32,32,2048]{2,0,1:T(8,128)}), f32[32,32,2048]{2,0,1:T(8,128)}, u32[]{:S(2)}, u32[]{:S(2)}) %all-to-all-start.2) | async-done | bytes 8388640 | tf_op jit(solution)/shard_map/all_to_all | solution.py:216
  2236.2 31.9 %copy.249 = f32[32,32,32,64]{1,0,3,2:T(8,128)} copy(f32[32,32,32,64]{1,3,2,0:T(8,128)} %bitcast.255) | data formatting | bytes 16777216 | tf_op jit(solution)/shard_map/transpose | solution.py:221
  2373.3 26.3 copy.252
  2436.8 171.9 %all-to-all-done.3 = f32[8,1,262144]{2,1,0:T(1,128)} async-done(((f32[8,1,262144]{2,1,0:T(1,128)}), f32[8,1,262144]{2,1,0:T(1,128)}, u32[]{:S(2)}, u32[]{:S(2)}) %all-to-all-start.3) | async-done | bytes 8388640 | tf_op jit(solution)/shard_map/all_to_all | solution.py:229
  2608.7 26.3 reduce
  2635.0 25.3 reshape.392
  2779.6 26.8 slice_subtract_fusion
  2806.4 59.2 %reshape.328 = f32[3,1,32,8,32,8,32]{6,5,4,3,2,0,1:T(8,128)} reshape(f32[3,32,256,256]{3,2,1,0:T(8,128)} %slice_subtract_fusion) | data formatting | bytes 50331648 | tf_op jit(solution)/shard_map/reshape | solution.py:137
  2865.6 65.6 %copy.291 = f32[3,1,32,8,32,8,32]{6,4,2,5,3,0,1:T(8,128)} copy(f32[3,1,32,8,32,8,32]{6,5,4,3,2,0,1:T(8,128)} %reshape.328) | data formatting | bytes 50331648 | tf_op jit(solution)/shard_map/reshape | solution.py:137
  2931.2 75.7 %reshape.329 = f32[3,64,32,1024]{3,2,1,0:T(8,128)} reshape(f32[3,1,8,8,32,32,32]{6,5,4,3,2,0,1:T(8,128)} %bitcast.231) | data formatting | bytes 50331648 | tf_op jit(solution)/shard_map/reshape | solution.py:138
  3090.0 26.1 reshape.379
  (313 shorter events, 1338.3 us)
Async XLA Ops:
  2.7 19.3 copy-start.16
  407.0 3.7 collective-permute-start
  409.3 5.5 collective-permute-start.1
  471.4 16.8 collective-permute-start.2
  486.3 11.2 collective-permute-start.3
  588.2 46.4 %slice-start = ((s8[12976128]{0:T(1024)(128)(4,1)}), s8[4194304]{0:T(1024)(128)(4,1)S(1)}, s32[]{:S(2)}) async-start(s8[12976128]{0:T(1024)(128)(4,1)} %bitcast.242), calls=%async_computation.7 | async-start | bytes 8388608
  588.2 46.4 %slice-start.1 = ((s8[12976128]{0:T(1024)(128)(4,1)}), s8[4194304]{0:T(1024)(128)(4,1)S(1)}, s32[]{:S(2)}) async-start(s8[12976128]{0:T(1024)(128)(4,1)} %bitcast.242), calls=%async_computation.8 | async-start | bytes 8388608
  611.6 23.0 slice-start.2
  611.6 23.0 slice-start.3
  759.6 32.5 %copy-start.10 = (f32[3,32]{1,0:T(4,128)S(1)}, f32[3,32]{1,0:T(4,128)}, u32[]{:S(2)}) copy-start(f32[3,32]{1,0:T(4,128)} %stack.48) | copy-start | bytes 1156
  857.5 188.8 %all-to-all-start = ((f32[32,256,256]{2,0,1:T(8,128)}), f32[32,256,256]{2,0,1:T(8,128)}, u32[]{:S(2)}, u32[]{:S(2)}) async-start(f32[32,256,256]{2,0,1:T(8,128)} %copy.225), calls=%async_computation | async-start | bytes 16777216 | tf_op jit(solution)/shard_map/all_to_all | solution.py:190
  864.5 214.8 %copy-start.12 = (s32[1024]{0:T(1024)}, s32[1024]{0:T(1024)S(1)}, u32[]{:S(2)}) copy-start(s32[1024]{0:T(1024)S(1)} %fusion.162) | copy-start | bytes 12292
  864.5 249.5 %copy-start.8 = (s32[1024]{0:T(1024)}, s32[1024]{0:T(1024)S(1)}, u32[]{:S(2)}) copy-start(s32[1024]{0:T(1024)S(1)} %get-tuple-element.317) | copy-start | bytes 12292
  864.5 249.5 %copy-start.14 = (s32[1024]{0:T(1024)}, s32[1024]{0:T(1024)S(1)}, u32[]{:S(2)}) copy-start(s32[1024]{0:T(1024)S(1)} %get-tuple-element.316) | copy-start | bytes 12292
  1079.3 34.8 %copy-start.7 = (f32[32,32,1024]{2,1,0:T(8,128)S(1)}, f32[32,32,1024]{2,1,0:T(8,128)}, u32[]{:S(2)}) copy-start(f32[32,32,1024]{2,1,0:T(8,128)} %rev.15) | copy-start | bytes 12582916
  1235.1 191.4 %all-to-all-start.1 = ((f32[32,32,2048]{2,0,1:T(8,128)}), f32[32,32,2048]{2,0,1:T(8,128)}, u32[]{:S(2)}, u32[]{:S(2)}) async-start(f32[32,32,2048]{2,0,1:T(8,128)} %reshape.388), calls=%async_computation.1 | async-start | bytes 16777216 | tf_op jit(solution)/shard_map/all_to_all | solution.py:197
  1555.2 23.8 copy-start.1
  1851.7 153.7 %all-to-all-start.5 = ((f32[32,1,2048]{2,1,0:T(1,128)}), f32[32,1,2048]{2,1,0:T(1,128)S(1)}, u32[]{:S(2)}, u32[]{:S(2)}) async-start(f32[32,1,2048]{2,1,0:T(1,128)} %reshape.393), calls=%async_computation.5 | async-start | bytes 524288 | tf_op jit(solution)/shard_map/all_to_all | solution.py:217
  2005.4 23.4 copy-start.13
  2005.4 191.9 %all-to-all-start.2 = ((f32[32,32,2048]{2,0,1:T(8,128)}), f32[32,32,2048]{2,0,1:T(8,128)}, u32[]{:S(2)}, u32[]{:S(2)}) async-start(f32[32,32,2048]{2,0,1:T(8,128)} %reshape.389), calls=%async_computation.2 | async-start | bytes 16777216 | tf_op jit(solution)/shard_map/all_to_all | solution.py:216
  2197.3 169.9 %all-to-all-start.6 = ((f32[8,1,8192]{2,1,0:T(1,128)}), f32[8,1,8192]{2,1,0:T(1,128)S(1)}, u32[]{:S(2)}, u32[]{:S(2)}) async-start(f32[8,1,8192]{2,1,0:T(1,128)} %reshape.395), calls=%async_computation.6 | async-start | bytes 524288 | tf_op jit(solution)/shard_map/all_to_all | solution.py:231
  2367.3 52.8 %all-to-all-start.4 = ((f32[8,1,1024]{2,1,0:T(1,128)}), f32[8,1,1024]{2,1,0:T(1,128)S(1)}, u32[]{:S(2)}, u32[]{:S(2)}) async-start(f32[8,1,1024]{2,1,0:T(1,128)} %reshape.397), calls=%async_computation.4 | async-start | bytes 65536 | tf_op jit(solution)/shard_map/all_to_all | solution.py:230
  2420.1 188.6 %all-to-all-start.3 = ((f32[8,1,262144]{2,1,0:T(1,128)}), f32[8,1,262144]{2,1,0:T(1,128)}, u32[]{:S(2)}, u32[]{:S(2)}) async-start(f32[8,1,262144]{2,1,0:T(1,128)} %reshape.391), calls=%async_computation.3 | async-start | bytes 16777216 | tf_op jit(solution)/shard_map/all_to_all | solution.py:229
  3006.9 19.3 copy-start.17
  3026.2 42.2 %slice-start.4 = ((s8[33554432]{0:T(1024)(128)(4,1)}), s8[4194304]{0:T(1024)(128)(4,1)S(1)}, s32[]{:S(2)}) async-start(s8[33554432]{0:T(1024)(128)(4,1)} %bitcast.251), calls=%async_computation.11 | async-start | bytes 8388608
  3026.2 42.2 %slice-start.5 = ((s8[33554432]{0:T(1024)(128)(4,1)}), s8[4194304]{0:T(1024)(128)(4,1)S(1)}, s32[]{:S(2)}) async-start(s8[33554432]{0:T(1024)(128)(4,1)} %bitcast.251), calls=%async_computation.12 | async-start | bytes 8388608
  3026.2 42.2 %slice-start.6 = ((s8[33554432]{0:T(1024)(128)(4,1)}), s8[4194304]{0:T(1024)(128)(4,1)S(1)}, s32[]{:S(2)}) async-start(s8[33554432]{0:T(1024)(128)(4,1)} %bitcast.251), calls=%async_computation.13 | async-start | bytes 8388608
  3026.2 42.2 %slice-start.7 = ((s8[33554432]{0:T(1024)(128)(4,1)}), s8[4194304]{0:T(1024)(128)(4,1)S(1)}, s32[]{:S(2)}) async-start(s8[33554432]{0:T(1024)(128)(4,1)} %bitcast.251), calls=%async_computation.14 | async-start | bytes 8388608
  3026.2 42.2 %slice-start.8 = ((s8[33554432]{0:T(1024)(128)(4,1)}), s8[4194304]{0:T(1024)(128)(4,1)S(1)}, s32[]{:S(2)}) async-start(s8[33554432]{0:T(1024)(128)(4,1)} %bitcast.251), calls=%async_computation.15 | async-start | bytes 8388608
  3047.3 21.1 slice-start.9
  3047.3 21.1 slice-start.10
  3047.3 21.1 slice-start.11
  (13 other events, 141.7 us)
where the time goes:
time: 3160 us; the launch traced here: 3130 us
  local copies, waits for them, and re-layouts  1570 us (50%)
  waiting for transfers between devices  640 us (20%)
  other arithmetic  617 us (20%)
  matrix products  229 us (7%)
  starting transfers between devices  51.3 us (2%)
    reshape x4, local copies, waits for them, and re-layouts, to_tile(): ordered.reshape(channels, NZ // B, row_span // B, col_span // B, B, B, B)  233 us
    all_to_all x1, waiting for transfers between devices, shards(): lax.all_to_all(packed, ('pa', 'pb'), split_axis=1, concat_axis=1, tiled=T...  186 us
    all_to_all x1, waiting for transfers between devices, shards(): lax.all_to_all(divergence, 'pb', split_axis=1, concat_axis=2, tiled=True)  182 us
    all_to_all x1, waiting for transfers between devices, shards(): lax.all_to_all(pressure_rows, 'pb', split_axis=2, concat_axis=1, tiled=True)  172 us
    another operation x3, other arithmetic, shards(): provisional = jnp.stack(updated) * wall_mask(NZ)  144 us
    unnamed x86, local copies, waits for them, and re-layouts  140 us
    reshape x2, local copies, waits for them, and re-layouts, from_tile(): field.reshape(channels, layer_count // B, B, row_span // B, B, col_span /...  125 us
    dynamic_update_slice x62, other arithmetic, solve_columns(): lax.scan(eliminate, (first_ratio, first_value), (source[1:], top_flags))  120 us
  transfers between devices with their start and end apart: 11, of which 5 were waited for; matrix products, arithmetic and copies ran while one was open for 15% of the time, Pallas kernels for 0%

commit v1 on v0

v1 whole, which is shorter than its diff:
```python
import functools

import jax
import jax.numpy as jnp
import ml_dtypes
import numpy as np
from jax import lax
from jax.experimental import pallas as pl
from jax.experimental.pallas import tpu as pltpu
from jax.sharding import PartitionSpec as P

NX = 2048
NY = 1024
NZ = 32
B = 32
LANES = 128
highest = lax.Precision.HIGHEST
f32 = jnp.float32
VMEM_LIMIT = 56 * 1024 * 1024


def cosine_basis():
    k = np.arange(NZ)[:, None]
    z = np.arange(NZ)[None, :]
    table = np.cos(np.pi * k * (z + 0.5) / NZ)
    table /= np.sqrt((table**2).sum(axis=1, keepdims=True))
    return table, 2.0 - 2.0 * np.cos(np.pi * np.arange(NZ) / NZ)


def sine_basis(length, lower_gap, upper_gap):
    span = length - 1 + lower_gap + upper_gap
    i = np.arange(length)[:, None]
    k = np.arange(1, length + 1)[None, :]
    table = np.sin(np.pi * k * (i + lower_gap) / span)
    table /= np.sqrt((table**2).sum(axis=0, keepdims=True))
    return table, 4.0 * np.sin(np.pi * np.arange(1, length + 1) / (2 * span)) ** 2


def tile_bases(length):
    return [sine_basis(length, *gaps) for gaps in ((1.0, 0.5), (0.5, 0.5), (0.5, 1.0))]


def split(table):
    table = np.asarray(table, np.float64)
    high = table.astype(np.float32).astype(ml_dtypes.bfloat16)
    low = (table - high.astype(np.float64)).astype(np.float32).astype(ml_dtypes.bfloat16)
    return np.stack([high, low], axis=-3)


def single(table):
    return np.asarray(table, np.float32)


def pieces(values):
    high = values.astype(jnp.bfloat16)
    return high, (values - high.astype(f32)).astype(jnp.bfloat16)


def mm(left, right):
    return jnp.dot(left, right, preferred_element_type=f32)


def table_times(table_ref, values):
    high, low = pieces(values)
    table_high, table_low = table_ref[0], table_ref[1]
    return mm(table_high, high) + (mm(table_high, low) + mm(table_low, high))


def times_table(values, table_ref):
    high, low = pieces(values)
    table_high, table_low = table_ref[0], table_ref[1]
    return mm(high, table_high) + (mm(high, table_low) + mm(low, table_high))


def dot_full(left, right, dims):
    return lax.dot_general(left, right, (dims, ((), ())), precision=highest, preferred_element_type=f32)


def lane_ids(rows=NZ):
    return lax.broadcasted_iota(jnp.int32, (rows, LANES), 1)


def swap_groups(four, lanes):
    low_half = lanes < 64
    even = (lanes & 32) == 0
    first = [
        jnp.where(low_half, four[0], pltpu.roll(four[2], 64, 1)),
        jnp.where(low_half, four[1], pltpu.roll(four[3], 64, 1)),
        jnp.where(low_half, pltpu.roll(four[0], 64, 1), four[2]),
        jnp.where(low_half, pltpu.roll(four[1], 64, 1), four[3]),
    ]
    out = []
    for pair in (0, 2):
        left, right = first[pair], first[pair + 1]
        out.append(jnp.where(even, left, pltpu.roll(right, 32, 1)))
        out.append(jnp.where(even, pltpu.roll(left, 96, 1), right))
    return out


def params():
    return pltpu.CompilerParams(vmem_limit_bytes=VMEM_LIMIT)


def gather_tile(velocity, fluid, inverse, rows_n, cols_n):
    y_span, x_span = rows_n * B, cols_n * B
    quads = cols_n // 4

    def kernel(inverse_ref, *refs):
        flow_refs = refs[:cols_n]
        fraction_refs = refs[cols_n : 2 * cols_n]
        out_ref, low_ref, high_ref = refs[2 * cols_n :]
        step = pl.program_id(0)
        lanes = lane_ids()
        place = step % 4
        chunk = pl.ds(pl.multiple_of(step // 4 * LANES, LANES), LANES)
        mine = (lanes // 32) == place
        for channel in range(4):
            low_edge = jnp.zeros((NZ, LANES), f32)
            high_edge = jnp.zeros((NZ, LANES), f32)
            for jq in range(8):
                for quad in range(quads):
                    four = []
                    for g in range(4):
                        at = quad * 4 + g
                        part = slice(jq * LANES, (jq + 1) * LANES)
                        if channel < 3:
                            four.append(flow_refs[at][channel, 0, :, part])
                        else:
                            four.append(fraction_refs[at][0, :, part])
                    rows = swap_groups(four, lanes)
                    for t in range(4):
                        j = jq * 4 + t
                        out_ref[channel, j, :, quad * LANES : (quad + 1) * LANES] = rows[t]
                        if channel < 3 and quad == 0:
                            low_edge = jnp.where(lanes == j, pltpu.roll(rows[t], j, 1), low_edge)
                        if channel < 3 and quad == quads - 1:
                            high_edge = jnp.where(lanes == j, pltpu.roll(rows[t], j + 1, 1), high_edge)
            if channel < 3:
                shift = place * 32
                low_ref[channel, :, chunk] = jnp.where(mine, pltpu.roll(low_edge, shift, 1), low_ref[channel, :, chunk])
                high_ref[channel, :, chunk] = jnp.where(mine, pltpu.roll(high_edge, shift, 1), high_ref[channel, :, chunk])

    def flow_spec(col):
        return pl.BlockSpec((3, 1, NZ, B * B), lambda s, inv: (0, inv[s * cols_n + col], 0, 0))

    def fraction_spec(col):
        return pl.BlockSpec((1, NZ, B * B), lambda s, inv: (inv[s * cols_n + col], 0, 0))

    edge = pl.BlockSpec((3, NZ, y_span), lambda s, inv: (0, 0, 0))
    return pl.pallas_call(
        kernel,
        grid_spec=pltpu.PrefetchScalarGridSpec(
            num_scalar_prefetch=1,
            grid=(rows_n,),
            in_specs=[flow_spec(c) for c in range(cols_n)] + [fraction_spec(c) for c in range(cols_n)],
            out_specs=[pl.BlockSpec((4, B, NZ, x_span), lambda s, inv: (0, s, 0, 0)), edge, edge],
        ),
        out_shape=[
            jax.ShapeDtypeStruct((4, y_span, NZ, x_span), f32),
            jax.ShapeDtypeStruct((3, NZ, y_span), f32),
            jax.ShapeDtypeStruct((3, NZ, y_span), f32),
        ],
        compiler_params=params(),
    )(inverse, *([velocity] * cols_n), *([fluid] * cols_n))


def advance(tile, x_below, x_above, y_below, y_above, cosine, sine_x, kinds):
    _, y_span, _, x_span = tile.shape
    steps = y_span // B
    chunks = x_span // LANES

    def kernel(kinds_ref, main_ref, prev_ref, next_ref, xb_ref, xa_ref, yb_ref, ya_ref, cosine_ref, sine_ref,
               star_ref, modes_ref, gx_ref, gy_ref, rows_ref, source_ref, carry_ref):
        step = pl.program_id(0)
        lanes = lane_ids()
        layers = lax.broadcasted_iota(jnp.int32, (NZ, LANES), 0)
        first_layer, last_layer = layers == 0, layers == NZ - 1
        first_lane, last_lane = lanes == 0, lanes == LANES - 1

        rows_ref[:, 1 : B + 1] = main_ref[:3]

        @pl.when(step == 0)
        def _():
            rows_ref[:, 0] = yb_ref[...]
            carry_ref[...] = jnp.zeros_like(carry_ref)

        @pl.when(step > 0)
        def _():
            rows_ref[:, 0] = prev_ref[:3, 0]

        @pl.when(step == steps - 1)
        def _():
            rows_ref[:, B + 1] = ya_ref[...]

        @pl.when(step < steps - 1)
        def _():
            rows_ref[:, B + 1] = next_ref[:3, 0]

        def row(j, _):
            y = step * B + j
            at = y % LANES
            y_chunk = pl.ds(pl.multiple_of(y // LANES * LANES, LANES), LANES)
            star = {}
            flow = {}
            for h in range(chunks):
                for c in range(3):
                    flow[c, h] = rows_ref[c, j + 1, :, h * LANES : (h + 1) * LANES]
            for h in range(chunks):
                part = slice(h * LANES, (h + 1) * LANES)
                take_up, take_down = [], []
                for e in range(3):
                    scaled = 0.125 * flow[e, h]
                    take_up.append(0.025 - scaled)
                    take_down.append(0.025 + scaled)
                fraction = main_ref[3, j, :, part]
                for c in range(3):
                    center = flow[c, h]
                    if h == 0:
                        before = pltpu.roll(xb_ref[c, :, y_chunk], (LANES - at) % LANES, 1)
                    else:
                        before = pltpu.roll(flow[c, h - 1], 1, 1)
                    if h == chunks - 1:
                        after = pltpu.roll(xa_ref[c, :, y_chunk], LANES - 1 - at, 1)
                    else:
                        after = pltpu.roll(flow[c, h + 1], LANES - 1, 1)
                    x_low = jnp.where(first_lane, before, pltpu.roll(center, 1, 1))
                    x_up = jnp.where(last_lane, after, pltpu.roll(center, LANES - 1, 1))
                    y_low = rows_ref[c, j, :, part]
                    y_up = rows_ref[c, j + 2, :, part]
                    z_low = jnp.where(first_layer, 0.0, pltpu.roll(center, 1, 0))
                    z_up = jnp.where(last_layer, 0.0, pltpu.roll(center, NZ - 1, 0))
                    total = (
                        0.85 * center
                        + (take_up[0] * x_up + take_down[0] * x_low)
                        + (take_up[1] * y_up + take_down[1] * y_low)
                        + (take_up[2] * z_up + take_down[2] * z_low)
                    )
                    value = fraction * total
                    if c == 2:
                        value = jnp.where(last_layer, 0.0, value)
                    star[c, h] = value
                    star_ref[c, j, :, part] = value
            for h in range(chunks):
                part = slice(h * LANES, (h + 1) * LANES)
                before = 0.0 if h == 0 else pltpu.roll(star[0, h - 1], 1, 1)
                x_low = jnp.where(first_lane, before, pltpu.roll(star[0, h], 1, 1))
                z_low = jnp.where(first_layer, 0.0, pltpu.roll(star[2, h], 1, 0))
                y_low = carry_ref[:, part]
                source_ref[j, :, part] = (x_low - star[0, h]) + (y_low - star[1, h]) + (z_low - star[2, h])
                carry_ref[:, part] = star[1, h]
            edge = pltpu.roll(star[0, chunks - 1], (at + 1) % LANES, 1)
            gx_ref[:, y_chunk] = jnp.where(lanes == at, edge, gx_ref[:, y_chunk])
            return _

        lax.fori_loop(0, B, row, 0)
        gy_ref[...] = carry_ref[...]
        for q in range(B // 8):
            part = source_ref[8 * q : 8 * q + 8].reshape(8 * NZ, x_span)
            layered = table_times(cosine_ref, part)
            modes = times_table(layered, sine_ref)
            modes_ref[:, 8 * q : 8 * q + 8, :] = modes.reshape(NZ, 8, x_span)

    full3 = pl.BlockSpec((3, NZ, y_span), lambda s, kinds: (0, 0, 0))
    return pl.pallas_call(
        kernel,
        grid_spec=pltpu.PrefetchScalarGridSpec(
            num_scalar_prefetch=1,
            grid=(steps,),
            in_specs=[
                pl.BlockSpec((4, B, NZ, x_span), lambda s, kinds: (0, s, 0, 0)),
                pl.BlockSpec((4, 1, NZ, x_span), lambda s, kinds: (0, jnp.maximum(s * B - 1, 0), 0, 0)),
                pl.BlockSpec((4, 1, NZ, x_span), lambda s, kinds: (0, jnp.minimum(s * B + B, y_span - 1), 0, 0)),
                full3,
                full3,
                pl.BlockSpec((3, NZ, x_span), lambda s, kinds: (0, 0, 0)),
                pl.BlockSpec((3, NZ, x_span), lambda s, kinds: (0, 0, 0)),
                pl.BlockSpec((2, 8 * NZ, 8 * NZ), lambda s, kinds: (0, 0, 0)),
                pl.BlockSpec((None, 2, x_span, x_span), lambda s, kinds: (kinds[1], 0, 0, 0)),
            ],
            out_specs=[
                pl.BlockSpec((3, B, NZ, x_span), lambda s, kinds: (0, s, 0, 0)),
                pl.BlockSpec((NZ, B, x_span), lambda s, kinds: (0, s, 0)),
                pl.BlockSpec((NZ, y_span), lambda s, kinds: (0, 0)),
                pl.BlockSpec((NZ, x_span), lambda s, kinds: (0, 0)),
            ],
            scratch_shapes=[
                pltpu.VMEM((3, B + 2, NZ, x_span), f32),
                pltpu.VMEM((B, NZ, x_span), f32),
                pltpu.VMEM((NZ, x_span), f32),
            ],
        ),
        out_shape=[
            jax.ShapeDtypeStruct((3, y_span, NZ, x_span), f32),
            jax.ShapeDtypeStruct((NZ, y_span, x_span), f32),
            jax.ShapeDtypeStruct((NZ, y_span), f32),
            jax.ShapeDtypeStruct((NZ, x_span), f32),
        ],
        compiler_params=params(),
    )(kinds, tile, tile, tile, x_below, x_above, y_below, y_above, cosine, sine_x)


def first_solve(modes, sine_yt, sine_xt, edge_y, edge_x, eigen, levels, kinds):
    layers, y_span, x_span = modes.shape

    def kernel(kinds_ref, modes_ref, yt_ref, xt_ref, edge_y_ref, edge_x_ref, eigen_ref, levels_ref,
               spectrum_ref, along_x_ref, along_y_ref):
        spectrum = table_times(yt_ref, modes_ref[...])
        spectrum_ref[...] = spectrum
        solved = spectrum / (eigen_ref[...] + levels_ref[pl.program_id(0)])
        row_edges = dot_full(edge_y_ref[...], solved, ((1,), (0,)))
        along_x_ref[...] = times_table(row_edges, xt_ref)
        column_edges = dot_full(edge_x_ref[...], solved, ((1,), (1,)))
        along_y_ref[...] = times_table(column_edges, yt_ref)

    return pl.pallas_call(
        kernel,
        grid_spec=pltpu.PrefetchScalarGridSpec(
            num_scalar_prefetch=1,
            grid=(layers,),
            in_specs=[
                pl.BlockSpec((None, y_span, x_span), lambda k, kinds: (k, 0, 0)),
                pl.BlockSpec((None, 2, y_span, y_span), lambda k, kinds: (kinds[0], 0, 0, 0)),
                pl.BlockSpec((None, 2, x_span, x_span), lambda k, kinds: (kinds[1], 0, 0, 0)),
                pl.BlockSpec((None, 8, y_span), lambda k, kinds: (kinds[0], 0, 0)),
                pl.BlockSpec((None, 8, x_span), lambda k, kinds: (kinds[1], 0, 0)),
                pl.BlockSpec((None, y_span, x_span), lambda k, kinds: (kinds[0] * 3 + kinds[1], 0, 0)),
                pl.BlockSpec(memory_space=pltpu.SMEM),
            ],
            out_specs=[
                pl.BlockSpec((None, y_span, x_span), lambda k, kinds: (k, 0, 0)),
                pl.BlockSpec((None, 8, x_span), lambda k, kinds: (k, 0, 0)),
                pl.BlockSpec((None, 8, y_span), lambda k, kinds: (k, 0, 0)),
            ],
        ),
        out_shape=[
            jax.ShapeDtypeStruct((layers, y_span, x_span), f32),
            jax.ShapeDtypeStruct((layers, 8, x_span), f32),
            jax.ShapeDtypeStruct((layers, 8, y_span), f32),
        ],
        compiler_params=params(),
    )(kinds, modes, sine_yt, sine_xt, edge_y, edge_x, eigen, levels)


def second_solve(spectrum, sides_y, sides_x, sine_y, sine_yt, sine_x, sine_xt, edge_y, edge_x, eigen, levels, kinds):
    layers, y_span, x_span = spectrum.shape

    def kernel(kinds_ref, spectrum_ref, sides_y_ref, sides_x_ref, y_ref, x_ref, xt_ref, edge_y_ref, edge_x_ref,
               eigen_ref, levels_ref, out_ref):
        along_x = times_table(sides_y_ref[...], x_ref)
        along_y = times_table(sides_x_ref[...], y_ref)
        left = jnp.concatenate([edge_y_ref[...], along_y], axis=0)
        right = jnp.concatenate([along_x, edge_x_ref[...]], axis=0)
        added = dot_full(left, right, ((0,), (0,)))
        solved = (spectrum_ref[...] + added) / (eigen_ref[...] + levels_ref[pl.program_id(0)])
        out_ref[...] = times_table(table_times(y_ref, solved), xt_ref)

    return pl.pallas_call(
        kernel,
        grid_spec=pltpu.PrefetchScalarGridSpec(
            num_scalar_prefetch=1,
            grid=(layers,),
            in_specs=[
                pl.BlockSpec((None, y_span, x_span), lambda k, kinds: (k, 0, 0)),
                pl.BlockSpec((None, 8, x_span), lambda k, kinds: (k, 0, 0)),
                pl.BlockSpec((None, 8, y_span), lambda k, kinds: (k, 0, 0)),
                pl.BlockSpec((None, 2, y_span, y_span), lambda k, kinds: (kinds[0], 0, 0, 0)),
                pl.BlockSpec((None, 2, x_span, x_span), lambda k, kinds: (kinds[1], 0, 0, 0)),
                pl.BlockSpec((None, 2, x_span, x_span), lambda k, kinds: (kinds[1], 0, 0, 0)),
                pl.BlockSpec((None, 8, y_span), lambda k, kinds: (kinds[0], 0, 0)),
                pl.BlockSpec((None, 8, x_span), lambda k, kinds: (kinds[1], 0, 0)),
                pl.BlockSpec((None, y_span, x_span), lambda k, kinds: (kinds[0] * 3 + kinds[1], 0, 0)),
                pl.BlockSpec(memory_space=pltpu.SMEM),
            ],
            out_specs=pl.BlockSpec((None, y_span, x_span), lambda k, kinds: (k, 0, 0)),
        ),
        out_shape=jax.ShapeDtypeStruct((layers, y_span, x_span), f32),
        compiler_params=params(),
    )(kinds, spectrum, sides_y, sides_x, sine_y, sine_x, sine_xt, edge_y, edge_x, eigen, levels)


def finish(modes, star, sum_x, sum_y, cosine_t, inverse, kinds, slots):
    layers, y_span, x_span = modes.shape
    rows_n, cols_n = y_span // B, x_span // B
    chunks = x_span // LANES

    def kernel(inverse_ref, kinds_ref, modes_ref, after_ref, star_ref, sum_x_ref, sum_y_ref, cosine_ref,
               flow_out, pressure_out, rows_ref, blocks_ref):
        step, col = pl.program_id(0), pl.program_id(1)

        @pl.when(col == 0)
        def _():
            lanes = lane_ids()
            layers_at = lax.broadcasted_iota(jnp.int32, (NZ, LANES), 0)
            last_layer = layers_at == NZ - 1
            last_lane = lanes == LANES - 1
            for q in range(B // 8):
                part = modes_ref[:, 8 * q : 8 * q + 8, :].reshape(8 * NZ, x_span)
                rows_ref[8 * q : 8 * q + 8] = table_times(cosine_ref, part).reshape(8, NZ, x_span)

            @pl.when(step < rows_n - 1)
            def _():
                part = after_ref[...].reshape(8 * NZ, x_span)
                rows_ref[B] = table_times(cosine_ref, part).reshape(8, NZ, x_span)[0]

            @pl.when(step == rows_n - 1)
            def _():
                rows_ref[B] = jnp.where(kinds_ref[0] == 2, 0.0, sum_y_ref[...] - rows_ref[B - 1])

            def four_rows(jq, _):
                y = step * B + jq * 4
                y_chunk = pl.ds(pl.multiple_of(y // LANES * LANES, LANES), LANES)
                block = pl.ds(pl.multiple_of(jq * LANES, LANES), LANES)
                for h in range(chunks):
                    part = slice(h * LANES, (h + 1) * LANES)
                    found = [[], [], [], []]
                    for t in range(4):
                        j = jq * 4 + t
                        here = rows_ref[j, :, part]
                        if h == chunks - 1:
                            after = pltpu.roll(sum_x_ref[:, y_chunk], LANES - 1 - (y + t) % LANES, 1)
                            after = jnp.where(kinds_ref[1] == 2, 0.0, after - here)
                        else:
                            after = pltpu.roll(rows_ref[j, :, (h + 1) * LANES : (h + 2) * LANES], LANES - 1, 1)
                        x_up = jnp.where(last_lane, after, pltpu.roll(here, LANES - 1, 1))
                        y_up = rows_ref[j + 1, :, part]
                        z_up = jnp.where(last_layer, here, pltpu.roll(here, NZ - 1, 0))
                        found[0].append(star_ref[0, j, :, part] - (x_up - here))
                        found[1].append(star_ref[1, j, :, part] - (y_up - here))
                        found[2].append(star_ref[2, j, :, part] - (z_up - here))
                        found[3].append(here)
                    for channel in range(4):
                        swapped = swap_groups(found[channel], lanes)
                        for g in range(4):
                            blocks_ref[4 * h + g, channel, :, block] = swapped[g]
                return _

            lax.fori_loop(0, B // 4, four_rows, 0)

        flow_out[:, 0] = blocks_ref[col, :3]
        pressure_out[0] = blocks_ref[col, 3]

    return pl.pallas_call(
        kernel,
        grid_spec=pltpu.PrefetchScalarGridSpec(
            num_scalar_prefetch=2,
            grid=(rows_n, cols_n),
            in_specs=[
                pl.BlockSpec((layers, B, x_span), lambda s, c, inv, kinds: (0, s, 0)),
                pl.BlockSpec((layers, 8, x_span), lambda s, c, inv, kinds: (0, jnp.minimum((s + 1) * (B // 8), y_span // 8 - 1), 0)),
                pl.BlockSpec((3, B, NZ, x_span), lambda s, c, inv, kinds: (0, s, 0, 0)),
                pl.BlockSpec((NZ, y_span), lambda s, c, inv, kinds: (0, 0)),
                pl.BlockSpec((NZ, x_span), lambda s, c, inv, kinds: (0, 0)),
                pl.BlockSpec((2, 8 * NZ, 8 * NZ), lambda s, c, inv, kinds: (0, 0, 0)),
            ],
            out_specs=[
                pl.BlockSpec((3, 1, NZ, B * B), lambda s, c, inv, kinds: (0, inv[s * cols_n + c], 0, 0)),
                pl.BlockSpec((1, NZ, B * B), lambda s, c, inv, kinds: (inv[s * cols_n + c], 0, 0)),
            ],
            scratch_shapes=[
                pltpu.VMEM((B + 1, NZ, x_span), f32),
                pltpu.VMEM((cols_n, 4, NZ, B * B), f32),
            ],
        ),
        out_shape=[
            jax.ShapeDtypeStruct((3, slots, NZ, B * B), f32),
            jax.ShapeDtypeStruct((slots, NZ, B * B), f32),
        ],
        compiler_params=params(),
    )(inverse, kinds, modes, modes, star, sum_x, sum_y, cosine_t)


def solve_interfaces(lines_x, lines_y, level, global_tables):
    sine_gx, sine_gy, pick_x, pick_y, eig_x, eig_y = global_tables
    count_x, count_y = lines_x.shape[1], lines_y.shape[1]
    hat_x = jnp.dot(lines_x.reshape(2 * count_x, NY), sine_gy, precision=highest)
    hat_y = jnp.dot(lines_y.reshape(2 * count_y, NX), sine_gx, precision=highest)
    left = jnp.concatenate([pick_x, hat_y], axis=0)
    right = jnp.concatenate([hat_x, pick_y], axis=0)
    field = lax.dot_general(left, right, (((0,), (0,)), ((), ())), precision=highest)
    field = field / (eig_x[:, None] + eig_y[None, :] + level)
    sum_x = hat_x[:count_x] + jnp.dot(pick_x[:count_x], field, precision=highest)
    sum_y = hat_y[:count_y] + lax.dot_general(
        pick_y[:count_y], field, (((1,), (1,)), ((), ())), precision=highest
    )
    return jnp.dot(sum_x, sine_gy, precision=highest), jnp.dot(sum_y, sine_gx, precision=highest)


def shards(tables, velocity, fluid, block_place):
    pa_size = lax.axis_size("pa")
    pb_size = lax.axis_size("pb")
    group_count = pa_size * pb_size
    y_span, x_span = NY // pa_size, NX // pb_size
    rows_n, cols_n = y_span // B, x_span // B
    slots = block_place.shape[0]
    pa, pb = lax.axis_index("pa"), lax.axis_index("pb")

    def kind(index, size):
        return jnp.where(index == 0, 0, jnp.where(index == size - 1, 2, 1)).astype(jnp.int32)

    kinds = jnp.stack([kind(pa, pa_size), kind(pb, pb_size)])
    slot_ids = jnp.arange(slots, dtype=jnp.int32)
    matches = block_place[None, :] == slot_ids[:, None]
    inverse = jnp.sum(jnp.where(matches, slot_ids[None, :], 0), axis=1).astype(jnp.int32)

    tile, low_edge, high_edge = gather_tile(velocity, fluid, inverse, rows_n, cols_n)

    def up(values, axis, size):
        return lax.ppermute(values, axis, [(i, i + 1) for i in range(size - 1)])

    def down(values, axis, size):
        return lax.ppermute(values, axis, [(i + 1, i) for i in range(size - 1)])

    x_below, x_above = up(high_edge, "pb", pb_size), down(low_edge, "pb", pb_size)
    y_below, y_above = up(tile[:3, -1], "pa", pa_size), down(tile[:3, 0], "pa", pa_size)

    cosine = jnp.asarray(tables["cosine"])
    local = {name: jnp.asarray(tables[name]) for name in ("y", "yt", "x", "xt", "edge_y", "edge_x", "eigen", "levels")}
    star, modes, flux_x, flux_y = advance(
        tile, x_below, x_above, y_below, y_above, jnp.asarray(tables["cosine8"]), local["x"], kinds
    )
    spectrum, along_x, along_y = first_solve(
        modes, local["yt"], local["xt"], local["edge_y"], local["edge_x"], local["eigen"], local["levels"], kinds
    )
    flux_x = jnp.dot(cosine, flux_x, precision=highest)
    flux_y = jnp.dot(cosine, flux_y, precision=highest)

    repeats = group_count // NZ
    bundle = jnp.concatenate(
        [
            jnp.concatenate([along_x[:, :2], flux_y[:, None]], axis=1),
            jnp.concatenate([along_y[:, :2], flux_x[:, None]], axis=1),
        ],
        axis=2,
    )
    width = x_span + y_span
    bundle = bundle.reshape(NZ, 3 * width // LANES, LANES)
    bundle = jnp.repeat(bundle, repeats, axis=0) if repeats > 1 else bundle
    arrived = lax.all_to_all(bundle, ("pa", "pb"), split_axis=0, concat_axis=0, tiled=True)
    arrived = arrived.reshape(pa_size, pb_size, 3, width)
    on_y, on_x = arrived[..., :x_span], arrived[..., x_span:]
    sums_y = on_y[:-1, :, 1] + on_y[1:, :, 0]
    lines_y = jnp.stack([sums_y, on_y[:-1, :, 2]]).reshape(2, pa_size - 1, NX)
    sums_x = on_x[:, :-1, 1] + on_x[:, 1:, 0]
    lines_x = jnp.stack([sums_x, on_x[:, :-1, 2]]).transpose(0, 2, 1, 3).reshape(2, pb_size - 1, NY)
    level = local["levels"][(pa * pb_size + pb) // repeats]
    global_tables = [jnp.asarray(tables[name]) for name in ("gx", "gy", "pick_x", "pick_y", "eig_x", "eig_y")]
    sum_x, sum_y = solve_interfaces(lines_x, lines_y, level, global_tables)
    none_y, none_x = jnp.zeros((1, NX), f32), jnp.zeros((1, NY), f32)
    high_y = jnp.concatenate([sum_y, none_y]).reshape(pa_size, pb_size, x_span)
    low_y = jnp.concatenate([none_y, sum_y + lines_y[1]]).reshape(pa_size, pb_size, x_span)
    high_x = jnp.concatenate([sum_x, none_x]).reshape(pb_size, pa_size, y_span).transpose(1, 0, 2)
    low_x = jnp.concatenate([none_x, sum_x + lines_x[1]]).reshape(pb_size, pa_size, y_span).transpose(1, 0, 2)
    reply = jnp.stack([jnp.concatenate([low_y, low_x], axis=2), jnp.concatenate([high_y, high_x], axis=2)], axis=2)
    reply = reply.reshape(group_count, 2 * width // LANES, LANES)
    home = lax.all_to_all(reply, ("pa", "pb"), split_axis=0, concat_axis=0, tiled=True)
    home = home[::repeats].reshape(NZ, 2, width)
    blank = ((0, 0), (0, 6), (0, 0))
    sides_y, sides_x = jnp.pad(home[..., :x_span], blank), jnp.pad(home[..., x_span:], blank)
    pressure_modes = second_solve(
        spectrum, sides_y, sides_x, local["y"], local["yt"], local["x"], local["xt"], local["edge_y"],
        local["edge_x"], local["eigen"], local["levels"], kinds
    )
    beyond_y = jnp.dot(cosine.T, home[:, 1, :x_span], precision=highest)
    beyond_x = jnp.dot(cosine.T, home[:, 1, x_span:], precision=highest)
    return tuple(
        finish(pressure_modes, star, beyond_x, beyond_y, jnp.asarray(tables["cosine8t"]), inverse, kinds, slots)
    )


def make_tables(pa_size, pb_size):
    y_span, x_span = NY // pa_size, NX // pb_size
    cosine, levels = cosine_basis()
    cosine8 = np.einsum("kz,ab->kabz", cosine, np.eye(8)).reshape(8 * NZ, 8 * NZ)
    tables = {
        "cosine": single(cosine),
        "levels": single(levels),
        "cosine8": split(cosine8),
        "cosine8t": split(cosine8.T),
    }
    values = {}
    for name, length in (("y", y_span), ("x", x_span)):
        bases = tile_bases(length)
        tables[name] = np.stack([split(b) for b, _ in bases])
        tables[name + "t"] = np.stack([split(b.T) for b, _ in bases])
        edges = np.zeros((3, 8, length))
        for i, (b, _) in enumerate(bases):
            edges[i, 0], edges[i, 1] = b[0], b[-1]
        tables["edge_" + name] = single(edges)
        values[name] = [v for _, v in bases]
    tables["eigen"] = single(
        np.stack([ey[:, None] + ex[None, :] for ey in values["y"] for ex in values["x"]])
    )
    for name, length, tile, size in (("x", NX, x_span, pb_size), ("y", NY, y_span, pa_size)):
        basis, eig = sine_basis(length, 1.0, 1.0)
        above = basis[tile::tile]
        below = basis[tile - 1 : length - 1 : tile]
        tables["g" + name] = single(basis)
        tables["eig_" + name] = single(eig)
        tables["pick_" + name] = single(np.concatenate([above + below, above]))
    return tables


def solution(mesh):
    tables = make_tables(mesh.shape["pa"], mesh.shape["pb"])
    return jax.shard_map(
        functools.partial(shards, tables),
        mesh=mesh,
        in_specs=(P(None, ("pa", "pb"), None, None), P(("pa", "pb"), None, None), P(("pa", "pb"))),
        out_specs=(P(None, ("pa", "pb"), None, None), P(("pa", "pb"), None, None)),
        check_vma=False,
    )
```

time: 3160 us -> 436 us (0.14)
  local copies, waits for them, and re-layouts: 1570 us -> 7.59 us
  waiting for transfers between devices: 640 us -> 10.3 us
  other arithmetic: 617 us -> 2.36 us
  Pallas kernels: 0 us -> 329 us
  matrix products: 229 us -> 49.2 us
    reshape x15 -> x4, local copies, waits for them, and re-layouts: 671 us -> 1.06 us  [the longest x1 0.81 us: shards(): bundle = bundle.reshape(NZ, 3 * width // LANES, LANES)]
    all_to_all x7 -> x1, waiting for transfers between devices: 636 us -> 10 us  [shards(): lax.all_to_all(bundle, ('pa', 'pb'), split_axis=0, concat_axis=0, tiled=T...]
    pallas_call x0 -> x5, Pallas kernels: none -> 329 us  [the longest x1 98.7 us: finish(): pl.pallas_call(kernel, grid_spec=pltpu.PrefetchScalarGridSpec(num_scalar_...]
    slice x23 -> x6, local copies, waits for them, and re-layouts: 208 us -> 2.07 us  [the longest x1 0.97 us: shards(): along_y[:, :2]]
    dot_general x11, matrix products: 229 us -> 49.2 us  [the longest x1 11.9 us: solve_interfaces(): jnp.dot(lines_y.reshape(2 * count_y, NX), sine_gx, precision=highest)]
    another operation x5 -> x4, other arithmetic: 159 us -> 0.66 us  [the longest x1 0.59 us: shards(): kinds = jnp.stack([kind(pa, pa_size), kind(pb, pb_size)])]
    unnamed x86 -> x41, local copies, waits for them, and re-layouts: 140 us -> 1.2 us
    dynamic_update_slice x62 -> x0, other arithmetic: 120 us -> none  [solve_columns(): lax.scan(eliminate, (first_ratio, first_value), (source[1:], top_flags))]
  transfers between devices with their start and end apart: 11 -> 5, of which waited for: 5 -> 2; matrix products, arithmetic and copies ran while one was open for 15% -> 1% of each run, Pallas kernels for 0% -> 0%
where the time goes in v1:
time: 436 us; the launch traced here: 430 us
  Pallas kernels  329 us (75%)
  matrix products  49.2 us (11%)
  starting transfers between devices  19.9 us (5%)
  waiting for transfers between devices  10.3 us (2%)
  blocking collectives  9.9 us (2%)
  local copies, waits for them, and re-layouts  7.59 us (2%)
    pallas_call x1, Pallas kernels, finish(): pl.pallas_call(kernel, grid_spec=pltpu.PrefetchScalarGridSpec(num_scalar_...  98.7 us
    pallas_call x1, Pallas kernels, gather_tile(): pl.pallas_call(kernel, grid_spec=pltpu.PrefetchScalarGridSpec(num_scalar_...  79.2 us
    pallas_call x1, Pallas kernels, advance(): pl.pallas_call(kernel, grid_spec=pltpu.PrefetchScalarGridSpec(num_scalar_...  63 us
    pallas_call x1, Pallas kernels, second_solve(): pl.pallas_call(kernel, grid_spec=pltpu.PrefetchScalarGridSpec(num_scalar_...  48.9 us
    pallas_call x1, Pallas kernels, first_solve(): pl.pallas_call(kernel, grid_spec=pltpu.PrefetchScalarGridSpec(num_scalar_...  39.7 us
    dot_general x1, matrix products, solve_interfaces(): jnp.dot(lines_y.reshape(2 * count_y, NX), sine_gx, precision=highest)  11.9 us
    all_to_all x1, waiting for transfers between devices, shards(): lax.all_to_all(bundle, ('pa', 'pb'), split_axis=0, concat_axis=0, tiled=T...  10 us
    all_to_all x1, blocking collectives, shards(): lax.all_to_all(reply, ('pa', 'pb'), split_axis=0, concat_axis=0, tiled=True)  9.9 us
  transfers between devices with their start and end apart: 5, of which 2 were waited for; matrix products, arithmetic and copies ran while one was open for 1% of the time, Pallas kernels for 0%

profile of v1, /device:TPU:0, one launch (start us, length us, event | category | flops | bytes accessed | tf_op | source)
XLA Modules:
  0.0 430.1 jit_solution(17119815275312572596)
XLA Ops:
  0.6 1.4 select_reduce_fusion.inverse_ref
  2.0 79.2 %shard_map.203 = (f32[4,256,32,256]{3,2,1,0:T(8,128)}, f32[3,32,256]{2,1,0:T(8,128)}, f32[3,32,256]{2,1,0:T(8,128)}) custom-call(s32[64]{0:T(128)} %select_reduce_fusion.inverse_ref, f32[3,64,32,1024]{3,2,1,0:T(8,128)} %refs_7_.1, f32[3,64,32,1024]{3,2,1,0:T(8,128)} %refs_7_.1, f32[3,64,32,1024]{3,2,1,0:T(8,128)} %refs_7_.1, f32[3,64,32,1024]{3,2,1,0:T(8,128)} %refs_7_.1, ...), custom_call_target="tpu_custom_call" | custom-call | tf_op jit(solution)/shard_map/pallas_call | solution.py:150
  81.2 4.8 %collective-permute-start = (f32[3,32,256]{2,1,0:T(8,128)}, f32[3,32,256]{2,1,0:T(8,128)S(1)}, u32[]{:S(2)}, u32[]{:S(2)}) collective-permute-start(f32[3,32,256]{2,1,0:T(8,128)} %get-tuple-element.13), channel_id=1, source_target_pairs={{0,1},{1,2},{2,3},{3,4},{4,5},{5,6},{6,7},{8,9},{9,10},{10,11},{11... | collective-permute-start | bytes 294920 | tf_op jit(solution)/shard_map/ppermute | solution.py:508
  86.0 1.3 collective-permute-start.1
  87.3 1.0 slice_bitcast_fusion
  88.3 1.3 collective-permute-start.3
  89.6 3.0 collective-permute-start.2
  93.9 0.6 copy-done.5
  94.6 63.0 %shard_map.204 = (f32[3,256,32,256]{3,2,1,0:T(8,128)}, f32[32,256,256]{2,1,0:T(8,128)}, f32[32,256]{1,0:T(8,128)}, f32[32,256]{1,0:T(8,128)}) custom-call(s32[2]{0:T(128)} %pad_add_fusion.kinds_ref, f32[4,256,32,256]{3,2,1,0:T(8,128)} %get-tuple-element.12.main_ref.prev_ref.next_ref, f32[4,256,32,256]{3,2,1,0:T(8,128)} %get-tuple-element.12.main_ref.prev_ref.next_ref, ...), custom_call_target="tpu_custom_call" | custom-call | tf_op jit(solution)/shard_map/pallas_call | solution.py:264
  157.6 0.9 fusion.19
  158.5 0.9 fusion.20
  159.5 39.7 %shard_map.205 = (f32[32,256,256]{2,1,0:T(8,128)}, f32[32,8,256]{2,1,0:T(8,128)}, f32[32,8,256]{2,1,0:T(8,128)}) custom-call(s32[2]{0:T(128)} %pad_add_fusion.kinds_ref, f32[32,256,256]{2,1,0:T(8,128)} %get-tuple-element.15.modes_ref, bf16[3,2,256,256]{3,2,1,0:T(8,128)(2,1)} %constant.66.clone.yt_ref.xt_ref, ...), custom_call_target="tpu_custom_call" | custom-call | tf_op jit(solution)/shard_map/pallas_call | solution.py:315
  199.2 1.0 slice.70
  200.1 1.0 slice.71
  201.2 0.8 reshape.74
  202.1 9.4 %all-to-all-start = ((f32[32,12,128]{2,1,0:T(8,128)}), f32[32,12,128]{2,1,0:T(8,128)S(1)}, u32[]{:S(2)}, u32[]{:S(2)}) async-start(f32[32,12,128]{2,1,0:T(8,128)} %reshape.74), calls=%async_computation | async-start | bytes 524288 | tf_op jit(solution)/shard_map/all_to_all | solution.py:538
  211.5 0.6 dynamic_slice.3
  212.1 10.0 %all-to-all-done = f32[32,12,128]{2,1,0:T(8,128)S(1)} async-done(((f32[32,12,128]{2,1,0:T(8,128)}), f32[32,12,128]{2,1,0:T(8,128)S(1)}, u32[]{:S(2)}, u32[]{:S(2)}) %all-to-all-start) | async-done | bytes 196640 | tf_op jit(solution)/shard_map/all_to_all | solution.py:538
  222.7 4.3 fusion.22
  227.0 11.9 %fusion.21 = f32[6,2048]{1,0:T(8,128)S(1)} fusion(f32[6,2048]{1,0:T(8,128)S(1)} %bitcast.75, f32[2048,2048]{1,0:T(8,128)} %constant.71.clone), kind=kOutput, calls=%fused_computation.43 | convolution fusion | flops 301989888 | bytes 16875520 | tf_op jit(solution)/shard_map/dot_general | solution.py:476
  239.0 8.2 %add_divide_fusion = f32[2048,1024]{1,0:T(8,128)S(1)} fusion(f32[]{:T(128)} %bitcast.9, f32[1024]{0:T(1024)S(1)} %copy-done.12, f32[2048]{0:T(1024)S(1)} %copy-done.11, f32[6,2048]{1,0:T(8,128)S(1)} %fusion.21, f32[14,2048]{1,0:T(8,128)S(1)} %copy-done.9, f32[6,1024]{1,0:T(8,128)S(1)} %copy-done.10, f32[14,1024]{1,0:T(8,128)S(1)} %fusion.22), kind=kOutput, calls=%fused_computation | convolution fusion | flops 509669376 | bytes 8646660 | tf_op jit(solution)/shard_map/dot_general | solution.py:479
  247.3 4.0 convolution_add_fusion.1
  251.3 7.1 %convolution_add_fusion = f32[3,2048]{1,0:T(4,128)S(1)} fusion(f32[3,1024]{1,0:T(4,128)S(1)} %copy-done.7, f32[2048,1024]{1,0:T(8,128)S(1)} %add_divide_fusion, f32[6,2048]{1,0:T(8,128)S(1)} %fusion.21), kind=kOutput, calls=%fused_computation.1 | convolution fusion | flops 75503616 | bytes 8450048 | tf_op jit(solution)/shard_map/dot_general | solution.py:482
  258.4 8.2 %fusion.18 = (f32[3,2048]{1,0:T(4,128)S(1)}, f32[3,2048]{1,0:T(4,128)S(1)}) fusion(f32[3,2048]{1,0:T(4,128)S(1)} %bitcast.80, f32[3,2048]{1,0:T(4,128)S(1)} %convolution_add_fusion, f32[2048,2048]{1,0:T(8,128)S(1)} %bitcast.74), kind=kOutput, calls=%fused_computation.40 | convolution fusion | flops 151001088 | bytes 16875520 | tf_op jit(solution)/shard_map/dot_general | solution.py:485
  266.6 2.1 fusion.17
  269.0 9.9 %all_to_all.10 = f32[32,8,128]{2,1,0:T(8,128)S(1)} all-to-all(f32[32,8,128]{2,1,0:T(8,128)S(1)} %reshape.80), channel_id=1, replica_groups=mesh['pa'=4,'pb'=8] {'pa','pb'}, dimensions={0} | all-to-all | bytes 262144 | tf_op jit(solution)/shard_map/all_to_all | solution.py:555
  279.1 0.8 fusion.6.sum_y_ref
  280.0 0.8 fusion.9.sum_x_ref
  280.8 0.7 pad.12.sides_x_ref
  281.5 0.7 pad.11.sides_y_ref
  282.3 48.9 %shard_map.206.modes_ref.after_ref = f32[32,256,256]{2,1,0:T(8,128)} custom-call(s32[2]{0:T(128)} %pad_add_fusion.kinds_ref, f32[32,256,256]{2,1,0:T(8,128)} %get-tuple-element.16.spectrum_ref, f32[32,8,256]{2,1,0:T(8,128)} %pad.11.sides_y_ref, f32[32,8,256]{2,1,0:T(8,128)} %pad.12.sides_x_ref, bf16[3,2,256,256]{3,2,1,0:T(8,128)(2,1)} %constant.65.clone.sine_ref.y_ref.x_ref, ...), custom_call_target="tpu_custom_call" | custom-call | tf_op jit(solution)/shard_map/pallas_call | solution.py:357
  331.2 98.7 %shard_map.207 = (f32[3,64,32,1024]{3,2,1,0:T(8,128)}, f32[64,32,1024]{2,1,0:T(8,128)}) custom-call(s32[64]{0:T(128)} %select_reduce_fusion.inverse_ref, s32[2]{0:T(128)} %pad_add_fusion.kinds_ref, f32[32,256,256]{2,1,0:T(8,128)} %shard_map.206.modes_ref.after_ref, f32[32,256,256]{2,1,0:T(8,128)} %shard_map.206.modes_ref.after_ref, ...), custom_call_target="tpu_custom_call" | custom-call | tf_op jit(solution)/shard_map/pallas_call | solution.py:442
  (69 shorter events, 2.5 us)
Async XLA Ops:
  81.2 12.1 %collective-permute-start = (f32[3,32,256]{2,1,0:T(8,128)}, f32[3,32,256]{2,1,0:T(8,128)S(1)}, u32[]{:S(2)}, u32[]{:S(2)}) collective-permute-start(f32[3,32,256]{2,1,0:T(8,128)} %get-tuple-element.13), channel_id=1, source_target_pairs={{0,1},{1,2},{2,3},{3,4},{4,5},{5,6},{6,7},{8,9},{9,10},{10,11},{11... | collective-permute-start | bytes 294920 | tf_op jit(solution)/shard_map/ppermute | solution.py:508
  86.0 7.2 %collective-permute-start.1 = (f32[3,32,256]{2,1,0:T(8,128)}, f32[3,32,256]{2,1,0:T(8,128)S(1)}, u32[]{:S(2)}, u32[]{:S(2)}) collective-permute-start(f32[3,32,256]{2,1,0:T(8,128)} %get-tuple-element.14), channel_id=1, source_target_pairs={{1,0},{2,1},{3,2},{4,3},{5,4},{6,5},{7,6},{9,8},{10,9},{11,10},{12... | collective-permute-start | bytes 294920 | tf_op jit(solution)/shard_map/ppermute | solution.py:511
  88.3 5.0 %collective-permute-start.3 = (f32[3,32,256]{2,1,0:T(8,128)S(1)}, f32[3,32,256]{2,1,0:T(8,128)S(1)}, u32[]{:S(2)}, u32[]{:S(2)}) collective-permute-start(f32[3,32,256]{2,1,0:T(8,128)S(1)} %get-tuple-element.22), channel_id=1, source_target_pairs={{8,0},{16,8},{24,16},{9,1},{17,9},{25,17},{10,2},{18,10},{26,18},{... | collective-permute-start | bytes 294920 | tf_op jit(solution)/shard_map/ppermute | solution.py:511
  89.6 4.0 collective-permute-start.2
  93.2 64.3 %copy-start.1 = (f32[32,32]{1,0:T(8,128)S(1)}, f32[32,32]{1,0:T(8,128)}, u32[]{:S(2)}) copy-start(f32[32,32]{1,0:T(8,128)} %constant.64.clone) | copy-start | bytes 12292
  93.2 0.6 copy-start.2
  93.2 0.7 copy-start.3
  93.3 0.7 copy-start.4
  93.9 0.6 copy-start.5
  157.5 54.0 %copy-start.8 = (f32[32]{0:T(128)S(1)}, f32[32]{0:T(128)}, u32[]{:S(2)}) copy-start(f32[32]{0:T(128)} %constant.69.clone.levels_ref) | copy-start | bytes 388
  202.1 20.1 %all-to-all-start = ((f32[32,12,128]{2,1,0:T(8,128)}), f32[32,12,128]{2,1,0:T(8,128)S(1)}, u32[]{:S(2)}, u32[]{:S(2)}) async-start(f32[32,12,128]{2,1,0:T(8,128)} %reshape.74), calls=%async_computation | async-start | bytes 524288 | tf_op jit(solution)/shard_map/all_to_all | solution.py:538
  227.0 12.0 %copy-start.9 = (f32[14,2048]{1,0:T(8,128)S(1)}, f32[14,2048]{1,0:T(8,128)}, u32[]{:S(2)}) copy-start(f32[14,2048]{1,0:T(8,128)} %constant.73.clone) | copy-start | bytes 344068
  227.0 12.0 %copy-start.10 = (f32[6,1024]{1,0:T(8,128)S(1)}, f32[6,1024]{1,0:T(8,128)}, u32[]{:S(2)}) copy-start(f32[6,1024]{1,0:T(8,128)} %constant.74.clone) | copy-start | bytes 73732
  227.0 12.0 %copy-start.11 = (f32[2048]{0:T(1024)S(1)}, f32[2048]{0:T(1024)}, u32[]{:S(2)}) copy-start(f32[2048]{0:T(1024)} %constant.75.clone) | copy-start | bytes 24580
  227.0 12.0 %copy-start.12 = (f32[1024]{0:T(1024)S(1)}, f32[1024]{0:T(1024)}, u32[]{:S(2)}) copy-start(f32[1024]{0:T(1024)} %constant.76.clone) | copy-start | bytes 12292
  238.9 19.5 %slice-start = ((s8[16777216]{0:T(1024)(128)(4,1)}), s8[4194304]{0:T(1024)(128)(4,1)S(1)}, s32[]{:S(2)}) async-start(s8[16777216]{0:T(1024)(128)(4,1)} %bitcast.73), calls=%async_computation.2 | async-start | bytes 8388608
  239.0 8.3 %copy-start.6 = (f32[7,2048]{1,0:T(8,128)S(1)}, f32[7,2048]{1,0:T(8,128)}, u32[]{:S(2)}) copy-start(f32[7,2048]{1,0:T(8,128)} %constant.91) | copy-start | bytes 172036
  239.0 19.4 %slice-start.1 = ((s8[16777216]{0:T(1024)(128)(4,1)}), s8[4194304]{0:T(1024)(128)(4,1)S(1)}, s32[]{:S(2)}) async-start(s8[16777216]{0:T(1024)(128)(4,1)} %bitcast.73), calls=%async_computation.3 | async-start | bytes 8388608
  239.0 19.4 %slice-start.2 = ((s8[16777216]{0:T(1024)(128)(4,1)}), s8[4194304]{0:T(1024)(128)(4,1)S(1)}, s32[]{:S(2)}) async-start(s8[16777216]{0:T(1024)(128)(4,1)} %bitcast.73), calls=%async_computation.4 | async-start | bytes 8388608
  239.0 19.4 %slice-start.3 = ((s8[16777216]{0:T(1024)(128)(4,1)}), s8[4194304]{0:T(1024)(128)(4,1)S(1)}, s32[]{:S(2)}) async-start(s8[16777216]{0:T(1024)(128)(4,1)} %bitcast.73), calls=%async_computation.5 | async-start | bytes 8388608
  247.3 4.0 copy-start.7
  258.4 8.2 %copy-start = (f32[1024,1024]{1,0:T(8,128)S(1)}, f32[1024,1024]{1,0:T(8,128)}, u32[]{:S(2)}) copy-start(f32[1024,1024]{1,0:T(8,128)} %constant.72.clone) | copy-start | bytes 12582916

commit v2 on v1

v2 whole, which is shorter than its diff:
```python
import functools

import jax
import jax.numpy as jnp
import ml_dtypes
import numpy as np
from jax import lax
from jax.experimental import pallas as pl
from jax.experimental.pallas import tpu as pltpu
from jax.sharding import PartitionSpec as P

NX = 2048
NY = 1024
NZ = 32
B = 32
LANES = 128
highest = lax.Precision.HIGHEST
f32 = jnp.float32
VMEM_LIMIT = 56 * 1024 * 1024


def cosine_basis():
    k = np.arange(NZ)[:, None]
    z = np.arange(NZ)[None, :]
    table = np.cos(np.pi * k * (z + 0.5) / NZ)
    table /= np.sqrt((table**2).sum(axis=1, keepdims=True))
    return table, 2.0 - 2.0 * np.cos(np.pi * np.arange(NZ) / NZ)


def sine_basis(length, lower_gap, upper_gap):
    span = length - 1 + lower_gap + upper_gap
    i = np.arange(length)[:, None]
    k = np.arange(1, length + 1)[None, :]
    table = np.sin(np.pi * k * (i + lower_gap) / span)
    table /= np.sqrt((table**2).sum(axis=0, keepdims=True))
    return table, 4.0 * np.sin(np.pi * np.arange(1, length + 1) / (2 * span)) ** 2


def tile_bases(length):
    return [sine_basis(length, *gaps) for gaps in ((1.0, 0.5), (0.5, 0.5), (0.5, 1.0))]


def parts_of(table):
    table = np.asarray(table, np.float64)
    high = table.astype(np.float32).astype(ml_dtypes.bfloat16)
    low = (table - high.astype(np.float64)).astype(np.float32).astype(ml_dtypes.bfloat16)
    return high, low


def split(table):
    return np.stack(parts_of(table), axis=-3)


def left_table(table):
    high, low = parts_of(table)
    return np.concatenate([high, high, low], axis=-1)


def right_table(table):
    high, low = parts_of(table)
    return np.concatenate([high, low, high], axis=-2)


def single(table):
    return np.asarray(table, np.float32)


def pieces(values):
    high = values.astype(jnp.bfloat16)
    return high, (values - high.astype(f32)).astype(jnp.bfloat16)


def mm(left, right):
    return jnp.dot(left, right, preferred_element_type=f32)


def table_times(table_ref, values):
    high, low = pieces(values)
    return mm(table_ref[...], jnp.concatenate([high, low, high], axis=0))


def times_table(values, table_ref):
    high, low = pieces(values)
    return mm(jnp.concatenate([high, high, low], axis=1), table_ref[...])


def few_rows_times(values, high, low, product=mm):
    rows = values.shape[0]
    both = jnp.concatenate(pieces(values), axis=0)
    first = product(both, high)
    return first[:rows] + (first[rows:] + product(both[:rows], low))


def dot_full(left, right, dims):
    return lax.dot_general(left, right, (dims, ((), ())), precision=highest, preferred_element_type=f32)


def lane_ids(rows=NZ):
    return lax.broadcasted_iota(jnp.int32, (rows, LANES), 1)


def swap_groups(four, lanes):
    odd = (lanes & 32) != 0
    high = lanes >= 64
    pairs = [jnp.where(odd, four[(d + 1) % 4], four[d]) for d in range(4)]
    picked = [jnp.where(high, pairs[(d + 2) % 4], pairs[d]) for d in range(4)]
    moved = [picked[0]] + [pltpu.roll(picked[d], 32 * d, 1) for d in range(1, 4)]
    pairs = [jnp.where(odd, moved[(1 - t) % 4], moved[-t % 4]) for t in range(4)]
    return [jnp.where(high, pairs[(t - 2) % 4], pairs[t]) for t in range(4)]


def spread(part):
    high, low = pieces(part)
    return jnp.concatenate([high, high, low], axis=0)


def spread_other(part):
    high, low = pieces(part)
    return jnp.concatenate([high, low, high], axis=0)


def params():
    return pltpu.CompilerParams(vmem_limit_bytes=VMEM_LIMIT)


def gather_tile(velocity, fluid, inverse, rows_n, cols_n):
    y_span, x_span = rows_n * B, cols_n * B
    quads = cols_n // 4

    def kernel(inverse_ref, *refs):
        flow_refs = refs[:cols_n]
        fraction_refs = refs[cols_n : 2 * cols_n]
        out_ref, low_ref, high_ref = refs[2 * cols_n :]
        step = pl.program_id(0)
        lanes = lane_ids()
        place = step % 2
        chunk = pl.ds(pl.multiple_of(step // 2 * LANES, LANES), LANES)
        high_mine = ((lanes & 31) // 16) == place
        low_mine = (((lanes + 1) & 31) // 16) == place
        for channel in range(4):
            low_edge = jnp.zeros((NZ, LANES), f32)
            high_edge = jnp.zeros((NZ, LANES), f32)
            for jq in range(8):
                for quad in range(quads):
                    four = []
                    for g in range(4):
                        at = quad * 4 + g
                        part = slice(jq * LANES, (jq + 1) * LANES)
                        if channel < 3:
                            four.append(flow_refs[at][channel, 0, :, part])
                        else:
                            four.append(fraction_refs[at][0, :, part])
                    rows = swap_groups(four, lanes)
                    for t in range(4):
                        out_ref[channel, jq * 4 + t, :, quad * LANES : (quad + 1) * LANES] = rows[t]
                    if channel < 3 and quad == 0:
                        here = ((lanes + 1) & 31) == 2 * jq
                        low_edge = jnp.where(here, pltpu.roll(four[0], (2 * jq + 127) % LANES, 1), low_edge)
                    if channel < 3 and quad == quads - 1:
                        here = (lanes & 31) == 2 * jq
                        high_edge = jnp.where(here, pltpu.roll(four[3], 97 + 2 * jq, 1), high_edge)
            if channel < 3:
                shift = place * 16
                low_ref[channel, :, chunk] = jnp.where(low_mine, pltpu.roll(low_edge, shift, 1), low_ref[channel, :, chunk])
                high_ref[channel, :, chunk] = jnp.where(
                    high_mine, pltpu.roll(high_edge, shift, 1), high_ref[channel, :, chunk])

    def flow_spec(col):
        return pl.BlockSpec((3, 1, NZ, B * B), lambda s, inv: (0, inv[s * cols_n + col], 0, 0))

    def fraction_spec(col):
        return pl.BlockSpec((1, NZ, B * B), lambda s, inv: (inv[s * cols_n + col], 0, 0))

    edge = pl.BlockSpec((3, NZ, 2 * y_span), lambda s, inv: (0, 0, 0))
    return pl.pallas_call(
        kernel,
        grid_spec=pltpu.PrefetchScalarGridSpec(
            num_scalar_prefetch=1,
            grid=(rows_n,),
            in_specs=[flow_spec(c) for c in range(cols_n)] + [fraction_spec(c) for c in range(cols_n)],
            out_specs=[pl.BlockSpec((4, B, NZ, x_span), lambda s, inv: (0, s, 0, 0)), edge, edge],
        ),
        out_shape=[
            jax.ShapeDtypeStruct((4, y_span, NZ, x_span), f32),
            jax.ShapeDtypeStruct((3, NZ, 2 * y_span), f32),
            jax.ShapeDtypeStruct((3, NZ, 2 * y_span), f32),
        ],
        compiler_params=params(),
    )(inverse, *([velocity] * cols_n), *([fluid] * cols_n))


def advance(tile, x_below, x_above, y_below, y_above, cosine, sine_x, kinds):
    _, y_span, _, x_span = tile.shape
    steps = y_span // B
    chunks = x_span // LANES

    def kernel(kinds_ref, main_ref, prev_ref, next_ref, xb_ref, xa_ref, yb_ref, ya_ref, cosine_ref, sine_ref,
               star_ref, modes_ref, gx_ref, gy_ref, rows_ref, source_ref, carry_ref):
        step = pl.program_id(0)
        lanes = lane_ids()
        layers = lax.broadcasted_iota(jnp.int32, (NZ, LANES), 0)
        first_layer, last_layer = layers == 0, layers == NZ - 1
        first_lane, last_lane = lanes == 0, lanes == LANES - 1

        rows_ref[:, 1 : B + 1] = main_ref[:3]

        @pl.when(step == 0)
        def _():
            rows_ref[:, 0] = yb_ref[...]
            carry_ref[...] = jnp.zeros_like(carry_ref)

        @pl.when(step > 0)
        def _():
            rows_ref[:, 0] = prev_ref[:3, 0]

        @pl.when(step == steps - 1)
        def _():
            rows_ref[:, B + 1] = ya_ref[...]

        @pl.when(step < steps - 1)
        def _():
            rows_ref[:, B + 1] = next_ref[:3, 0]

        y_chunk = pl.ds(pl.multiple_of(step // 4 * LANES, LANES), LANES)
        halo_chunk = pl.ds(pl.multiple_of(step // 2 * LANES, LANES), LANES)
        even_lane = (lanes & 1) == 0

        def row(group, r):
            j = group * 8 + r
            held = r % 4 * 32 + (step % 2) * 16 + 2 * (group * 2 + r // 4)
            at = (step % 4) * B + j
            star = {}
            flow = {}
            for h in range(chunks):
                for c in range(3):
                    flow[c, h] = rows_ref[c, j + 1, :, h * LANES : (h + 1) * LANES]
            edge, to_right, to_left = {}, {}, {}
            for c in range(3):
                both = jnp.where(even_lane, xb_ref[c, :, halo_chunk], xa_ref[c, :, halo_chunk])
                edge[c] = pltpu.roll(both, (LANES - held) % LANES, 1)
                for h in range(chunks):
                    to_right[c, h] = pltpu.roll(flow[c, h], 1, 1)
                    to_left[c, h] = pltpu.roll(flow[c, h], LANES - 1, 1)
            for h in range(chunks):
                part = slice(h * LANES, (h + 1) * LANES)
                take_up, take_down = [], []
                for e in range(3):
                    scaled = 0.125 * flow[e, h]
                    take_up.append(0.025 - scaled)
                    take_down.append(0.025 + scaled)
                fraction = main_ref[3, j, :, part]
                for c in range(3):
                    center = flow[c, h]
                    before = edge[c] if h == 0 else to_right[c, h - 1]
                    after = edge[c] if h == chunks - 1 else to_left[c, h + 1]
                    x_low = jnp.where(first_lane, before, to_right[c, h])
                    x_up = jnp.where(last_lane, after, to_left[c, h])
                    y_low = rows_ref[c, j, :, part]
                    y_up = rows_ref[c, j + 2, :, part]
                    z_low = jnp.where(first_layer, 0.0, pltpu.roll(center, 1, 0))
                    z_up = jnp.where(last_layer, 0.0, pltpu.roll(center, NZ - 1, 0))
                    total = (
                        0.85 * center
                        + (take_up[0] * x_up + take_down[0] * x_low)
                        + (take_up[1] * y_up + take_down[1] * y_low)
                        + (take_up[2] * z_up + take_down[2] * z_low)
                    )
                    value = fraction * total
                    if c == 2:
                        value = jnp.where(last_layer, 0.0, value)
                    star[c, h] = value
                    star_ref[c, j, :, part] = value
            before = 0.0
            for h in range(chunks):
                part = slice(h * LANES, (h + 1) * LANES)
                moved = pltpu.roll(star[0, h], 1, 1)
                x_low = jnp.where(first_lane, before, moved)
                before = moved
                z_low = jnp.where(first_layer, 0.0, pltpu.roll(star[2, h], 1, 0))
                y_low = carry_ref[:, part]
                source_ref[j, :, part] = (x_low - star[0, h]) + (y_low - star[1, h]) + (z_low - star[2, h])
                carry_ref[:, part] = star[1, h]
            edge = pltpu.roll(star[0, chunks - 1], (at + 1) % LANES, 1)
            gx_ref[:, y_chunk] = jnp.where(lanes == at, edge, gx_ref[:, y_chunk])

        def transform(group):
            rows = pl.ds(pl.multiple_of(group * 8, 8), 8)
            part = source_ref[rows].reshape(8 * NZ, x_span)
            modes = times_table(table_times(cosine_ref, part), sine_ref)
            modes_ref[:, rows, :] = modes.reshape(NZ, 8, x_span)

        for r in range(8):
            row(0, r)

        def group_of_rows(group, _):
            transform(group - 1)
            for r in range(8):
                row(group, r)
            return _

        lax.fori_loop(1, B // 8, group_of_rows, 0)
        transform(B // 8 - 1)
        gy_ref[...] = carry_ref[...]

    full3 = pl.BlockSpec((3, NZ, 2 * y_span), lambda s, kinds: (0, 0, 0))
    return pl.pallas_call(
        kernel,
        grid_spec=pltpu.PrefetchScalarGridSpec(
            num_scalar_prefetch=1,
            grid=(steps,),
            in_specs=[
                pl.BlockSpec((4, B, NZ, x_span), lambda s, kinds: (0, s, 0, 0)),
                pl.BlockSpec((4, 1, NZ, x_span), lambda s, kinds: (0, jnp.maximum(s * B - 1, 0), 0, 0)),
                pl.BlockSpec((4, 1, NZ, x_span), lambda s, kinds: (0, jnp.minimum(s * B + B, y_span - 1), 0, 0)),
                full3,
                full3,
                pl.BlockSpec((3, NZ, x_span), lambda s, kinds: (0, 0, 0)),
                pl.BlockSpec((3, NZ, x_span), lambda s, kinds: (0, 0, 0)),
                pl.BlockSpec((8 * NZ, 24 * NZ), lambda s, kinds: (0, 0)),
                pl.BlockSpec((None, 3 * x_span, x_span), lambda s, kinds: (kinds[1], 0, 0)),
            ],
            out_specs=[
                pl.BlockSpec((3, B, NZ, x_span), lambda s, kinds: (0, s, 0, 0)),
                pl.BlockSpec((NZ, B, x_span), lambda s, kinds: (0, s, 0)),
                pl.BlockSpec((NZ, y_span), lambda s, kinds: (0, 0)),
                pl.BlockSpec((NZ, x_span), lambda s, kinds: (0, 0)),
            ],
            scratch_shapes=[
                pltpu.VMEM((3, B + 2, NZ, x_span), f32),
                pltpu.VMEM((B, NZ, x_span), f32),
                pltpu.VMEM((NZ, x_span), f32),
            ],
        ),
        out_shape=[
            jax.ShapeDtypeStruct((3, y_span, NZ, x_span), f32),
            jax.ShapeDtypeStruct((NZ, y_span, x_span), f32),
            jax.ShapeDtypeStruct((NZ, y_span), f32),
            jax.ShapeDtypeStruct((NZ, x_span), f32),
        ],
        compiler_params=params(),
    )(kinds, tile, tile, tile, x_below, x_above, y_below, y_above, cosine, sine_x)


def first_solve(modes, sine_y, sine_yt, sine_xt, edge_y, edge_xt, eigen, levels, flux_x, flux_y, cosine, kinds):
    layers, y_span, x_span = modes.shape
    batch = 4
    steps = layers // batch
    sides = 2 * layers

    def kernel(kinds_ref, modes_ref, y_ref, yt_ref, xt_ref, edge_y_ref, edge_xt_ref, eigen_ref, levels_ref,
               flux_x_ref, flux_y_ref, cosine_ref, spectrum_ref, bundle_ref, rows_ref, columns_ref):
        step = pl.program_id(0)
        row_ids = lax.broadcasted_iota(jnp.int32, (sides, y_span), 0)
        column_ids = lax.broadcasted_iota(jnp.int32, (x_span, LANES), 1)

        @pl.when(step == 0)
        def _():
            rows_ref[...] = jnp.zeros_like(rows_ref)
            columns_ref[...] = jnp.zeros_like(columns_ref)

        row_sum, column_sum = [], []
        for i in range(batch):
            k = step * batch + i
            spectrum = table_times(yt_ref, modes_ref[i])
            spectrum_ref[i] = spectrum
            high, low = pieces(spectrum / (eigen_ref[...] + levels_ref[k]))
            edge_high, edge_low = pieces(jnp.where(row_ids % layers == k, edge_y_ref[...], 0.0))
            edges = jnp.concatenate([edge_high, edge_low], axis=0)
            found = mm(edges, high)
            row_sum.append(found[:sides] + (found[sides:] + mm(edge_high, low)))
            edge_high, edge_low = pieces(jnp.where(column_ids % layers == k, edge_xt_ref[...], 0.0))
            column_sum.append(mm(
                jnp.concatenate([high, high, low], axis=1),
                jnp.concatenate([edge_high, edge_low, edge_high], axis=0)))
        rows_ref[...] += (row_sum[0] + row_sum[1]) + (row_sum[2] + row_sum[3])
        columns_ref[...] += (column_sum[0] + column_sum[1]) + (column_sum[2] + column_sum[3])

        @pl.when(step == steps - 1)
        def _():
            along_x = times_table(rows_ref[...], xt_ref)
            along_y = table_times(y_ref, columns_ref[...]).T[:sides]
            cosine_table = cosine_ref[...]
            for line, values, flux_ref in ((0, along_x, flux_y_ref), (x_span, along_y, flux_x_ref)):
                part = slice(line, line + values.shape[1])
                bundle_ref[0, :, part] = values[:layers]
                bundle_ref[1, :, part] = values[layers:]
                bundle_ref[2, :, part] = dot_full(cosine_table, flux_ref[...], ((1,), (0,)))

    return pl.pallas_call(
        kernel,
        grid_spec=pltpu.PrefetchScalarGridSpec(
            num_scalar_prefetch=1,
            grid=(steps,),
            in_specs=[
                pl.BlockSpec((batch, y_span, x_span), lambda k, kinds: (k, 0, 0)),
                pl.BlockSpec((None, y_span, 3 * y_span), lambda k, kinds: (kinds[0], 0, 0)),
                pl.BlockSpec((None, y_span, 3 * y_span), lambda k, kinds: (kinds[0], 0, 0)),
                pl.BlockSpec((None, 3 * x_span, x_span), lambda k, kinds: (kinds[1], 0, 0)),
                pl.BlockSpec((None, sides, y_span), lambda k, kinds: (kinds[0], 0, 0)),
                pl.BlockSpec((None, x_span, LANES), lambda k, kinds: (kinds[1], 0, 0)),
                pl.BlockSpec((None, y_span, x_span), lambda k, kinds: (kinds[0] * 3 + kinds[1], 0, 0)),
                pl.BlockSpec(memory_space=pltpu.SMEM),
                pl.BlockSpec((layers, y_span), lambda k, kinds: (0, 0)),
                pl.BlockSpec((layers, x_span), lambda k, kinds: (0, 0)),
                pl.BlockSpec((layers, layers), lambda k, kinds: (0, 0)),
            ],
            out_specs=[
                pl.BlockSpec((batch, y_span, x_span), lambda k, kinds: (k, 0, 0)),
                pl.BlockSpec((3, layers, x_span + y_span), lambda k, kinds: (0, 0, 0)),
            ],
            scratch_shapes=[pltpu.VMEM((sides, x_span), f32), pltpu.VMEM((y_span, LANES), f32)],
        ),
        out_shape=[
            jax.ShapeDtypeStruct((layers, y_span, x_span), f32),
            jax.ShapeDtypeStruct((3, layers, x_span + y_span), f32),
        ],
        compiler_params=params(),
    )(kinds, modes, sine_y, sine_yt, sine_xt, edge_y, edge_xt, eigen, levels, flux_x, flux_y, cosine)


def second_solve(spectrum, sums, sine_y, sine_yr, sine_x, sine_xt, edge_y, edge_x, eigen, levels, kinds):
    layers, y_span, x_span = spectrum.shape
    batch = 4
    sides = 2 * layers

    def kernel(kinds_ref, spectrum_ref, sums_ref, y_ref, yr_ref, x_ref, xt_ref, edge_y_ref, edge_x_ref,
               eigen_ref, levels_ref, out_ref, left_ref, right_ref):
        step = pl.program_id(0)

        @pl.when(step == 0)
        def _():
            right_ref[:sides] = edge_x_ref[...]
            right_ref[sides:] = times_table(sums_ref[:, :x_span], x_ref)
            left = jnp.concatenate([times_table(sums_ref[:, x_span:], yr_ref), edge_y_ref[...]], axis=0)
            left_high, left_low = pieces(left.T)
            left_ref[...] = jnp.concatenate([left_high, left_high, left_low], axis=1)

        row_ids = lax.broadcasted_iota(jnp.int32, (2 * sides, x_span), 0) % layers
        for i in range(batch):
            k = step * batch + i
            high, low = pieces(jnp.where(row_ids == k, right_ref[...], 0.0))
            added = mm(left_ref[...], jnp.concatenate([high, low, high], axis=0))
            solved = (spectrum_ref[i] + added) / (eigen_ref[...] + levels_ref[k])
            out_ref[i] = times_table(table_times(y_ref, solved), xt_ref)

    return pl.pallas_call(
        kernel,
        grid_spec=pltpu.PrefetchScalarGridSpec(
            num_scalar_prefetch=1,
            grid=(layers // batch,),
            in_specs=[
                pl.BlockSpec((batch, y_span, x_span), lambda k, kinds: (k, 0, 0)),
                pl.BlockSpec((sides, x_span + y_span), lambda k, kinds: (0, 0)),
                pl.BlockSpec((None, y_span, 3 * y_span), lambda k, kinds: (kinds[0], 0, 0)),
                pl.BlockSpec((None, 3 * y_span, y_span), lambda k, kinds: (kinds[0], 0, 0)),
                pl.BlockSpec((None, 3 * x_span, x_span), lambda k, kinds: (kinds[1], 0, 0)),
                pl.BlockSpec((None, 3 * x_span, x_span), lambda k, kinds: (kinds[1], 0, 0)),
                pl.BlockSpec((None, sides, y_span), lambda k, kinds: (kinds[0], 0, 0)),
                pl.BlockSpec((None, sides, x_span), lambda k, kinds: (kinds[1], 0, 0)),
                pl.BlockSpec((None, y_span, x_span), lambda k, kinds: (kinds[0] * 3 + kinds[1], 0, 0)),
                pl.BlockSpec(memory_space=pltpu.SMEM),
            ],
            out_specs=pl.BlockSpec((batch, y_span, x_span), lambda k, kinds: (k, 0, 0)),
            scratch_shapes=[
                pltpu.VMEM((y_span, 6 * sides), jnp.bfloat16),
                pltpu.VMEM((2 * sides, x_span), f32),
            ],
        ),
        out_shape=jax.ShapeDtypeStruct((layers, y_span, x_span), f32),
        compiler_params=params(),
    )(kinds, spectrum, sums, sine_y, sine_yr, sine_x, sine_xt, edge_y, edge_x, eigen, levels)


def finish(modes, star, sums, cosine_inverse, cosine_t, inverse, kinds, slots):
    layers, y_span, x_span = modes.shape
    rows_n, cols_n = y_span // B, x_span // B
    chunks = x_span // LANES

    def kernel(inverse_ref, kinds_ref, modes_ref, after_ref, star_ref, sums_ref, inverse_cosine_ref, cosine_ref,
               flow_out, pressure_out, rows_ref, blocks_ref, beyond_ref, flow_sem, pressure_sem):
        step = pl.program_id(0)
        half = step % 2

        def copies(at_step, at_half):
            found = []
            for col in range(cols_n):
                slot = inverse_ref[at_step * cols_n + col]
                found.append(pltpu.make_async_copy(
                    blocks_ref.at[at_half, col, pl.ds(0, 3)], flow_out.at[:, slot], flow_sem.at[at_half, col]))
                found.append(pltpu.make_async_copy(
                    blocks_ref.at[at_half, col, 3], pressure_out.at[slot], pressure_sem.at[at_half, col]))
            return found

        @pl.when(step >= 2)
        def _():
            for copy in copies(step - 2, half):
                copy.wait()

        @pl.when(step == 0)
        def _():
            beyond_ref[...] = dot_full(inverse_cosine_ref[...], sums_ref[layers:], ((1,), (0,)))

        lanes = lane_ids()
        layers_at = lax.broadcasted_iota(jnp.int32, (NZ, LANES), 0)
        last_layer = layers_at == NZ - 1
        last_lane = lanes == LANES - 1
        for q in range(B // 8):
            part = modes_ref[:, 8 * q : 8 * q + 8, :].reshape(8 * NZ, x_span)
            rows_ref[8 * q : 8 * q + 8] = table_times(cosine_ref, part).reshape(8, NZ, x_span)

        @pl.when(step < rows_n - 1)
        def _():
            part = after_ref[...].reshape(8 * NZ, x_span)
            rows_ref[B] = table_times(cosine_ref, part).reshape(8, NZ, x_span)[0]

        @pl.when(step == rows_n - 1)
        def _():
            rows_ref[B] = jnp.where(kinds_ref[0] == 2, 0.0, beyond_ref[:, :x_span] - rows_ref[B - 1])

        def four_rows(jq, _):
            y = step * B + jq * 4
            y_chunk = pl.ds(pl.multiple_of(x_span + y // LANES * LANES, LANES), LANES)
            block = pl.ds(pl.multiple_of(jq * LANES, LANES), LANES)
            to_left = [
                [pltpu.roll(rows_ref[jq * 4 + t, :, h * LANES : (h + 1) * LANES], LANES - 1, 1) for t in range(4)]
                for h in range(chunks)
            ]
            for h in range(chunks):
                part = slice(h * LANES, (h + 1) * LANES)
                found = [[], [], [], []]
                for t in range(4):
                    j = jq * 4 + t
                    here = rows_ref[j, :, part]
                    if h == chunks - 1:
                        after = pltpu.roll(beyond_ref[:, y_chunk], LANES - 1 - (y + t) % LANES, 1)
                        after = jnp.where(kinds_ref[1] == 2, 0.0, after - here)
                    else:
                        after = to_left[h + 1][t]
                    x_up = jnp.where(last_lane, after, to_left[h][t])
                    y_up = rows_ref[j + 1, :, part]
                    z_up = jnp.where(last_layer, here, pltpu.roll(here, NZ - 1, 0))
                    found[0].append(star_ref[0, j, :, part] - (x_up - here))
                    found[1].append(star_ref[1, j, :, part] - (y_up - here))
                    found[2].append(star_ref[2, j, :, part] - (z_up - here))
                    found[3].append(here)
                for channel in range(4):
                    swapped = swap_groups(found[channel], lanes)
                    for g in range(4):
                        blocks_ref[half, 4 * h + g, channel, :, block] = swapped[g]
            return _

        lax.fori_loop(0, B // 4, four_rows, 0)

        for copy in copies(step, half):
            copy.start()

        @pl.when(step == rows_n - 1)
        def _():
            for copy in copies(step - 1, 1 - half) + copies(step, half):
                copy.wait()

    return pl.pallas_call(
        kernel,
        grid_spec=pltpu.PrefetchScalarGridSpec(
            num_scalar_prefetch=2,
            grid=(rows_n,),
            in_specs=[
                pl.BlockSpec((layers, B, x_span), lambda s, inv, kinds: (0, s, 0)),
                pl.BlockSpec((layers, 8, x_span), lambda s, inv, kinds: (0, jnp.minimum((s + 1) * (B // 8), y_span // 8 - 1), 0)),
                pl.BlockSpec((3, B, NZ, x_span), lambda s, inv, kinds: (0, s, 0, 0)),
                pl.BlockSpec((2 * layers, x_span + y_span), lambda s, inv, kinds: (0, 0)),
                pl.BlockSpec((layers, layers), lambda s, inv, kinds: (0, 0)),
                pl.BlockSpec((8 * NZ, 24 * NZ), lambda s, inv, kinds: (0, 0)),
            ],
            out_specs=[pl.BlockSpec(memory_space=pl.ANY), pl.BlockSpec(memory_space=pl.ANY)],
            scratch_shapes=[
                pltpu.VMEM((B + 1, NZ, x_span), f32),
                pltpu.VMEM((2, cols_n, 4, NZ, B * B), f32),
                pltpu.VMEM((NZ, x_span + y_span), f32),
                pltpu.SemaphoreType.DMA((2, cols_n)),
                pltpu.SemaphoreType.DMA((2, cols_n)),
            ],
        ),
        out_shape=[
            jax.ShapeDtypeStruct((3, slots, NZ, B * B), f32),
            jax.ShapeDtypeStruct((slots, NZ, B * B), f32),
        ],
        compiler_params=params(),
    )(inverse, kinds, modes, modes, star, sums, cosine_inverse, cosine_t)


def solve_interfaces(lines_x, lines_y, picks_x, picks_y, table_x, table_y, eig_x, eig_y, levels, kinds):
    rows_x, rows_y = lines_x.shape[0], lines_y.shape[1]
    half_x = lines_y.shape[2]
    width = min(256, half_x)

    def kernel(kinds_ref, lines_x_ref, lines_y_ref, picks_x_ref, picks_y_ref, table_x_ref, table_y_ref, eig_x_ref,
               eig_y_ref, levels_ref, sum_x_ref, fold_ref, hat_ref, out_hat_ref):
        level = levels_ref[kinds_ref[2]]
        hat_x = few_rows_times(lines_x_ref[...], table_y_ref[0], table_y_ref[1])
        for parity in range(2):
            hat_ref[:, parity * half_x : (parity + 1) * half_x] = few_rows_times(
                lines_y_ref[parity], table_x_ref[parity, 0], table_x_ref[parity, 1])
        right = spread(jnp.concatenate([hat_x, picks_y_ref[0]], axis=0))

        def transposed(a, b):
            return lax.dot_general(a, b, (((1,), (1,)), ((), ())), preferred_element_type=f32)

        along = jnp.zeros((rows_x, NY), f32)
        for start in range(0, 2 * half_x, width):
            part = slice(start, start + width)
            left = spread_other(jnp.concatenate([picks_x_ref[0, :, part], hat_ref[:, part]], axis=0))
            field = lax.dot_general(left, right, (((0,), (0,)), ((), ())), preferred_element_type=f32)
            field = field / (eig_x_ref[part, :1] + eig_y_ref[:1] + level)
            high, low = pieces(field)
            along += few_rows_times(picks_x_ref[1, :, part], high, low)
            out_hat_ref[:, part] = hat_ref[:, part] + few_rows_times(picks_y_ref[1], high, low, transposed)
        sum_x_ref[...] = few_rows_times(hat_x + along, table_y_ref[0], table_y_ref[1])
        for parity in range(2):
            fold_ref[parity] = few_rows_times(
                out_hat_ref[:, parity * half_x : (parity + 1) * half_x],
                table_x_ref[parity, 0], table_x_ref[parity, 1], transposed)

    vmem = pl.BlockSpec(memory_space=pltpu.VMEM)
    return pl.pallas_call(
        kernel,
        grid_spec=pltpu.PrefetchScalarGridSpec(
            num_scalar_prefetch=1,
            grid=(),
            in_specs=[vmem] * 8 + [pl.BlockSpec(memory_space=pltpu.SMEM)],
            out_specs=[vmem, vmem],
            scratch_shapes=[pltpu.VMEM((rows_y, NX), f32), pltpu.VMEM((rows_y, NX), f32)],
        ),
        out_shape=[
            jax.ShapeDtypeStruct((rows_x, NY), f32),
            jax.ShapeDtypeStruct((2, rows_y, half_x), f32),
        ],
        compiler_params=params(),
    )(kinds, lines_x, lines_y, picks_x, picks_y, table_x, table_y, eig_x, eig_y, levels)


def padded_rows(count):
    return -(-2 * count // 16) * 16


def shards(tables, velocity, fluid, block_place):
    pa_size = lax.axis_size("pa")
    pb_size = lax.axis_size("pb")
    group_count = pa_size * pb_size
    y_span, x_span = NY // pa_size, NX // pb_size
    rows_n, cols_n = y_span // B, x_span // B
    slots = block_place.shape[0]
    pa, pb = lax.axis_index("pa"), lax.axis_index("pb")

    def kind(index, size):
        return jnp.where(index == 0, 0, jnp.where(index == size - 1, 2, 1)).astype(jnp.int32)

    repeats = group_count // NZ
    kinds = jnp.stack([kind(pa, pa_size), kind(pb, pb_size), (pa * pb_size + pb) // repeats])
    slot_ids = jnp.arange(slots, dtype=jnp.int32)
    matches = block_place[None, :] == slot_ids[:, None]
    inverse = jnp.sum(jnp.where(matches, slot_ids[None, :], 0), axis=1).astype(jnp.int32)

    tile, low_edge, high_edge = gather_tile(velocity, fluid, inverse, rows_n, cols_n)

    def up(values, axis, size):
        return lax.ppermute(values, axis, [(i, i + 1) for i in range(size - 1)])

    def down(values, axis, size):
        return lax.ppermute(values, axis, [(i + 1, i) for i in range(size - 1)])

    x_below, x_above = up(high_edge, "pb", pb_size), down(low_edge, "pb", pb_size)
    y_below, y_above = up(tile[:3, -1], "pa", pa_size), down(tile[:3, 0], "pa", pa_size)

    cosine = jnp.asarray(tables["cosine"])
    local = {name: jnp.asarray(tables[name]) for name in (
        "y", "yr", "yt", "x", "xt", "edge_y", "edge_x", "edge_xt", "eigen", "levels", "picks_x", "picks_y", "fold_x", "line_y",
        "eig_x", "eig_y")}
    star, modes, flux_x, flux_y = advance(
        tile, x_below, x_above, y_below, y_above, jnp.asarray(tables["cosine8"]), local["x"], kinds
    )
    spectrum, bundle = first_solve(
        modes, local["y"], local["yt"], local["xt"], local["edge_y"], local["edge_xt"], local["eigen"],
        local["levels"], flux_x, flux_y, cosine, kinds
    )
    width = x_span + y_span
    bundle = jnp.repeat(bundle, repeats, axis=1) if repeats > 1 else bundle
    arrived = lax.all_to_all(bundle, ("pa", "pb"), split_axis=1, concat_axis=1, tiled=True)
    arrived = arrived.reshape(3, pa_size, pb_size, width)
    on_y, on_x = arrived[..., :x_span], arrived[..., x_span:]
    count_y, count_x = pa_size - 1, pb_size - 1
    rows_y, rows_x = padded_rows(count_y), padded_rows(count_x)
    sums_y = on_y[1, :-1] + on_y[0, 1:]
    lines_y = jnp.concatenate([sums_y, on_y[2, :-1]]).reshape(2 * count_y, NX)
    lines_y = jnp.pad(lines_y, ((0, rows_y - 2 * count_y), (0, 0)))
    sums_x = on_x[1, :, :-1] + on_x[0, :, 1:]
    lines_x = jnp.stack([sums_x, on_x[2, :, :-1]]).transpose(0, 2, 1, 3).reshape(2 * count_x, NY)
    lines_x = jnp.pad(lines_x, ((0, rows_x - 2 * count_x), (0, 0)))
    lower, upper = lines_y[:, : NX // 2], lines_y[:, NX // 2 :][:, ::-1]
    sum_x, folded = solve_interfaces(
        lines_x, jnp.stack([lower + upper, lower - upper]), local["picks_x"], local["picks_y"], local["fold_x"],
        local["line_y"], local["eig_x"], local["eig_y"], local["levels"], kinds
    )
    sum_x = sum_x[:count_x]
    even, odd = folded[0, :count_y], folded[1, :count_y]
    sum_y = jnp.concatenate([even + odd, (even - odd)[:, ::-1]], axis=1)
    flux_y, flux_x = lines_y[count_y : 2 * count_y], lines_x[count_x : 2 * count_x]
    none_y, none_x = jnp.zeros((1, NX), f32), jnp.zeros((1, NY), f32)
    high_y = jnp.concatenate([sum_y, none_y]).reshape(pa_size, pb_size, x_span)
    low_y = jnp.concatenate([none_y, sum_y + flux_y]).reshape(pa_size, pb_size, x_span)
    high_x = jnp.concatenate([sum_x, none_x]).reshape(pb_size, pa_size, y_span).transpose(1, 0, 2)
    low_x = jnp.concatenate([none_x, sum_x + flux_x]).reshape(pb_size, pa_size, y_span).transpose(1, 0, 2)
    reply = jnp.stack([jnp.concatenate([low_y, low_x], axis=2), jnp.concatenate([high_y, high_x], axis=2)])
    reply = reply.reshape(2, group_count, width)
    home = lax.all_to_all(reply, ("pa", "pb"), split_axis=1, concat_axis=1, tiled=True)
    sums = home[:, ::repeats].reshape(2 * NZ, width)
    pressure_modes = second_solve(
        spectrum, sums, local["y"], local["yr"], local["x"], local["xt"], local["edge_y"], local["edge_x"],
        local["eigen"], local["levels"], kinds
    )
    return tuple(
        finish(pressure_modes, star, sums, jnp.asarray(tables["cosine_t"]), jnp.asarray(tables["cosine8t"]), inverse,
               kinds, slots)
    )


def make_tables(pa_size, pb_size):
    y_span, x_span = NY // pa_size, NX // pb_size
    cosine, levels = cosine_basis()
    cosine8 = np.einsum("kz,ab->kabz", cosine, np.eye(8)).reshape(8 * NZ, 8 * NZ)
    tables = {
        "cosine": single(cosine),
        "levels": single(levels),
        "cosine_t": single(cosine.T),
        "cosine8": left_table(cosine8),
        "cosine8t": left_table(cosine8.T),
    }
    values = {}
    for name, length in (("y", y_span), ("x", x_span)):
        bases = tile_bases(length)
        if name == "x":
            tables["x"] = np.stack([right_table(b) for b, _ in bases])
            tables["xt"] = np.stack([right_table(b.T) for b, _ in bases])
        else:
            tables["y"] = np.stack([left_table(b) for b, _ in bases])
            tables["yr"] = np.stack([right_table(b) for b, _ in bases])
            tables["yt"] = np.stack([left_table(b.T) for b, _ in bases])
        edges = np.stack([np.repeat(b[[0, -1]], NZ, axis=0) for b, _ in bases])
        tables["edge_" + name] = single(edges)
        blank = np.zeros((3, length, LANES - 2 * NZ))
        tables["edge_" + name + "t"] = single(np.concatenate([edges.transpose(0, 2, 1), blank], axis=2))
        values[name] = [v for _, v in bases]
    tables["eigen"] = single(
        np.stack([ey[:, None] + ex[None, :] for ey in values["y"] for ex in values["x"]])
    )
    basis_x, eig_x = sine_basis(NX, 1.0, 1.0)
    basis_y, eig_y = sine_basis(NY, 1.0, 1.0)
    half = NX // 2
    order = np.concatenate([np.arange(0, NX, 2), np.arange(1, NX, 2)])
    tables["fold_x"] = np.stack([split(basis_x[:half, parity::2]) for parity in range(2)])
    tables["line_y"] = split(basis_y)
    tables["eig_x"] = single(np.repeat(eig_x[order][:, None], LANES, axis=1))
    tables["eig_y"] = single(np.repeat(eig_y[None, :], 8, axis=0))
    for name, basis, tile in (("x", basis_x[:, order], x_span), ("y", basis_y, y_span)):
        above, below = basis[tile::tile], basis[tile - 1 : -1 : tile]
        count, length = above.shape
        picks = np.zeros((2, padded_rows(count), length))
        picks[0, : 2 * count] = np.concatenate([above + below, above])
        picks[1, :count] = above + below
        tables["picks_" + name] = single(picks)
    return tables


def solution(mesh):
    tables = make_tables(mesh.shape["pa"], mesh.shape["pb"])
    return jax.shard_map(
        functools.partial(shards, tables),
        mesh=mesh,
        in_specs=(P(None, ("pa", "pb"), None, None), P(("pa", "pb"), None, None), P(("pa", "pb"))),
        out_specs=(P(None, ("pa", "pb"), None, None), P(("pa", "pb"), None, None)),
        check_vma=False,
    )
```

time: 436 us -> 221 us (0.51); the launches traced: 430 us -> 221 us
  Pallas kernels: 329 us -> 167 us
  matrix products: 49.2 us -> 0 us
  blocking collectives: 9.9 us -> 29.7 us
  starting transfers between devices: 19.9 us -> 10.5 us
  waiting for transfers between devices: 10.3 us -> 1.27 us
    pallas_call x1, Pallas kernels: 98.7 us -> 34.8 us  [finish(): pl.pallas_call(kernel, grid_spec=pltpu.PrefetchScalarGridSpec(num_scalar_...]
    pallas_call x1, Pallas kernels: 79.2 us -> 26.9 us  [gather_tile(): pl.pallas_call(kernel, grid_spec=pltpu.PrefetchScalarGridSpec(num_scalar_...]
    dot_general x11 -> x0, matrix products: 49.2 us -> none  [the longest x1 11.9 us: solve_interfaces(): jnp.dot(lines_y.reshape(2 * count_y, NX), sine_gx, precision=highest)]
    pallas_call x1, Pallas kernels: 48.9 us -> 22.7 us  [second_solve(): pl.pallas_call(kernel, grid_spec=pltpu.PrefetchScalarGridSpec(num_scalar_...]
    all_to_all x1 -> x2, blocking collectives: 9.9 us -> 29.7 us  [the longest x1 19.8 us: shards(): lax.all_to_all(bundle, ('pa', 'pb'), split_axis=1, concat_axis=1, tiled=T...]
    pallas_call x1, Pallas kernels: 39.7 us -> 20.4 us  [first_solve(): pl.pallas_call(kernel, grid_spec=pltpu.PrefetchScalarGridSpec(num_scalar_...]
    pallas_call x1, Pallas kernels: 63 us -> 46.4 us  [advance(): pl.pallas_call(kernel, grid_spec=pltpu.PrefetchScalarGridSpec(num_scalar_...]
    pallas_call x0 -> x1, Pallas kernels: none -> 16 us  [solve_interfaces(): pl.pallas_call(kernel, grid_spec=pltpu.PrefetchScalarGridSpec(num_scalar_...]
  transfers between devices with their start and end apart: 5 -> 4, of which waited for: 2 -> 2; matrix products, arithmetic and copies ran while one was open for 1% -> 1% of each run, Pallas kernels for 0% -> 0%
where the time goes in v2:
time: 221 us
  Pallas kernels  167 us (76%)
  blocking collectives  29.7 us (13%)
  starting transfers between devices  10.5 us (5%)
  local copies, waits for them, and re-layouts  5.75 us (3%)
  other arithmetic  5.11 us (2%)
    pallas_call x1, Pallas kernels, advance(): pl.pallas_call(kernel, grid_spec=pltpu.PrefetchScalarGridSpec(num_scalar_...  46.4 us
    pallas_call x1, Pallas kernels, finish(): pl.pallas_call(kernel, grid_spec=pltpu.PrefetchScalarGridSpec(num_scalar_...  34.8 us
    pallas_call x1, Pallas kernels, gather_tile(): pl.pallas_call(kernel, grid_spec=pltpu.PrefetchScalarGridSpec(num_scalar_...  26.9 us
    pallas_call x1, Pallas kernels, second_solve(): pl.pallas_call(kernel, grid_spec=pltpu.PrefetchScalarGridSpec(num_scalar_...  22.7 us
    pallas_call x1, Pallas kernels, first_solve(): pl.pallas_call(kernel, grid_spec=pltpu.PrefetchScalarGridSpec(num_scalar_...  20.4 us
    all_to_all x1, blocking collectives, shards(): lax.all_to_all(bundle, ('pa', 'pb'), split_axis=1, concat_axis=1, tiled=T...  19.8 us
    pallas_call x1, Pallas kernels, solve_interfaces(): pl.pallas_call(kernel, grid_spec=pltpu.PrefetchScalarGridSpec(num_scalar_...  16 us
    all_to_all x1, blocking collectives, shards(): lax.all_to_all(reply, ('pa', 'pb'), split_axis=1, concat_axis=1, tiled=True)  9.91 us
  transfers between devices with their start and end apart: 4, of which 2 were waited for; matrix products, arithmetic and copies ran while one was open for 1% of the time, Pallas kernels for 0%

profile of v2, /device:TPU:0, one launch (start us, length us, event | category | flops | bytes accessed | tf_op | source)
XLA Modules:
  0.0 220.5 jit_solution(5696827892075468827)
XLA Ops:
  0.6 1.3 select_reduce_fusion.inverse_ref
  1.9 26.9 %shard_map.230 = (f32[4,256,32,256]{3,2,1,0:T(8,128)}, f32[3,32,512]{2,1,0:T(8,128)}, f32[3,32,512]{2,1,0:T(8,128)}) custom-call(s32[64]{0:T(128)} %select_reduce_fusion.inverse_ref, f32[3,64,32,1024]{3,2,1,0:T(8,128)} %refs_7_.1, f32[3,64,32,1024]{3,2,1,0:T(8,128)} %refs_7_.1, f32[3,64,32,1024]{3,2,1,0:T(8,128)} %refs_7_.1, f32[3,64,32,1024]{3,2,1,0:T(8,128)} %refs_7_.1, ...), custom_call_target="tpu_custom_call" | custom-call | tf_op jit(solution)/shard_map/pallas_call | solution.py:175
  28.8 4.9 %collective-permute-start = (f32[3,32,512]{2,1,0:T(8,128)}, f32[3,32,512]{2,1,0:T(8,128)S(1)}, u32[]{:S(2)}, u32[]{:S(2)}) collective-permute-start(f32[3,32,512]{2,1,0:T(8,128)} %get-tuple-element.14), channel_id=1, source_target_pairs={{0,1},{1,2},{2,3},{3,4},{4,5},{5,6},{6,7},{8,9},{9,10},{10,11},{11... | collective-permute-start | bytes 589832 | tf_op jit(solution)/shard_map/ppermute | solution.py:667
  33.7 1.3 collective-permute-start.1
  35.0 1.0 slice_bitcast_fusion
  36.0 1.3 collective-permute-start.3
  37.3 3.0 %collective-permute-start.2 = (f32[3,32,256]{2,1,0:T(8,128)S(1)}, f32[3,32,256]{2,1,0:T(8,128)S(1)}, u32[]{:S(2)}, u32[]{:S(2)}) collective-permute-start(f32[3,32,256]{2,1,0:T(8,128)S(1)} %get-tuple-element.25), channel_id=1, source_target_pairs={{0,8},{8,16},{16,24},{1,9},{9,17},{17,25},{2,10},{10,18},{18,26},{... | collective-permute-start | bytes 294920 | tf_op jit(solution)/shard_map/ppermute | solution.py:667
  40.3 0.6 pad_add_fusion.kinds_ref
  40.9 0.3 collective-permute-done.2.yb_ref
  41.2 0.9 collective-permute-done.1.xa_ref
  42.2 0.7 copy-done.1
  42.9 46.4 %shard_map.231 = (f32[3,256,32,256]{3,2,1,0:T(8,128)}, f32[32,256,256]{2,1,0:T(8,128)}, f32[32,256]{1,0:T(8,128)}, f32[32,256]{1,0:T(8,128)}) custom-call(s32[3]{0:T(128)} %pad_add_fusion.kinds_ref, f32[4,256,32,256]{3,2,1,0:T(8,128)} %get-tuple-element.13.main_ref.prev_ref.next_ref, f32[4,256,32,256]{3,2,1,0:T(8,128)} %get-tuple-element.13.main_ref.prev_ref.next_ref, ...), custom_call_target="tpu_custom_call" | custom-call | tf_op jit(solution)/shard_map/pallas_call | solution.py:306
  89.2 20.4 %shard_map.232 = (f32[32,256,256]{2,1,0:T(8,128)}, f32[3,32,512]{2,1,0:T(8,128)}) custom-call(s32[3]{0:T(128)} %pad_add_fusion.kinds_ref, f32[32,256,256]{2,1,0:T(8,128)} %get-tuple-element.16.modes_ref, bf16[3,256,768]{2,1,0:T(8,128)(2,1)} %constant.73.clone.y_ref, bf16[3,256,768]{2,1,0:T(8,128)(2,1)} %constant.75.clone.yt_ref, ...), custom_call_target="tpu_custom_call" | custom-call | tf_op jit(solution)/shard_map/pallas_call | solution.py:389
  109.6 1.1 copy.42
  110.7 19.8 %all_to_all.10 = f32[3,32,512]{2,0,1:T(4,128)S(1)} all-to-all(f32[3,32,512]{2,0,1:T(4,128)S(1)} %copy.42), channel_id=1, replica_groups=mesh['pa'=4,'pb'=8] {'pa','pb'}, dimensions={1} | all-to-all | bytes 393216 | tf_op jit(solution)/shard_map/all_to_all | solution.py:688
  130.5 0.1 fusion.3
  130.5 0.1 fusion.4
  130.8 0.6 pad.12.lines_x_ref
  131.5 0.6 rev.6
  132.1 0.7 pad_maximum_fusion.lines_y_ref
  132.8 16.0 %shard_map.233 = (f32[16,1024]{1,0:T(8,128)}, f32[2,16,1024]{2,1,0:T(8,128)}) custom-call(s32[3]{0:T(128)} %pad_add_fusion.kinds_ref, f32[16,1024]{1,0:T(8,128)} %pad.12.lines_x_ref, f32[2,16,1024]{2,1,0:T(8,128)} %pad_maximum_fusion.lines_y_ref, f32[2,16,2048]{2,1,0:T(8,128)} %constant.81.clone.picks_x_ref, f32[2,16,1024]{2,1,0:T(8,128)} %constant.82.clone.picks_y_ref, ...), custom_call_target="tpu_custom_call" | custom-call | tf_op jit(solution)/shard_map/pallas_call | solution.py:625
  148.8 0.8 add_bitcast_fusion.1
  149.6 0.8 slice_add_fusion
  150.3 0.8 slice_select_fusion
  151.3 0.7 rev.7
  152.0 0.1 concatenate.52
  152.1 0.1 concatenate.51
  152.2 0.1 maximum_maximum_fusion
  152.3 9.9 %all_to_all.11 = f32[2,32,512]{2,0,1:T(2,128)S(1)} all-to-all(f32[2,32,512]{2,0,1:T(2,128)S(1)} %maximum_maximum_fusion), channel_id=1, replica_groups=mesh['pa'=4,'pb'=8] {'pa','pb'}, dimensions={1} | all-to-all | bytes 262144 | tf_op jit(solution)/shard_map/all_to_all | solution.py:715
  162.2 0.7 copy.51
  162.9 22.7 %shard_map.234.modes_ref.after_ref = f32[32,256,256]{2,1,0:T(8,128)} custom-call(s32[3]{0:T(128)} %pad_add_fusion.kinds_ref, f32[32,256,256]{2,1,0:T(8,128)} %get-tuple-element.19.spectrum_ref, f32[64,512]{1,0:T(8,128)} %bitcast.41, bf16[3,256,768]{2,1,0:T(8,128)(2,1)} %constant.73.clone.y_ref, bf16[3,768,256]{2,1,0:T(8,128)(2,1)} %constant.74.clone.sine_ref.yr_ref.x_ref, ...), custom_call_target="tpu_custom_call" | custom-call | tf_op jit(solution)/shard_map/pallas_call | solution.py:446
  185.6 34.8 %shard_map.235 = (f32[3,64,32,1024]{3,2,1,0:T(8,128)}, f32[64,32,1024]{2,1,0:T(8,128)}) custom-call(s32[64]{0:T(128)} %select_reduce_fusion.inverse_ref, s32[3]{0:T(128)} %pad_add_fusion.kinds_ref, f32[32,256,256]{2,1,0:T(8,128)} %shard_map.234.modes_ref.after_ref, f32[32,256,256]{2,1,0:T(8,128)} %shard_map.234.modes_ref.after_ref, ...), custom_call_target="tpu_custom_call" | custom-call | tf_op jit(solution)/shard_map/pallas_call | solution.py:562
  (30 shorter events, 0.3 us)
Async XLA Ops:
  28.8 12.4 %collective-permute-start = (f32[3,32,512]{2,1,0:T(8,128)}, f32[3,32,512]{2,1,0:T(8,128)S(1)}, u32[]{:S(2)}, u32[]{:S(2)}) collective-permute-start(f32[3,32,512]{2,1,0:T(8,128)} %get-tuple-element.14), channel_id=1, source_target_pairs={{0,1},{1,2},{2,3},{3,4},{4,5},{5,6},{6,7},{8,9},{9,10},{10,11},{11... | collective-permute-start | bytes 589832 | tf_op jit(solution)/shard_map/ppermute | solution.py:667
  33.7 8.5 %collective-permute-start.1 = (f32[3,32,512]{2,1,0:T(8,128)}, f32[3,32,512]{2,1,0:T(8,128)S(1)}, u32[]{:S(2)}, u32[]{:S(2)}) collective-permute-start(f32[3,32,512]{2,1,0:T(8,128)} %get-tuple-element.15), channel_id=1, source_target_pairs={{1,0},{2,1},{3,2},{4,3},{5,4},{6,5},{7,6},{9,8},{10,9},{11,10},{12... | collective-permute-start | bytes 589832 | tf_op jit(solution)/shard_map/ppermute | solution.py:670
  36.0 4.9 %collective-permute-start.3 = (f32[3,32,256]{2,1,0:T(8,128)S(1)}, f32[3,32,256]{2,1,0:T(8,128)S(1)}, u32[]{:S(2)}, u32[]{:S(2)}) collective-permute-start(f32[3,32,256]{2,1,0:T(8,128)S(1)} %get-tuple-element.24), channel_id=1, source_target_pairs={{8,0},{16,8},{24,16},{9,1},{17,9},{25,17},{10,2},{18,10},{26,18},{... | collective-permute-start | bytes 294920 | tf_op jit(solution)/shard_map/ppermute | solution.py:670
  37.3 4.0 %collective-permute-start.2 = (f32[3,32,256]{2,1,0:T(8,128)S(1)}, f32[3,32,256]{2,1,0:T(8,128)S(1)}, u32[]{:S(2)}, u32[]{:S(2)}) collective-permute-start(f32[3,32,256]{2,1,0:T(8,128)S(1)} %get-tuple-element.25), channel_id=1, source_target_pairs={{0,8},{8,16},{16,24},{1,9},{9,17},{17,25},{2,10},{10,18},{18,26},{... | collective-permute-start | bytes 294920 | tf_op jit(solution)/shard_map/ppermute | solution.py:667
  40.9 1.3 copy-start.2
  41.2 0.9 copy-start.3
  41.2 0.9 copy-start
  42.2 0.7 copy-start.1
  130.5 19.9 %copy-start.4 = (pred[8]{0:T(512)(128)(4,1)S(1)}, pred[8]{0:T(512)(128)(4,1)}, u32[]{:S(2)}) copy-start(pred[8]{0:T(512)(128)(4,1)} %constant.71.clone.1) | copy-start | bytes 28

commit v3 on v2

--- a/solution.py
+++ b/solution.py
@@ -84,11 +84,21 @@
     return mm(jnp.concatenate([high, high, low], axis=1), table_ref[...])
 
 
+def mm_transposed(left, right):
+    return lax.dot_general(left, right, (((1,), (1,)), ((), ())), preferred_element_type=f32)
+
+
 def few_rows_times(values, high, low, product=mm):
     rows = values.shape[0]
     both = jnp.concatenate(pieces(values), axis=0)
     first = product(both, high)
     return first[:rows] + (first[rows:] + product(both[:rows], low))
+
+
+def inverse_of(values):
+    found = pl.reciprocal(values, approx=True)
+    found = found * (2.0 - values * found)
+    return found * (2.0 - values * found)
 
 
 def dot_full(left, right, dims):
@@ -189,13 +199,13 @@
     )(inverse, *([velocity] * cols_n), *([fluid] * cols_n))
 
 
-def advance(tile, x_below, x_above, y_below, y_above, cosine, sine_x, kinds):
+def advance(tile, x_below, x_above, y_below, y_above, cosine, sine_x, shift, kinds):
     _, y_span, _, x_span = tile.shape
     steps = y_span // B
     chunks = x_span // LANES
 
-    def kernel(kinds_ref, main_ref, prev_ref, next_ref, xb_ref, xa_ref, yb_ref, ya_ref, cosine_ref, sine_ref,
-               star_ref, modes_ref, gx_ref, gy_ref, rows_ref, source_ref, carry_ref):
+    def kernel(kinds_ref, main_ref, prev_ref, next_ref, xb_ref, xa_ref, yb_ref, ya_ref, cosine_ref, sine_ref, shift_ref,
+               star_ref, modes_ref, gx_ref, gy_ref, rows_ref, source_ref, carry_ref, even_ref, odd_ref):
         step = pl.program_id(0)
         lanes = lane_ids()
         layers = lax.broadcasted_iota(jnp.int32, (NZ, LANES), 0)
@@ -225,7 +235,7 @@
         halo_chunk = pl.ds(pl.multiple_of(step // 2 * LANES, LANES), LANES)
         even_lane = (lanes & 1) == 0
 
-        def row(group, r):
+        def row(group, r, moved_ref):
             j = group * 8 + r
             held = r % 4 * 32 + (step % 2) * 16 + 2 * (group * 2 + r // 4)
             at = (step % 4) * B + j
@@ -234,13 +244,10 @@
             for h in range(chunks):
                 for c in range(3):
                     flow[c, h] = rows_ref[c, j + 1, :, h * LANES : (h + 1) * LANES]
-            edge, to_right, to_left = {}, {}, {}
+            edge = {}
             for c in range(3):
                 both = jnp.where(even_lane, xb_ref[c, :, halo_chunk], xa_ref[c, :, halo_chunk])
                 edge[c] = pltpu.roll(both, (LANES - held) % LANES, 1)
-                for h in range(chunks):
-                    to_right[c, h] = pltpu.roll(flow[c, h], 1, 1)
-                    to_left[c, h] = pltpu.roll(flow[c, h], LANES - 1, 1)
             for h in range(chunks):
                 part = slice(h * LANES, (h + 1) * LANES)
                 take_up, take_down = [], []
@@ -251,10 +258,12 @@
                 fraction = main_ref[3, j, :, part]
                 for c in range(3):
                     center = flow[c, h]
-                    before = edge[c] if h == 0 else to_right[c, h - 1]
-                    after = edge[c] if h == chunks - 1 else to_left[c, h + 1]
-                    x_low = jnp.where(first_lane, before, to_right[c, h])
-                    x_up = jnp.where(last_lane, after, to_left[c, h])
+                    x_low = moved_ref[c, r, :, part]
+                    x_up = moved_ref[c, r, :, x_span + h * LANES : x_span + (h + 1) * LANES]
+                    if h == 0:
+                        x_low = jnp.where(first_lane, edge[c], x_low)
+                    if h == chunks - 1:
+                        x_up = jnp.where(last_lane, edge[c], x_up)
                     y_low = rows_ref[c, j, :, part]
                     y_up = rows_ref[c, j + 2, :, part]
                     z_low = jnp.where(first_layer, 0.0, pltpu.roll(center, 1, 0))
@@ -289,16 +298,27 @@
             modes = times_table(table_times(cosine_ref, part), sine_ref)
             modes_ref[:, rows, :] = modes.reshape(NZ, 8, x_span)
 
-        for r in range(8):
-            row(0, r)
-
-        def group_of_rows(group, _):
-            transform(group - 1)
+        def shift(group, moved_ref):
+            for c in range(3):
+                center = rows_ref[c, pl.ds(group * 8 + 1, 8)].reshape(8 * NZ, x_span)
+                moved = mm(jnp.concatenate(pieces(center), axis=1), shift_ref[...])
+                moved_ref[c] = moved.reshape(8, NZ, 2 * x_span)
+
+        shift(0, even_ref)
+
+        def two_groups(pair, _):
+            group = 2 * pair
+            transform(jnp.maximum(group - 1, 0))
+            shift(group + 1, odd_ref)
             for r in range(8):
-                row(group, r)
+                row(group, r, even_ref)
+            transform(group)
+            shift(jnp.minimum(group + 2, B // 8 - 1), even_ref)
+            for r in range(8):
+                row(group + 1, r, odd_ref)
             return _
 
-        lax.fori_loop(1, B // 8, group_of_rows, 0)
+        lax.fori_loop(0, B // 16, two_groups, 0)
         transform(B // 8 - 1)
         gy_ref[...] = carry_ref[...]
 
@@ -318,6 +338,7 @@
                 pl.BlockSpec((3, NZ, x_span), lambda s, kinds: (0, 0, 0)),
                 pl.BlockSpec((8 * NZ, 24 * NZ), lambda s, kinds: (0, 0)),
                 pl.BlockSpec((None, 3 * x_span, x_span), lambda s, kinds: (kinds[1], 0, 0)),
+                pl.BlockSpec((2 * x_span, 2 * x_span), lambda s, kinds: (0, 0)),
             ],
             out_specs=[
                 pl.BlockSpec((3, B, NZ, x_span), lambda s, kinds: (0, s, 0, 0)),
@@ -329,6 +350,8 @@
                 pltpu.VMEM((3, B + 2, NZ, x_span), f32),
                 pltpu.VMEM((B, NZ, x_span), f32),
                 pltpu.VMEM((NZ, x_span), f32),
+                pltpu.VMEM((3, 8, NZ, 2 * x_span), f32),
+                pltpu.VMEM((3, 8, NZ, 2 * x_span), f32),
             ],
         ),
         out_shape=[
@@ -338,47 +361,36 @@
             jax.ShapeDtypeStruct((NZ, x_span), f32),
         ],
         compiler_params=params(),
-    )(kinds, tile, tile, tile, x_below, x_above, y_below, y_above, cosine, sine_x)
-
-
-def first_solve(modes, sine_y, sine_yt, sine_xt, edge_y, edge_xt, eigen, levels, flux_x, flux_y, cosine, kinds):
+    )(kinds, tile, tile, tile, x_below, x_above, y_below, y_above, cosine, sine_x, shift)
+
+
+def first_solve(modes, sine_yt, sine_ytr, sine_xt, edge_y, edge_x, eigen, levels, flux_x, flux_y, cosine, kinds):
     layers, y_span, x_span = modes.shape
     batch = 4
     steps = layers // batch
     sides = 2 * layers
 
-    def kernel(kinds_ref, modes_ref, y_ref, yt_ref, xt_ref, edge_y_ref, edge_xt_ref, eigen_ref, levels_ref,
+    def kernel(kinds_ref, modes_ref, yt_ref, ytr_ref, xt_ref, edge_y_ref, edge_x_ref, eigen_ref, levels_ref,
                flux_x_ref, flux_y_ref, cosine_ref, spectrum_ref, bundle_ref, rows_ref, columns_ref):
         step = pl.program_id(0)
-        row_ids = lax.broadcasted_iota(jnp.int32, (sides, y_span), 0)
-        column_ids = lax.broadcasted_iota(jnp.int32, (x_span, LANES), 1)
-
-        @pl.when(step == 0)
-        def _():
-            rows_ref[...] = jnp.zeros_like(rows_ref)
-            columns_ref[...] = jnp.zeros_like(columns_ref)
-
-        row_sum, column_sum = [], []
         for i in range(batch):
             k = step * batch + i
             spectrum = table_times(yt_ref, modes_ref[i])
             spectrum_ref[i] = spectrum
-            high, low = pieces(spectrum / (eigen_ref[...] + levels_ref[k]))
-            edge_high, edge_low = pieces(jnp.where(row_ids % layers == k, edge_y_ref[...], 0.0))
-            edges = jnp.concatenate([edge_high, edge_low], axis=0)
-            found = mm(edges, high)
-            row_sum.append(found[:sides] + (found[sides:] + mm(edge_high, low)))
-            edge_high, edge_low = pieces(jnp.where(column_ids % layers == k, edge_xt_ref[...], 0.0))
-            column_sum.append(mm(
-                jnp.concatenate([high, high, low], axis=1),
-                jnp.concatenate([edge_high, edge_low, edge_high], axis=0)))
-        rows_ref[...] += (row_sum[0] + row_sum[1]) + (row_sum[2] + row_sum[3])
-        columns_ref[...] += (column_sum[0] + column_sum[1]) + (column_sum[2] + column_sum[3])
+            high, low = pieces(spectrum * inverse_of(eigen_ref[...] + levels_ref[k]))
+            found = mm(edge_y_ref[...], high) + mm(edge_y_ref[...], low)
+            found = found[:8] + found[8:]
+            rows_ref[pl.ds(k, 1)] = found[0:1]
+            rows_ref[pl.ds(layers + k, 1)] = found[1:2]
+            found = mm_transposed(edge_x_ref[...], high) + mm_transposed(edge_x_ref[...], low)
+            found = found[:8] + found[8:]
+            columns_ref[pl.ds(k, 1)] = found[0:1]
+            columns_ref[pl.ds(layers + k, 1)] = found[1:2]
 
         @pl.when(step == steps - 1)
         def _():
             along_x = times_table(rows_ref[...], xt_ref)
-            along_y = table_times(y_ref, columns_ref[...]).T[:sides]
+            along_y = times_table(columns_ref[...], ytr_ref)
             cosine_table = cosine_ref[...]
             for line, values, flux_ref in ((0, along_x, flux_y_ref), (x_span, along_y, flux_x_ref)):
                 part = slice(line, line + values.shape[1])
@@ -394,10 +406,10 @@
             in_specs=[
                 pl.BlockSpec((batch, y_span, x_span), lambda k, kinds: (k, 0, 0)),
                 pl.BlockSpec((None, y_span, 3 * y_span), lambda k, kinds: (kinds[0], 0, 0)),
-                pl.BlockSpec((None, y_span, 3 * y_span), lambda k, kinds: (kinds[0], 0, 0)),
+                pl.BlockSpec((None, 3 * y_span, y_span), lambda k, kinds: (kinds[0], 0, 0)),
                 pl.BlockSpec((None, 3 * x_span, x_span), lambda k, kinds: (kinds[1], 0, 0)),
-                pl.BlockSpec((None, sides, y_span), lambda k, kinds: (kinds[0], 0, 0)),
-                pl.BlockSpec((None, x_span, LANES), lambda k, kinds: (kinds[1], 0, 0)),
+                pl.BlockSpec((None, 16, y_span), lambda k, kinds: (kinds[0], 0, 0)),
+                pl.BlockSpec((None, 16, x_span), lambda k, kinds: (kinds[1], 0, 0)),
                 pl.BlockSpec((None, y_span, x_span), lambda k, kinds: (kinds[0] * 3 + kinds[1], 0, 0)),
                 pl.BlockSpec(memory_space=pltpu.SMEM),
                 pl.BlockSpec((layers, y_span), lambda k, kinds: (0, 0)),
@@ -408,14 +420,14 @@
                 pl.BlockSpec((batch, y_span, x_span), lambda k, kinds: (k, 0, 0)),
                 pl.BlockSpec((3, layers, x_span + y_span), lambda k, kinds: (0, 0, 0)),
             ],
-            scratch_shapes=[pltpu.VMEM((sides, x_span), f32), pltpu.VMEM((y_span, LANES), f32)],
+            scratch_shapes=[pltpu.VMEM((sides, x_span), f32), pltpu.VMEM((sides, y_span), f32)],
         ),
         out_shape=[
             jax.ShapeDtypeStruct((layers, y_span, x_span), f32),
             jax.ShapeDtypeStruct((3, layers, x_span + y_span), f32),
         ],
         compiler_params=params(),
-    )(kinds, modes, sine_y, sine_yt, sine_xt, edge_y, edge_xt, eigen, levels, flux_x, flux_y, cosine)
+    )(kinds, modes, sine_yt, sine_ytr, sine_xt, edge_y, edge_x, eigen, levels, flux_x, flux_y, cosine)
 
 
 def second_solve(spectrum, sums, sine_y, sine_yr, sine_x, sine_xt, edge_y, edge_x, eigen, levels, kinds):
@@ -435,12 +447,12 @@
             left_high, left_low = pieces(left.T)
             left_ref[...] = jnp.concatenate([left_high, left_high, left_low], axis=1)
 
-        row_ids = lax.broadcasted_iota(jnp.int32, (2 * sides, x_span), 0) % layers
+        row_ids = lax.broadcasted_iota(jnp.int32, (2 * sides, x_span), 0) & (layers - 1)
         for i in range(batch):
             k = step * batch + i
             high, low = pieces(jnp.where(row_ids == k, right_ref[...], 0.0))
             added = mm(left_ref[...], jnp.concatenate([high, low, high], axis=0))
-            solved = (spectrum_ref[i] + added) / (eigen_ref[...] + levels_ref[k])
+            solved = (spectrum_ref[i] + added) * inverse_of(eigen_ref[...] + levels_ref[k])
             out_ref[i] = times_table(table_times(y_ref, solved), xt_ref)
 
     return pl.pallas_call(
@@ -602,24 +614,20 @@
             hat_ref[:, parity * half_x : (parity + 1) * half_x] = few_rows_times(
                 lines_y_ref[parity], table_x_ref[parity, 0], table_x_ref[parity, 1])
         right = spread(jnp.concatenate([hat_x, picks_y_ref[0]], axis=0))
-
-        def transposed(a, b):
-            return lax.dot_general(a, b, (((1,), (1,)), ((), ())), preferred_element_type=f32)
-
         along = jnp.zeros((rows_x, NY), f32)
         for start in range(0, 2 * half_x, width):
             part = slice(start, start + width)
             left = spread_other(jnp.concatenate([picks_x_ref[0, :, part], hat_ref[:, part]], axis=0))
             field = lax.dot_general(left, right, (((0,), (0,)), ((), ())), preferred_element_type=f32)
-            field = field / (eig_x_ref[part, :1] + eig_y_ref[:1] + level)
+            field = field * inverse_of(eig_x_ref[part, :1] + eig_y_ref[:1] + level)
             high, low = pieces(field)
             along += few_rows_times(picks_x_ref[1, :, part], high, low)
-            out_hat_ref[:, part] = hat_ref[:, part] + few_rows_times(picks_y_ref[1], high, low, transposed)
+            out_hat_ref[:, part] = hat_ref[:, part] + few_rows_times(picks_y_ref[1], high, low, mm_transposed)
         sum_x_ref[...] = few_rows_times(hat_x + along, table_y_ref[0], table_y_ref[1])
         for parity in range(2):
             fold_ref[parity] = few_rows_times(
                 out_hat_ref[:, parity * half_x : (parity + 1) * half_x],
-                table_x_ref[parity, 0], table_x_ref[parity, 1], transposed)
+                table_x_ref[parity, 0], table_x_ref[parity, 1], mm_transposed)
 
     vmem = pl.BlockSpec(memory_space=pltpu.VMEM)
     return pl.pallas_call(
@@ -674,13 +682,14 @@
 
     cosine = jnp.asarray(tables["cosine"])
     local = {name: jnp.asarray(tables[name]) for name in (
-        "y", "yr", "yt", "x", "xt", "edge_y", "edge_x", "edge_xt", "eigen", "levels", "picks_x", "picks_y", "fold_x", "line_y",
+        "y", "yr", "yt", "ytr", "x", "xt", "edge_y", "edge_x", "few_y", "few_x", "eigen", "levels", "picks_x", "picks_y", "fold_x", "line_y",
         "eig_x", "eig_y")}
     star, modes, flux_x, flux_y = advance(
-        tile, x_below, x_above, y_below, y_above, jnp.asarray(tables["cosine8"]), local["x"], kinds
+        tile, x_below, x_above, y_below, y_above, jnp.asarray(tables["cosine8"]), local["x"],
+        jnp.asarray(tables["shift"]), kinds
     )
     spectrum, bundle = first_solve(
-        modes, local["y"], local["yt"], local["xt"], local["edge_y"], local["edge_xt"], local["eigen"],
+        modes, local["yt"], local["ytr"], local["xt"], local["few_y"], local["few_x"], local["eigen"],
         local["levels"], flux_x, flux_y, cosine, kinds
     )
     width = x_span + y_span
@@ -735,6 +744,9 @@
         "cosine8": left_table(cosine8),
         "cosine8t": left_table(cosine8.T),
     }
+    below = np.eye(x_span, k=1)
+    shift = np.concatenate([below, below.T], axis=1)
+    tables["shift"] = np.concatenate([shift, shift], axis=0).astype(ml_dtypes.bfloat16)
     values = {}
     for name, length in (("y", y_span), ("x", x_span)):
         bases = tile_bases(length)
@@ -745,10 +757,13 @@
             tables["y"] = np.stack([left_table(b) for b, _ in bases])
             tables["yr"] = np.stack([right_table(b) for b, _ in bases])
             tables["yt"] = np.stack([left_table(b.T) for b, _ in bases])
+            tables["ytr"] = np.stack([right_table(b.T) for b, _ in bases])
         edges = np.stack([np.repeat(b[[0, -1]], NZ, axis=0) for b, _ in bases])
         tables["edge_" + name] = single(edges)
-        blank = np.zeros((3, length, LANES - 2 * NZ))
-        tables["edge_" + name + "t"] = single(np.concatenate([edges.transpose(0, 2, 1), blank], axis=2))
+        few = np.zeros((3, 16, length), ml_dtypes.bfloat16)
+        for i, (b, _) in enumerate(bases):
+            few[i, 0:2], few[i, 8:10] = parts_of(b[[0, -1]])
+        tables["few_" + name] = few
         values[name] = [v for _, v in bases]
     tables["eigen"] = single(
         np.stack([ey[:, None] + ex[None, :] for ey in values["y"] for ex in values["x"]])

time: 221 us -> 230 us (1.041)
  Pallas kernels: 167 us -> 176 us
    pallas_call x1, Pallas kernels: 46.4 us -> 59.4 us  [advance(): pl.pallas_call(kernel, grid_spec=pltpu.PrefetchScalarGridSpec(num_scalar_...]
    pallas_call x1, Pallas kernels: 20.4 us -> 15.5 us  [first_solve(): pl.pallas_call(kernel, grid_spec=pltpu.PrefetchScalarGridSpec(num_scalar_...]
where the time goes in v3:
time: 230 us; the launch traced here: 229 us
  Pallas kernels  176 us (77%)
  blocking collectives  29.6 us (13%)
  starting transfers between devices  10.5 us (5%)
  local copies, waits for them, and re-layouts  5.75 us (2%)
  other arithmetic  5.11 us (2%)
    pallas_call x1, Pallas kernels, advance(): pl.pallas_call(kernel, grid_spec=pltpu.PrefetchScalarGridSpec(num_scalar_...  59.4 us
    pallas_call x1, Pallas kernels, finish(): pl.pallas_call(kernel, grid_spec=pltpu.PrefetchScalarGridSpec(num_scalar_...  34.8 us
    pallas_call x1, Pallas kernels, gather_tile(): pl.pallas_call(kernel, grid_spec=pltpu.PrefetchScalarGridSpec(num_scalar_...  26.9 us
    pallas_call x1, Pallas kernels, second_solve(): pl.pallas_call(kernel, grid_spec=pltpu.PrefetchScalarGridSpec(num_scalar_...  22.7 us
    all_to_all x1, blocking collectives, shards(): lax.all_to_all(bundle, ('pa', 'pb'), split_axis=1, concat_axis=1, tiled=T...  19.7 us
    pallas_call x1, Pallas kernels, solve_interfaces(): pl.pallas_call(kernel, grid_spec=pltpu.PrefetchScalarGridSpec(num_scalar_...  16.2 us
    pallas_call x1, Pallas kernels, first_solve(): pl.pallas_call(kernel, grid_spec=pltpu.PrefetchScalarGridSpec(num_scalar_...  15.5 us
    all_to_all x1, blocking collectives, shards(): lax.all_to_all(reply, ('pa', 'pb'), split_axis=1, concat_axis=1, tiled=True)  9.9 us
  transfers between devices with their start and end apart: 4, of which 2 were waited for; matrix products, arithmetic and copies ran while one was open for 1% of the time, Pallas kernels for 0%

profile of v3, /device:TPU:0, one launch (start us, length us, event | category | flops | bytes accessed | tf_op | source)
XLA Modules:
  0.0 228.9 jit_solution(556825176029076643)
XLA Ops:
  0.6 1.3 select_reduce_fusion.inverse_ref
  1.9 26.9 %shard_map.257 = (f32[4,256,32,256]{3,2,1,0:T(8,128)}, f32[3,32,512]{2,1,0:T(8,128)}, f32[3,32,512]{2,1,0:T(8,128)}) custom-call(s32[64]{0:T(128)} %select_reduce_fusion.inverse_ref, f32[3,64,32,1024]{3,2,1,0:T(8,128)} %refs_7_.1, f32[3,64,32,1024]{3,2,1,0:T(8,128)} %refs_7_.1, f32[3,64,32,1024]{3,2,1,0:T(8,128)} %refs_7_.1, f32[3,64,32,1024]{3,2,1,0:T(8,128)} %refs_7_.1, ...), custom_call_target="tpu_custom_call" | custom-call | tf_op jit(solution)/shard_map/pallas_call | solution.py:185
  28.8 4.9 %collective-permute-start = (f32[3,32,512]{2,1,0:T(8,128)}, f32[3,32,512]{2,1,0:T(8,128)S(1)}, u32[]{:S(2)}, u32[]{:S(2)}) collective-permute-start(f32[3,32,512]{2,1,0:T(8,128)} %get-tuple-element.14), channel_id=1, source_target_pairs={{0,1},{1,2},{2,3},{3,4},{4,5},{5,6},{6,7},{8,9},{9,10},{10,11},{11... | collective-permute-start | bytes 589832 | tf_op jit(solution)/shard_map/ppermute | solution.py:675
  33.7 1.3 collective-permute-start.1
  35.0 1.0 slice_bitcast_fusion
  36.0 1.3 collective-permute-start.3
  37.3 3.0 %collective-permute-start.2 = (f32[3,32,256]{2,1,0:T(8,128)S(1)}, f32[3,32,256]{2,1,0:T(8,128)S(1)}, u32[]{:S(2)}, u32[]{:S(2)}) collective-permute-start(f32[3,32,256]{2,1,0:T(8,128)S(1)} %get-tuple-element.25), channel_id=1, source_target_pairs={{0,8},{8,16},{16,24},{1,9},{9,17},{17,25},{2,10},{10,18},{18,26},{... | collective-permute-start | bytes 294920 | tf_op jit(solution)/shard_map/ppermute | solution.py:675
  40.3 0.6 pad_add_fusion.kinds_ref
  40.9 0.3 collective-permute-done.2.yb_ref
  41.2 0.9 collective-permute-done.1.xa_ref
  42.2 0.7 copy-done.1
  42.9 59.4 %shard_map.258 = (f32[3,256,32,256]{3,2,1,0:T(8,128)}, f32[32,256,256]{2,1,0:T(8,128)}, f32[32,256]{1,0:T(8,128)}, f32[32,256]{1,0:T(8,128)}) custom-call(s32[3]{0:T(128)} %pad_add_fusion.kinds_ref, f32[4,256,32,256]{3,2,1,0:T(8,128)} %get-tuple-element.13.main_ref.prev_ref.next_ref, f32[4,256,32,256]{3,2,1,0:T(8,128)} %get-tuple-element.13.main_ref.prev_ref.next_ref, ...), custom_call_target="tpu_custom_call" | custom-call | tf_op jit(solution)/shard_map/pallas_call | solution.py:326
  102.3 15.5 %shard_map.259 = (f32[32,256,256]{2,1,0:T(8,128)}, f32[3,32,512]{2,1,0:T(8,128)}) custom-call(s32[3]{0:T(128)} %pad_add_fusion.kinds_ref, f32[32,256,256]{2,1,0:T(8,128)} %get-tuple-element.16.modes_ref, bf16[3,256,768]{2,1,0:T(8,128)(2,1)} %constant.77.clone.yt_ref, bf16[3,768,256]{2,1,0:T(8,128)(2,1)} %constant.78.clone.ytr_ref.xt_ref, ...), custom_call_target="tpu_custom_call" | custom-call | tf_op jit(solution)/shard_map/pallas_call | solution.py:401
  117.8 1.1 copy.45
  118.8 19.7 %all_to_all.10 = f32[3,32,512]{2,0,1:T(4,128)S(1)} all-to-all(f32[3,32,512]{2,0,1:T(4,128)S(1)} %copy.45), channel_id=1, replica_groups=mesh['pa'=4,'pb'=8] {'pa','pb'}, dimensions={1} | all-to-all | bytes 393216 | tf_op jit(solution)/shard_map/all_to_all | solution.py:697
  138.6 0.1 fusion.3
  138.6 0.1 fusion.4
  138.9 0.6 pad.12.lines_x_ref
  139.6 0.6 rev.6
  140.2 0.7 pad_maximum_fusion.lines_y_ref
  140.9 16.2 %shard_map.260 = (f32[16,1024]{1,0:T(8,128)}, f32[2,16,1024]{2,1,0:T(8,128)}) custom-call(s32[3]{0:T(128)} %pad_add_fusion.kinds_ref, f32[16,1024]{1,0:T(8,128)} %pad.12.lines_x_ref, f32[2,16,1024]{2,1,0:T(8,128)} %pad_maximum_fusion.lines_y_ref, f32[2,16,2048]{2,1,0:T(8,128)} %constant.83.clone.picks_x_ref, f32[2,16,1024]{2,1,0:T(8,128)} %constant.84.clone.picks_y_ref, ...), custom_call_target="tpu_custom_call" | custom-call | tf_op jit(solution)/shard_map/pallas_call | solution.py:633
  157.1 0.8 add_bitcast_fusion.1
  157.8 0.8 slice_add_fusion
  158.6 0.8 slice_select_fusion
  159.5 0.7 rev.7
  160.3 0.1 concatenate.52
  160.4 0.1 concatenate.51
  160.4 0.1 maximum_maximum_fusion
  160.6 9.9 %all_to_all.11 = f32[2,32,512]{2,0,1:T(2,128)S(1)} all-to-all(f32[2,32,512]{2,0,1:T(2,128)S(1)} %maximum_maximum_fusion), channel_id=1, replica_groups=mesh['pa'=4,'pb'=8] {'pa','pb'}, dimensions={1} | all-to-all | bytes 262144 | tf_op jit(solution)/shard_map/all_to_all | solution.py:724
  170.5 0.7 copy.54
  171.1 22.7 %shard_map.261.modes_ref.after_ref = f32[32,256,256]{2,1,0:T(8,128)} custom-call(s32[3]{0:T(128)} %pad_add_fusion.kinds_ref, f32[32,256,256]{2,1,0:T(8,128)} %get-tuple-element.19.spectrum_ref, f32[64,512]{1,0:T(8,128)} %bitcast.41, bf16[3,256,768]{2,1,0:T(8,128)(2,1)} %constant.75.clone.y_ref, bf16[3,768,256]{2,1,0:T(8,128)(2,1)} %constant.76.clone.sine_ref.yr_ref.x_ref, ...), custom_call_target="tpu_custom_call" | custom-call | tf_op jit(solution)/shard_map/pallas_call | solution.py:458
  193.9 34.8 %shard_map.262 = (f32[3,64,32,1024]{3,2,1,0:T(8,128)}, f32[64,32,1024]{2,1,0:T(8,128)}) custom-call(s32[64]{0:T(128)} %select_reduce_fusion.inverse_ref, s32[3]{0:T(128)} %pad_add_fusion.kinds_ref, f32[32,256,256]{2,1,0:T(8,128)} %shard_map.261.modes_ref.after_ref, f32[32,256,256]{2,1,0:T(8,128)} %shard_map.261.modes_ref.after_ref, ...), custom_call_target="tpu_custom_call" | custom-call | tf_op jit(solution)/shard_map/pallas_call | solution.py:574
  (30 shorter events, 0.3 us)
Async XLA Ops:
  28.8 12.4 %collective-permute-start = (f32[3,32,512]{2,1,0:T(8,128)}, f32[3,32,512]{2,1,0:T(8,128)S(1)}, u32[]{:S(2)}, u32[]{:S(2)}) collective-permute-start(f32[3,32,512]{2,1,0:T(8,128)} %get-tuple-element.14), channel_id=1, source_target_pairs={{0,1},{1,2},{2,3},{3,4},{4,5},{5,6},{6,7},{8,9},{9,10},{10,11},{11... | collective-permute-start | bytes 589832 | tf_op jit(solution)/shard_map/ppermute | solution.py:675
  33.7 8.5 %collective-permute-start.1 = (f32[3,32,512]{2,1,0:T(8,128)}, f32[3,32,512]{2,1,0:T(8,128)S(1)}, u32[]{:S(2)}, u32[]{:S(2)}) collective-permute-start(f32[3,32,512]{2,1,0:T(8,128)} %get-tuple-element.15), channel_id=1, source_target_pairs={{1,0},{2,1},{3,2},{4,3},{5,4},{6,5},{7,6},{9,8},{10,9},{11,10},{12... | collective-permute-start | bytes 589832 | tf_op jit(solution)/shard_map/ppermute | solution.py:678
  36.0 4.9 %collective-permute-start.3 = (f32[3,32,256]{2,1,0:T(8,128)S(1)}, f32[3,32,256]{2,1,0:T(8,128)S(1)}, u32[]{:S(2)}, u32[]{:S(2)}) collective-permute-start(f32[3,32,256]{2,1,0:T(8,128)S(1)} %get-tuple-element.24), channel_id=1, source_target_pairs={{8,0},{16,8},{24,16},{9,1},{17,9},{25,17},{10,2},{18,10},{26,18},{... | collective-permute-start | bytes 294920 | tf_op jit(solution)/shard_map/ppermute | solution.py:678
  37.3 4.0 %collective-permute-start.2 = (f32[3,32,256]{2,1,0:T(8,128)S(1)}, f32[3,32,256]{2,1,0:T(8,128)S(1)}, u32[]{:S(2)}, u32[]{:S(2)}) collective-permute-start(f32[3,32,256]{2,1,0:T(8,128)S(1)} %get-tuple-element.25), channel_id=1, source_target_pairs={{0,8},{8,16},{16,24},{1,9},{9,17},{17,25},{2,10},{10,18},{18,26},{... | collective-permute-start | bytes 294920 | tf_op jit(solution)/shard_map/ppermute | solution.py:675
  40.9 1.3 copy-start.2
  41.2 0.9 copy-start.3
  41.2 0.9 copy-start
  42.2 0.7 copy-start.1
  138.6 20.0 %copy-start.4 = (pred[8]{0:T(512)(128)(4,1)S(1)}, pred[8]{0:T(512)(128)(4,1)}, u32[]{:S(2)}) copy-start(pred[8]{0:T(512)(128)(4,1)} %constant.73.clone.1) | copy-start | bytes 28

commit v4 on v3

--- a/solution.py
+++ b/solution.py
@@ -52,8 +52,7 @@
 
 
 def left_table(table):
-    high, low = parts_of(table)
-    return np.concatenate([high, high, low], axis=-1)
+    return np.concatenate(parts_of(table), axis=-2)
 
 
 def right_table(table):
@@ -76,7 +75,9 @@
 
 def table_times(table_ref, values):
     high, low = pieces(values)
-    return mm(table_ref[...], jnp.concatenate([high, low, high], axis=0))
+    rows = table_ref.shape[0] // 2
+    found = mm(table_ref[...], high)
+    return found[:rows] + (found[rows:] + mm(table_ref[:rows], low))
 
 
 def times_table(values, table_ref):
@@ -199,21 +200,19 @@
     )(inverse, *([velocity] * cols_n), *([fluid] * cols_n))
 
 
-def advance(tile, x_below, x_above, y_below, y_above, cosine, sine_x, shift, kinds):
+def advance(tile, x_below, x_above, y_below, y_above, cosine, sine_x, kinds):
     _, y_span, _, x_span = tile.shape
     steps = y_span // B
     chunks = x_span // LANES
 
-    def kernel(kinds_ref, main_ref, prev_ref, next_ref, xb_ref, xa_ref, yb_ref, ya_ref, cosine_ref, sine_ref, shift_ref,
-               star_ref, modes_ref, gx_ref, gy_ref, rows_ref, source_ref, carry_ref, even_ref, odd_ref):
+    def kernel(kinds_ref, main_ref, prev_ref, next_ref, xb_ref, xa_ref, yb_ref, ya_ref, cosine_ref, sine_ref,
+               star_ref, modes_ref, gx_ref, gy_ref, rows_ref, source_ref, carry_ref):
         step = pl.program_id(0)
         lanes = lane_ids()
         layers = lax.broadcasted_iota(jnp.int32, (NZ, LANES), 0)
         first_layer, last_layer = layers == 0, layers == NZ - 1
         first_lane, last_lane = lanes == 0, lanes == LANES - 1
 
-        rows_ref[:, 1 : B + 1] = main_ref[:3]
-
         @pl.when(step == 0)
         def _():
             rows_ref[:, 0] = yb_ref[...]
@@ -225,100 +224,96 @@
 
         @pl.when(step == steps - 1)
         def _():
-            rows_ref[:, B + 1] = ya_ref[...]
+            rows_ref[:, 1] = ya_ref[...]
 
         @pl.when(step < steps - 1)
         def _():
-            rows_ref[:, B + 1] = next_ref[:3, 0]
+            rows_ref[:, 1] = next_ref[:3, 0]
 
         y_chunk = pl.ds(pl.multiple_of(step // 4 * LANES, LANES), LANES)
         halo_chunk = pl.ds(pl.multiple_of(step // 2 * LANES, LANES), LANES)
         even_lane = (lanes & 1) == 0
 
-        def row(group, r, moved_ref):
-            j = group * 8 + r
-            held = r % 4 * 32 + (step % 2) * 16 + 2 * (group * 2 + r // 4)
-            at = (step % 4) * B + j
-            star = {}
-            flow = {}
-            for h in range(chunks):
+        def neighbour_row(group, r, c, part):
+            if 0 <= r < 8:
+                return main_ref[c, group * 8 + r, :, part]
+            if r < 0:
+                inside = main_ref[c, jnp.maximum(group * 8 - 1, 0), :, part]
+                return jnp.where(group == 0, rows_ref[c, 0, :, part], inside)
+            inside = main_ref[c, jnp.minimum(group * 8 + 8, B - 1), :, part]
+            return jnp.where(group == B // 8 - 1, rows_ref[c, 1, :, part], inside)
+
+        lane_parts = [slice(h * LANES, (h + 1) * LANES) for h in range(chunks)]
+
+        def rows(group):
+            carried = [carry_ref[:, part] for part in lane_parts]
+            gathered = gx_ref[:, y_chunk]
+            for r in range(8):
+                j = group * 8 + r
+                held = r % 4 * 32 + (step % 2) * 16 + 2 * (group * 2 + r // 4)
+                at = (step % 4) * B + j
+                speed = [[0.125 * main_ref[e, j, :, part] for part in lane_parts] for e in range(3)]
+                source = []
                 for c in range(3):
-                    flow[c, h] = rows_ref[c, j + 1, :, h * LANES : (h + 1) * LANES]
-            edge = {}
-            for c in range(3):
-                both = jnp.where(even_lane, xb_ref[c, :, halo_chunk], xa_ref[c, :, halo_chunk])
-                edge[c] = pltpu.roll(both, (LANES - held) % LANES, 1)
-            for h in range(chunks):
-                part = slice(h * LANES, (h + 1) * LANES)
-                take_up, take_down = [], []
-                for e in range(3):
-                    scaled = 0.125 * flow[e, h]
-                    take_up.append(0.025 - scaled)
-                    take_down.append(0.025 + scaled)
-                fraction = main_ref[3, j, :, part]
-                for c in range(3):
-                    center = flow[c, h]
-                    x_low = moved_ref[c, r, :, part]
-                    x_up = moved_ref[c, r, :, x_span + h * LANES : x_span + (h + 1) * LANES]
-                    if h == 0:
-                        x_low = jnp.where(first_lane, edge[c], x_low)
-                    if h == chunks - 1:
-                        x_up = jnp.where(last_lane, edge[c], x_up)
-                    y_low = rows_ref[c, j, :, part]
-                    y_up = rows_ref[c, j + 2, :, part]
-                    z_low = jnp.where(first_layer, 0.0, pltpu.roll(center, 1, 0))
-                    z_up = jnp.where(last_layer, 0.0, pltpu.roll(center, NZ - 1, 0))
-                    total = (
-                        0.85 * center
-                        + (take_up[0] * x_up + take_down[0] * x_low)
-                        + (take_up[1] * y_up + take_down[1] * y_low)
-                        + (take_up[2] * z_up + take_down[2] * z_low)
-                    )
-                    value = fraction * total
-                    if c == 2:
-                        value = jnp.where(last_layer, 0.0, value)
-                    star[c, h] = value
-                    star_ref[c, j, :, part] = value
-            before = 0.0
-            for h in range(chunks):
-                part = slice(h * LANES, (h + 1) * LANES)
-                moved = pltpu.roll(star[0, h], 1, 1)
-                x_low = jnp.where(first_lane, before, moved)
-                before = moved
-                z_low = jnp.where(first_layer, 0.0, pltpu.roll(star[2, h], 1, 0))
-                y_low = carry_ref[:, part]
-                source_ref[j, :, part] = (x_low - star[0, h]) + (y_low - star[1, h]) + (z_low - star[2, h])
-                carry_ref[:, part] = star[1, h]
-            edge = pltpu.roll(star[0, chunks - 1], (at + 1) % LANES, 1)
-            gx_ref[:, y_chunk] = jnp.where(lanes == at, edge, gx_ref[:, y_chunk])
+                    both = jnp.where(even_lane, xb_ref[c, :, halo_chunk], xa_ref[c, :, halo_chunk])
+                    edge = pltpu.roll(both, (LANES - held) % LANES, 1)
+                    centers = [main_ref[c, j, :, part] for part in lane_parts]
+                    to_right = [pltpu.roll(center, 1, 1) for center in centers]
+                    to_left = [pltpu.roll(center, LANES - 1, 1) for center in centers]
+                    star = []
+                    for h, part in enumerate(lane_parts):
+                        center = centers[h]
+                        before = edge if h == 0 else to_right[h - 1]
+                        after = edge if h == chunks - 1 else to_left[h + 1]
+                        x_low = jnp.where(first_lane, before, to_right[h])
+                        x_up = jnp.where(last_lane, after, to_left[h])
+                        total = x_up + x_low
+                        moved = speed[0][h] * (x_up - x_low)
+                        y_low = neighbour_row(group, r - 1, c, part)
+                        y_up = neighbour_row(group, r + 1, c, part)
+                        total = total + (y_up + y_low)
+                        moved = moved + speed[1][h] * (y_up - y_low)
+                        z_low = jnp.where(first_layer, 0.0, pltpu.roll(center, 1, 0))
+                        z_up = jnp.where(last_layer, 0.0, pltpu.roll(center, NZ - 1, 0))
+                        total = total + (z_up + z_low)
+                        moved = moved + speed[2][h] * (z_up - z_low)
+                        value = main_ref[3, j, :, part] * ((0.85 * center + 0.025 * total) - moved)
+                        if c == 2:
+                            value = jnp.where(last_layer, 0.0, value)
+                        star_ref[c, j, :, part] = value
+                        star.append(value)
+                    if c == 0:
+                        moved = [pltpu.roll(value, 1, 1) for value in star]
+                        for h in range(chunks):
+                            before = 0.0 if h == 0 else moved[h - 1]
+                            source.append(jnp.where(first_lane, before, moved[h]) - star[h])
+                        edge = pltpu.roll(star[-1], (at + 1) % LANES, 1)
+                        gathered = jnp.where(lanes == at, edge, gathered)
+                    elif c == 1:
+                        source = [source[h] + (carried[h] - star[h]) for h in range(chunks)]
+                        carried = star
+                    else:
+                        for h, part in enumerate(lane_parts):
+                            z_low = jnp.where(first_layer, 0.0, pltpu.roll(star[h], 1, 0))
+                            source_ref[j, :, part] = source[h] + (z_low - star[h])
+            for h, part in enumerate(lane_parts):
+                carry_ref[:, part] = carried[h]
+            gx_ref[:, y_chunk] = gathered
 
         def transform(group):
-            rows = pl.ds(pl.multiple_of(group * 8, 8), 8)
-            part = source_ref[rows].reshape(8 * NZ, x_span)
+            rows_at = pl.ds(pl.multiple_of(group * 8, 8), 8)
+            part = source_ref[rows_at].reshape(8 * NZ, x_span)
             modes = times_table(table_times(cosine_ref, part), sine_ref)
-            modes_ref[:, rows, :] = modes.reshape(NZ, 8, x_span)
-
-        def shift(group, moved_ref):
-            for c in range(3):
-                center = rows_ref[c, pl.ds(group * 8 + 1, 8)].reshape(8 * NZ, x_span)
-                moved = mm(jnp.concatenate(pieces(center), axis=1), shift_ref[...])
-                moved_ref[c] = moved.reshape(8, NZ, 2 * x_span)
-
-        shift(0, even_ref)
-
-        def two_groups(pair, _):
-            group = 2 * pair
-            transform(jnp.maximum(group - 1, 0))
-            shift(group + 1, odd_ref)
-            for r in range(8):
-                row(group, r, even_ref)
-            transform(group)
-            shift(jnp.minimum(group + 2, B // 8 - 1), even_ref)
-            for r in range(8):
-                row(group + 1, r, odd_ref)
+            modes_ref[:, rows_at, :] = modes.reshape(NZ, 8, x_span)
+
+        rows(0)
+
+        def group_of_rows(group, _):
+            transform(group - 1)
+            rows(group)
             return _
 
-        lax.fori_loop(0, B // 16, two_groups, 0)
+        lax.fori_loop(1, B // 8, group_of_rows, 0)
         transform(B // 8 - 1)
         gy_ref[...] = carry_ref[...]
 
@@ -336,9 +331,8 @@
                 full3,
                 pl.BlockSpec((3, NZ, x_span), lambda s, kinds: (0, 0, 0)),
                 pl.BlockSpec((3, NZ, x_span), lambda s, kinds: (0, 0, 0)),
-                pl.BlockSpec((8 * NZ, 24 * NZ), lambda s, kinds: (0, 0)),
+                pl.BlockSpec((16 * NZ, 8 * NZ), lambda s, kinds: (0, 0)),
                 pl.BlockSpec((None, 3 * x_span, x_span), lambda s, kinds: (kinds[1], 0, 0)),
-                pl.BlockSpec((2 * x_span, 2 * x_span), lambda s, kinds: (0, 0)),
             ],
             out_specs=[
                 pl.BlockSpec((3, B, NZ, x_span), lambda s, kinds: (0, s, 0, 0)),
@@ -347,11 +341,9 @@
                 pl.BlockSpec((NZ, x_span), lambda s, kinds: (0, 0)),
             ],
             scratch_shapes=[
-                pltpu.VMEM((3, B + 2, NZ, x_span), f32),
+                pltpu.VMEM((3, 2, NZ, x_span), f32),
                 pltpu.VMEM((B, NZ, x_span), f32),
                 pltpu.VMEM((NZ, x_span), f32),
-                pltpu.VMEM((3, 8, NZ, 2 * x_span), f32),
-                pltpu.VMEM((3, 8, NZ, 2 * x_span), f32),
             ],
         ),
         out_shape=[
@@ -361,7 +353,7 @@
             jax.ShapeDtypeStruct((NZ, x_span), f32),
         ],
         compiler_params=params(),
-    )(kinds, tile, tile, tile, x_below, x_above, y_below, y_above, cosine, sine_x, shift)
+    )(kinds, tile, tile, tile, x_below, x_above, y_below, y_above, cosine, sine_x)
 
 
 def first_solve(modes, sine_yt, sine_ytr, sine_xt, edge_y, edge_x, eigen, levels, flux_x, flux_y, cosine, kinds):
@@ -377,11 +369,14 @@
             k = step * batch + i
             spectrum = table_times(yt_ref, modes_ref[i])
             spectrum_ref[i] = spectrum
-            high, low = pieces(spectrum * inverse_of(eigen_ref[...] + levels_ref[k]))
-            found = mm(edge_y_ref[...], high) + mm(edge_y_ref[...], low)
-            found = found[:8] + found[8:]
-            rows_ref[pl.ds(k, 1)] = found[0:1]
-            rows_ref[pl.ds(layers + k, 1)] = found[1:2]
+            solved = spectrum * inverse_of(eigen_ref[...] + levels_ref[k])
+            high, low = pieces(solved)
+            for side in range(2):
+                found = [
+                    jnp.sum(solved[:, start : start + LANES] * edge_y_ref[side], axis=0, keepdims=True)
+                    for start in range(0, x_span, LANES)
+                ]
+                rows_ref[pl.ds(side * layers + k, 1)] = jnp.concatenate(found, axis=1)
             found = mm_transposed(edge_x_ref[...], high) + mm_transposed(edge_x_ref[...], low)
             found = found[:8] + found[8:]
             columns_ref[pl.ds(k, 1)] = found[0:1]
@@ -405,10 +400,10 @@
             grid=(steps,),
             in_specs=[
                 pl.BlockSpec((batch, y_span, x_span), lambda k, kinds: (k, 0, 0)),
-                pl.BlockSpec((None, y_span, 3 * y_span), lambda k, kinds: (kinds[0], 0, 0)),
+                pl.BlockSpec((None, 2 * y_span, y_span), lambda k, kinds: (kinds[0], 0, 0)),
                 pl.BlockSpec((None, 3 * y_span, y_span), lambda k, kinds: (kinds[0], 0, 0)),
                 pl.BlockSpec((None, 3 * x_span, x_span), lambda k, kinds: (kinds[1], 0, 0)),
-                pl.BlockSpec((None, 16, y_span), lambda k, kinds: (kinds[0], 0, 0)),
+                pl.BlockSpec((None, 2, y_span, LANES), lambda k, kinds: (kinds[0], 0, 0, 0)),
                 pl.BlockSpec((None, 16, x_span), lambda k, kinds: (kinds[1], 0, 0)),
                 pl.BlockSpec((None, y_span, x_span), lambda k, kinds: (kinds[0] * 3 + kinds[1], 0, 0)),
                 pl.BlockSpec(memory_space=pltpu.SMEM),
@@ -432,28 +427,36 @@
 
 def second_solve(spectrum, sums, sine_y, sine_yr, sine_x, sine_xt, edge_y, edge_x, eigen, levels, kinds):
     layers, y_span, x_span = spectrum.shape
-    batch = 4
+    batch = 8
     sides = 2 * layers
 
     def kernel(kinds_ref, spectrum_ref, sums_ref, y_ref, yr_ref, x_ref, xt_ref, edge_y_ref, edge_x_ref,
-               eigen_ref, levels_ref, out_ref, left_ref, right_ref):
+               eigen_ref, levels_ref, out_ref, along_x_ref, along_y_ref):
         step = pl.program_id(0)
 
         @pl.when(step == 0)
         def _():
-            right_ref[:sides] = edge_x_ref[...]
-            right_ref[sides:] = times_table(sums_ref[:, :x_span], x_ref)
-            left = jnp.concatenate([times_table(sums_ref[:, x_span:], yr_ref), edge_y_ref[...]], axis=0)
-            left_high, left_low = pieces(left.T)
-            left_ref[...] = jnp.concatenate([left_high, left_high, left_low], axis=1)
-
-        row_ids = lax.broadcasted_iota(jnp.int32, (2 * sides, x_span), 0) & (layers - 1)
-        for i in range(batch):
-            k = step * batch + i
-            high, low = pieces(jnp.where(row_ids == k, right_ref[...], 0.0))
-            added = mm(left_ref[...], jnp.concatenate([high, low, high], axis=0))
-            solved = (spectrum_ref[i] + added) * inverse_of(eigen_ref[...] + levels_ref[k])
-            out_ref[i] = times_table(table_times(y_ref, solved), xt_ref)
+            along_x_ref[...] = times_table(sums_ref[:, :x_span], x_ref)
+            along_y_ref[...] = times_table(sums_ref[:, x_span:], yr_ref)
+
+        low_side = pl.ds(pl.multiple_of(step * batch, batch), batch)
+        high_side = pl.ds(pl.multiple_of(layers + step * batch, batch), batch)
+        left = jnp.concatenate([along_y_ref[low_side], along_y_ref[high_side], edge_y_ref[...]], axis=0)
+        right = jnp.concatenate([edge_x_ref[...], along_x_ref[low_side], along_x_ref[high_side]], axis=0)
+        left_high = left.astype(jnp.bfloat16).astype(f32)
+        blank = jnp.zeros((LANES - 12 * batch, y_span), f32)
+        left = jnp.concatenate([left_high, left_high, left - left_high, blank], axis=0).T.astype(jnp.bfloat16)
+        blank = jnp.zeros((LANES - 12 * batch, x_span), jnp.bfloat16)
+        row_ids = lax.broadcasted_iota(jnp.int32, (4 * batch, x_span), 0) & (batch - 1)
+        for start in range(0, batch, 4):
+            along_y = []
+            for i in range(start, start + 4):
+                high, low = pieces(jnp.where(row_ids == i, right, 0.0))
+                added = mm(left, jnp.concatenate([high, low, high, blank], axis=0))
+                solved = (spectrum_ref[i] + added) * inverse_of(eigen_ref[...] + levels_ref[step * batch + i])
+                along_y.append(table_times(y_ref, solved))
+            found = times_table(jnp.concatenate(along_y, axis=0), xt_ref)
+            out_ref[start : start + 4] = found.reshape(4, y_span, x_span)
 
     return pl.pallas_call(
         kernel,
@@ -463,19 +466,19 @@
             in_specs=[
                 pl.BlockSpec((batch, y_span, x_span), lambda k, kinds: (k, 0, 0)),
                 pl.BlockSpec((sides, x_span + y_span), lambda k, kinds: (0, 0)),
-                pl.BlockSpec((None, y_span, 3 * y_span), lambda k, kinds: (kinds[0], 0, 0)),
+                pl.BlockSpec((None, 2 * y_span, y_span), lambda k, kinds: (kinds[0], 0, 0)),
                 pl.BlockSpec((None, 3 * y_span, y_span), lambda k, kinds: (kinds[0], 0, 0)),
                 pl.BlockSpec((None, 3 * x_span, x_span), lambda k, kinds: (kinds[1], 0, 0)),
                 pl.BlockSpec((None, 3 * x_span, x_span), lambda k, kinds: (kinds[1], 0, 0)),
-                pl.BlockSpec((None, sides, y_span), lambda k, kinds: (kinds[0], 0, 0)),
-                pl.BlockSpec((None, sides, x_span), lambda k, kinds: (kinds[1], 0, 0)),
+                pl.BlockSpec((None, 2 * batch, y_span), lambda k, kinds: (kinds[0], 0, 0)),
+                pl.BlockSpec((None, 2 * batch, x_span), lambda k, kinds: (kinds[1], 0, 0)),
                 pl.BlockSpec((None, y_span, x_span), lambda k, kinds: (kinds[0] * 3 + kinds[1], 0, 0)),
                 pl.BlockSpec(memory_space=pltpu.SMEM),
             ],
             out_specs=pl.BlockSpec((batch, y_span, x_span), lambda k, kinds: (k, 0, 0)),
             scratch_shapes=[
-                pltpu.VMEM((y_span, 6 * sides), jnp.bfloat16),
-                pltpu.VMEM((2 * sides, x_span), f32),
+                pltpu.VMEM((sides, x_span), f32),
+                pltpu.VMEM((sides, y_span), f32),
             ],
         ),
         out_shape=jax.ShapeDtypeStruct((layers, y_span, x_span), f32),
@@ -516,23 +519,21 @@
         layers_at = lax.broadcasted_iota(jnp.int32, (NZ, LANES), 0)
         last_layer = layers_at == NZ - 1
         last_lane = lanes == LANES - 1
-        for q in range(B // 8):
-            part = modes_ref[:, 8 * q : 8 * q + 8, :].reshape(8 * NZ, x_span)
-            rows_ref[8 * q : 8 * q + 8] = table_times(cosine_ref, part).reshape(8, NZ, x_span)
-
-        @pl.when(step < rows_n - 1)
-        def _():
-            part = after_ref[...].reshape(8 * NZ, x_span)
-            rows_ref[B] = table_times(cosine_ref, part).reshape(8, NZ, x_span)[0]
-
-        @pl.when(step == rows_n - 1)
-        def _():
-            rows_ref[B] = jnp.where(kinds_ref[0] == 2, 0.0, beyond_ref[:, :x_span] - rows_ref[B - 1])
-
-        def four_rows(jq, _):
+        def layers_of(part):
+            return table_times(cosine_ref, part.reshape(8 * NZ, x_span)).reshape(8, NZ, x_span)
+
+        @pl.when(step == 0)
+        def _():
+            rows_ref[:8] = layers_of(modes_ref[:, :8, :])
+
+        @pl.when(step > 0)
+        def _():
+            rows_ref[:8] = rows_ref[B:]
+
+        def four_rows(jq):
             y = step * B + jq * 4
-            y_chunk = pl.ds(pl.multiple_of(x_span + y // LANES * LANES, LANES), LANES)
-            block = pl.ds(pl.multiple_of(jq * LANES, LANES), LANES)
+            y_chunk = pl.ds(pl.multiple_of(x_span + step * B // LANES * LANES, LANES), LANES)
+            block = slice(jq * LANES, (jq + 1) * LANES)
             to_left = [
                 [pltpu.roll(rows_ref[jq * 4 + t, :, h * LANES : (h + 1) * LANES], LANES - 1, 1) for t in range(4)]
                 for h in range(chunks)
@@ -559,9 +560,20 @@
                     swapped = swap_groups(found[channel], lanes)
                     for g in range(4):
                         blocks_ref[half, 4 * h + g, channel, :, block] = swapped[g]
-            return _
-
-        lax.fori_loop(0, B // 4, four_rows, 0)
+
+        groups = B // 8
+        rows_ref[8:16] = layers_of(modes_ref[:, 8:16, :])
+        for group in range(groups):
+            ahead = group + 2
+            if ahead < groups:
+                rows_ref[8 * ahead : 8 * ahead + 8] = layers_of(modes_ref[:, 8 * ahead : 8 * ahead + 8, :])
+            elif ahead == groups:
+                beyond = jnp.where(kinds_ref[0] == 2, 0.0, beyond_ref[:, :x_span] - rows_ref[B - 1])
+                found = layers_of(after_ref[...])
+                rows_ref[B] = jnp.where(step == rows_n - 1, beyond, found[0])
+                rows_ref[B + 1 :] = found[1:]
+            four_rows(2 * group)
+            four_rows(2 * group + 1)
 
         for copy in copies(step, half):
             copy.start()
@@ -582,11 +594,11 @@
                 pl.BlockSpec((3, B, NZ, x_span), lambda s, inv, kinds: (0, s, 0, 0)),
                 pl.BlockSpec((2 * layers, x_span + y_span), lambda s, inv, kinds: (0, 0)),
                 pl.BlockSpec((layers, layers), lambda s, inv, kinds: (0, 0)),
-                pl.BlockSpec((8 * NZ, 24 * NZ), lambda s, inv, kinds: (0, 0)),
+                pl.BlockSpec((16 * NZ, 8 * NZ), lambda s, inv, kinds: (0, 0)),
             ],
             out_specs=[pl.BlockSpec(memory_space=pl.ANY), pl.BlockSpec(memory_space=pl.ANY)],
             scratch_shapes=[
-                pltpu.VMEM((B + 1, NZ, x_span), f32),
+                pltpu.VMEM((B + 8, NZ, x_span), f32),
                 pltpu.VMEM((2, cols_n, 4, NZ, B * B), f32),
                 pltpu.VMEM((NZ, x_span + y_span), f32),
                 pltpu.SemaphoreType.DMA((2, cols_n)),
@@ -682,14 +694,13 @@
 
     cosine = jnp.asarray(tables["cosine"])
     local = {name: jnp.asarray(tables[name]) for name in (
-        "y", "yr", "yt", "ytr", "x", "xt", "edge_y", "edge_x", "few_y", "few_x", "eigen", "levels", "picks_x", "picks_y", "fold_x", "line_y",
+        "y", "yr", "yt", "ytr", "x", "xt", "edge_y", "edge_x", "wide_y", "few_x", "eigen", "levels", "picks_x", "picks_y", "fold_x", "line_y",
         "eig_x", "eig_y")}
     star, modes, flux_x, flux_y = advance(
-        tile, x_below, x_above, y_below, y_above, jnp.asarray(tables["cosine8"]), local["x"],
-        jnp.asarray(tables["shift"]), kinds
+        tile, x_below, x_above, y_below, y_above, jnp.asarray(tables["cosine8"]), local["x"], kinds
     )
     spectrum, bundle = first_solve(
-        modes, local["yt"], local["ytr"], local["xt"], local["few_y"], local["few_x"], local["eigen"],
+        modes, local["yt"], local["ytr"], local["xt"], local["wide_y"], local["few_x"], local["eigen"],
         local["levels"], flux_x, flux_y, cosine, kinds
     )
     width = x_span + y_span
@@ -744,9 +755,6 @@
         "cosine8": left_table(cosine8),
         "cosine8t": left_table(cosine8.T),
     }
-    below = np.eye(x_span, k=1)
-    shift = np.concatenate([below, below.T], axis=1)
-    tables["shift"] = np.concatenate([shift, shift], axis=0).astype(ml_dtypes.bfloat16)
     values = {}
     for name, length in (("y", y_span), ("x", x_span)):
         bases = tile_bases(length)
@@ -758,12 +766,14 @@
             tables["yr"] = np.stack([right_table(b) for b, _ in bases])
             tables["yt"] = np.stack([left_table(b.T) for b, _ in bases])
             tables["ytr"] = np.stack([right_table(b.T) for b, _ in bases])
-        edges = np.stack([np.repeat(b[[0, -1]], NZ, axis=0) for b, _ in bases])
+        edges = np.stack([np.repeat(b[[0, -1]], 8, axis=0) for b, _ in bases])
         tables["edge_" + name] = single(edges)
         few = np.zeros((3, 16, length), ml_dtypes.bfloat16)
         for i, (b, _) in enumerate(bases):
             few[i, 0:2], few[i, 8:10] = parts_of(b[[0, -1]])
         tables["few_" + name] = few
+        tables["wide_" + name] = single(np.stack([
+            np.repeat(b[[0, -1]][:, :, None], LANES, axis=2) for b, _ in bases]))
         values[name] = [v for _, v in bases]
     tables["eigen"] = single(
         np.stack([ey[:, None] + ex[None, :] for ey in values["y"] for ex in values["x"]])

time: 230 us -> 221 us (0.961)
  Pallas kernels: 176 us -> 167 us
    pallas_call x1, Pallas kernels: 22.7 us -> 16.9 us  [second_solve(): pl.pallas_call(kernel, grid_spec=pltpu.PrefetchScalarGridSpec(num_scalar_...]
    pallas_call x1, Pallas kernels: 34.8 us -> 31.2 us  [finish(): pl.pallas_call(kernel, grid_spec=pltpu.PrefetchScalarGridSpec(num_scalar_...]
    pallas_call x1, Pallas kernels: 15.5 us -> 18.8 us  [first_solve(): pl.pallas_call(kernel, grid_spec=pltpu.PrefetchScalarGridSpec(num_scalar_...]
    pallas_call x1, Pallas kernels: 59.4 us -> 56.6 us  [advance(): pl.pallas_call(kernel, grid_spec=pltpu.PrefetchScalarGridSpec(num_scalar_...]
where the time goes in v4:
time: 221 us; the launch traced here: 220 us
  Pallas kernels  167 us (76%)
  blocking collectives  29.8 us (13%)
  starting transfers between devices  10.5 us (5%)
  local copies, waits for them, and re-layouts  5.75 us (3%)
  other arithmetic  5.11 us (2%)
    pallas_call x1, Pallas kernels, advance(): pl.pallas_call(kernel, grid_spec=pltpu.PrefetchScalarGridSpec(num_scalar_...  56.6 us
    pallas_call x1, Pallas kernels, finish(): pl.pallas_call(kernel, grid_spec=pltpu.PrefetchScalarGridSpec(num_scalar_...  31.2 us
    pallas_call x1, Pallas kernels, gather_tile(): pl.pallas_call(kernel, grid_spec=pltpu.PrefetchScalarGridSpec(num_scalar_...  26.9 us
    all_to_all x1, blocking collectives, shards(): lax.all_to_all(bundle, ('pa', 'pb'), split_axis=1, concat_axis=1, tiled=T...  19.9 us
    pallas_call x1, Pallas kernels, first_solve(): pl.pallas_call(kernel, grid_spec=pltpu.PrefetchScalarGridSpec(num_scalar_...  18.8 us
    pallas_call x1, Pallas kernels, second_solve(): pl.pallas_call(kernel, grid_spec=pltpu.PrefetchScalarGridSpec(num_scalar_...  16.9 us
    pallas_call x1, Pallas kernels, solve_interfaces(): pl.pallas_call(kernel, grid_spec=pltpu.PrefetchScalarGridSpec(num_scalar_...  16.2 us
    all_to_all x1, blocking collectives, shards(): lax.all_to_all(reply, ('pa', 'pb'), split_axis=1, concat_axis=1, tiled=True)  9.9 us
  transfers between devices with their start and end apart: 4, of which 2 were waited for; matrix products, arithmetic and copies ran while one was open for 1% of the time, Pallas kernels for 0%

profile of v4, /device:TPU:0, one launch (start us, length us, event | category | flops | bytes accessed | tf_op | source)
XLA Modules:
  0.0 220.0 jit_solution(12856823476495618089)
XLA Ops:
  0.6 1.3 select_reduce_fusion.inverse_ref
  1.9 26.9 %shard_map.248 = (f32[4,256,32,256]{3,2,1,0:T(8,128)}, f32[3,32,512]{2,1,0:T(8,128)}, f32[3,32,512]{2,1,0:T(8,128)}) custom-call(s32[64]{0:T(128)} %select_reduce_fusion.inverse_ref, f32[3,64,32,1024]{3,2,1,0:T(8,128)} %refs_7_.1, f32[3,64,32,1024]{3,2,1,0:T(8,128)} %refs_7_.1, f32[3,64,32,1024]{3,2,1,0:T(8,128)} %refs_7_.1, f32[3,64,32,1024]{3,2,1,0:T(8,128)} %refs_7_.1, ...), custom_call_target="tpu_custom_call" | custom-call | tf_op jit(solution)/shard_map/pallas_call | solution.py:186
  28.8 4.9 %collective-permute-start = (f32[3,32,512]{2,1,0:T(8,128)}, f32[3,32,512]{2,1,0:T(8,128)S(1)}, u32[]{:S(2)}, u32[]{:S(2)}) collective-permute-start(f32[3,32,512]{2,1,0:T(8,128)} %get-tuple-element.14), channel_id=1, source_target_pairs={{0,1},{1,2},{2,3},{3,4},{4,5},{5,6},{6,7},{8,9},{9,10},{10,11},{11... | collective-permute-start | bytes 589832 | tf_op jit(solution)/shard_map/ppermute | solution.py:687
  33.7 1.3 collective-permute-start.1
  35.0 1.0 slice_bitcast_fusion
  36.0 1.3 collective-permute-start.3
  37.3 3.0 %collective-permute-start.2 = (f32[3,32,256]{2,1,0:T(8,128)S(1)}, f32[3,32,256]{2,1,0:T(8,128)S(1)}, u32[]{:S(2)}, u32[]{:S(2)}) collective-permute-start(f32[3,32,256]{2,1,0:T(8,128)S(1)} %get-tuple-element.25), channel_id=1, source_target_pairs={{0,8},{8,16},{16,24},{1,9},{9,17},{17,25},{2,10},{10,18},{18,26},{... | collective-permute-start | bytes 294920 | tf_op jit(solution)/shard_map/ppermute | solution.py:687
  40.3 0.6 pad_add_fusion.kinds_ref
  40.9 0.3 collective-permute-done.2.yb_ref
  41.2 0.9 collective-permute-done.1.xa_ref
  42.2 0.7 copy-done.1
  42.9 56.6 %shard_map.249 = (f32[3,256,32,256]{3,2,1,0:T(8,128)}, f32[32,256,256]{2,1,0:T(8,128)}, f32[32,256]{1,0:T(8,128)}, f32[32,256]{1,0:T(8,128)}) custom-call(s32[3]{0:T(128)} %pad_add_fusion.kinds_ref, f32[4,256,32,256]{3,2,1,0:T(8,128)} %get-tuple-element.13.main_ref.prev_ref.next_ref, f32[4,256,32,256]{3,2,1,0:T(8,128)} %get-tuple-element.13.main_ref.prev_ref.next_ref, ...), custom_call_target="tpu_custom_call" | custom-call | tf_op jit(solution)/shard_map/pallas_call | solution.py:321
  99.4 18.8 %shard_map.250 = (f32[32,256,256]{2,1,0:T(8,128)}, f32[3,32,512]{2,1,0:T(8,128)}) custom-call(s32[3]{0:T(128)} %pad_add_fusion.kinds_ref, f32[32,256,256]{2,1,0:T(8,128)} %get-tuple-element.16.modes_ref, bf16[3,512,256]{2,1,0:T(8,128)(2,1)} %constant.77.clone.yt_ref, bf16[3,768,256]{2,1,0:T(8,128)(2,1)} %constant.78.clone.ytr_ref.xt_ref, ...), custom_call_target="tpu_custom_call" | custom-call | tf_op jit(solution)/shard_map/pallas_call | solution.py:396
  118.2 1.1 copy.44
  119.3 19.9 %all_to_all.10 = f32[3,32,512]{2,0,1:T(4,128)S(1)} all-to-all(f32[3,32,512]{2,0,1:T(4,128)S(1)} %copy.44), channel_id=1, replica_groups=mesh['pa'=4,'pb'=8] {'pa','pb'}, dimensions={1} | all-to-all | bytes 393216 | tf_op jit(solution)/shard_map/all_to_all | solution.py:708
  139.2 0.1 fusion.3
  139.2 0.1 fusion.4
  139.5 0.6 pad.12.lines_x_ref
  140.2 0.6 rev.6
  140.8 0.7 pad_maximum_fusion.lines_y_ref
  141.5 16.2 %shard_map.251 = (f32[16,1024]{1,0:T(8,128)}, f32[2,16,1024]{2,1,0:T(8,128)}) custom-call(s32[3]{0:T(128)} %pad_add_fusion.kinds_ref, f32[16,1024]{1,0:T(8,128)} %pad.12.lines_x_ref, f32[2,16,1024]{2,1,0:T(8,128)} %pad_maximum_fusion.lines_y_ref, f32[2,16,2048]{2,1,0:T(8,128)} %constant.84.clone.picks_x_ref, f32[2,16,1024]{2,1,0:T(8,128)} %constant.85.clone.picks_y_ref, ...), custom_call_target="tpu_custom_call" | custom-call | tf_op jit(solution)/shard_map/pallas_call | solution.py:645
  157.7 0.8 add_bitcast_fusion.1
  158.4 0.8 slice_add_fusion
  159.2 0.8 slice_select_fusion
  160.1 0.7 rev.7
  160.9 0.1 concatenate.52
  161.0 0.1 concatenate.51
  161.0 0.1 maximum_maximum_fusion
  161.2 9.9 %all_to_all.11 = f32[2,32,512]{2,0,1:T(2,128)S(1)} all-to-all(f32[2,32,512]{2,0,1:T(2,128)S(1)} %maximum_maximum_fusion), channel_id=1, replica_groups=mesh['pa'=4,'pb'=8] {'pa','pb'}, dimensions={1} | all-to-all | bytes 262144 | tf_op jit(solution)/shard_map/all_to_all | solution.py:735
  171.1 0.7 copy.53
  171.7 16.9 %shard_map.252.modes_ref.after_ref = f32[32,256,256]{2,1,0:T(8,128)} custom-call(s32[3]{0:T(128)} %pad_add_fusion.kinds_ref, f32[32,256,256]{2,1,0:T(8,128)} %get-tuple-element.19.spectrum_ref, f32[64,512]{1,0:T(8,128)} %bitcast.41, bf16[3,512,256]{2,1,0:T(8,128)(2,1)} %constant.75.clone.y_ref, bf16[3,768,256]{2,1,0:T(8,128)(2,1)} %constant.76.clone.sine_ref.yr_ref.x_ref, ...), custom_call_target="tpu_custom_call" | custom-call | tf_op jit(solution)/shard_map/pallas_call | solution.py:461
  188.7 31.2 %shard_map.253 = (f32[3,64,32,1024]{3,2,1,0:T(8,128)}, f32[64,32,1024]{2,1,0:T(8,128)}) custom-call(s32[64]{0:T(128)} %select_reduce_fusion.inverse_ref, s32[3]{0:T(128)} %pad_add_fusion.kinds_ref, f32[32,256,256]{2,1,0:T(8,128)} %shard_map.252.modes_ref.after_ref, f32[32,256,256]{2,1,0:T(8,128)} %shard_map.252.modes_ref.after_ref, ...), custom_call_target="tpu_custom_call" | custom-call | tf_op jit(solution)/shard_map/pallas_call | solution.py:586
  (30 shorter events, 0.3 us)
Async XLA Ops:
  28.8 12.4 %collective-permute-start = (f32[3,32,512]{2,1,0:T(8,128)}, f32[3,32,512]{2,1,0:T(8,128)S(1)}, u32[]{:S(2)}, u32[]{:S(2)}) collective-permute-start(f32[3,32,512]{2,1,0:T(8,128)} %get-tuple-element.14), channel_id=1, source_target_pairs={{0,1},{1,2},{2,3},{3,4},{4,5},{5,6},{6,7},{8,9},{9,10},{10,11},{11... | collective-permute-start | bytes 589832 | tf_op jit(solution)/shard_map/ppermute | solution.py:687
  33.7 8.5 %collective-permute-start.1 = (f32[3,32,512]{2,1,0:T(8,128)}, f32[3,32,512]{2,1,0:T(8,128)S(1)}, u32[]{:S(2)}, u32[]{:S(2)}) collective-permute-start(f32[3,32,512]{2,1,0:T(8,128)} %get-tuple-element.15), channel_id=1, source_target_pairs={{1,0},{2,1},{3,2},{4,3},{5,4},{6,5},{7,6},{9,8},{10,9},{11,10},{12... | collective-permute-start | bytes 589832 | tf_op jit(solution)/shard_map/ppermute | solution.py:690
  36.0 4.9 %collective-permute-start.3 = (f32[3,32,256]{2,1,0:T(8,128)S(1)}, f32[3,32,256]{2,1,0:T(8,128)S(1)}, u32[]{:S(2)}, u32[]{:S(2)}) collective-permute-start(f32[3,32,256]{2,1,0:T(8,128)S(1)} %get-tuple-element.24), channel_id=1, source_target_pairs={{8,0},{16,8},{24,16},{9,1},{17,9},{25,17},{10,2},{18,10},{26,18},{... | collective-permute-start | bytes 294920 | tf_op jit(solution)/shard_map/ppermute | solution.py:690
  37.3 4.0 %collective-permute-start.2 = (f32[3,32,256]{2,1,0:T(8,128)S(1)}, f32[3,32,256]{2,1,0:T(8,128)S(1)}, u32[]{:S(2)}, u32[]{:S(2)}) collective-permute-start(f32[3,32,256]{2,1,0:T(8,128)S(1)} %get-tuple-element.25), channel_id=1, source_target_pairs={{0,8},{8,16},{16,24},{1,9},{9,17},{17,25},{2,10},{10,18},{18,26},{... | collective-permute-start | bytes 294920 | tf_op jit(solution)/shard_map/ppermute | solution.py:687
  40.9 1.3 copy-start.2
  41.2 0.9 copy-start.3
  41.2 0.9 copy-start
  42.2 0.7 copy-start.1
  139.2 20.0 %copy-start.4 = (pred[8]{0:T(512)(128)(4,1)S(1)}, pred[8]{0:T(512)(128)(4,1)}, u32[]{:S(2)}) copy-start(pred[8]{0:T(512)(128)(4,1)} %constant.73.clone.1) | copy-start | bytes 28

commit v5 on v3

--- a/solution.py
+++ b/solution.py
@@ -199,13 +199,13 @@
     )(inverse, *([velocity] * cols_n), *([fluid] * cols_n))
 
 
-def advance(tile, x_below, x_above, y_below, y_above, cosine, sine_x, shift, kinds):
+def advance(tile, x_below, x_above, y_below, y_above, cosine, sine_x, kinds):
     _, y_span, _, x_span = tile.shape
     steps = y_span // B
     chunks = x_span // LANES
 
-    def kernel(kinds_ref, main_ref, prev_ref, next_ref, xb_ref, xa_ref, yb_ref, ya_ref, cosine_ref, sine_ref, shift_ref,
-               star_ref, modes_ref, gx_ref, gy_ref, rows_ref, source_ref, carry_ref, even_ref, odd_ref):
+    def kernel(kinds_ref, main_ref, prev_ref, next_ref, xb_ref, xa_ref, yb_ref, ya_ref, cosine_ref, sine_ref,
+               star_ref, modes_ref, gx_ref, gy_ref, mean_ref, rows_ref, source_ref, carry_ref):
         step = pl.program_id(0)
         lanes = lane_ids()
         layers = lax.broadcasted_iota(jnp.int32, (NZ, LANES), 0)
@@ -235,7 +235,7 @@
         halo_chunk = pl.ds(pl.multiple_of(step // 2 * LANES, LANES), LANES)
         even_lane = (lanes & 1) == 0
 
-        def row(group, r, moved_ref):
+        def row(group, r):
             j = group * 8 + r
             held = r % 4 * 32 + (step % 2) * 16 + 2 * (group * 2 + r // 4)
             at = (step % 4) * B + j
@@ -244,10 +244,13 @@
             for h in range(chunks):
                 for c in range(3):
                     flow[c, h] = rows_ref[c, j + 1, :, h * LANES : (h + 1) * LANES]
-            edge = {}
+            edge, to_right, to_left = {}, {}, {}
             for c in range(3):
                 both = jnp.where(even_lane, xb_ref[c, :, halo_chunk], xa_ref[c, :, halo_chunk])
                 edge[c] = pltpu.roll(both, (LANES - held) % LANES, 1)
+                for h in range(chunks):
+                    to_right[c, h] = pltpu.roll(flow[c, h], 1, 1)
+                    to_left[c, h] = pltpu.roll(flow[c, h], LANES - 1, 1)
             for h in range(chunks):
                 part = slice(h * LANES, (h + 1) * LANES)
                 take_up, take_down = [], []
@@ -258,12 +261,10 @@
                 fraction = main_ref[3, j, :, part]
                 for c in range(3):
                     center = flow[c, h]
-                    x_low = moved_ref[c, r, :, part]
-                    x_up = moved_ref[c, r, :, x_span + h * LANES : x_span + (h + 1) * LANES]
-                    if h == 0:
-                        x_low = jnp.where(first_lane, edge[c], x_low)
-                    if h == chunks - 1:
-                        x_up = jnp.where(last_lane, edge[c], x_up)
+                    before = edge[c] if h == 0 else to_right[c, h - 1]
+                    after = edge[c] if h == chunks - 1 else to_left[c, h + 1]
+                    x_low = jnp.where(first_lane, before, to_right[c, h])
+                    x_up = jnp.where(last_lane, after, to_left[c, h])
                     y_low = rows_ref[c, j, :, part]
                     y_up = rows_ref[c, j + 2, :, part]
                     z_low = jnp.where(first_layer, 0.0, pltpu.roll(center, 1, 0))
@@ -294,31 +295,22 @@
 
         def transform(group):
             rows = pl.ds(pl.multiple_of(group * 8, 8), 8)
-            part = source_ref[rows].reshape(8 * NZ, x_span)
+            part = source_ref[rows]
+            mean_ref[rows, :] = jnp.sum(part, axis=1) * NZ**-0.5
+            part = part.reshape(8 * NZ, x_span)
             modes = times_table(table_times(cosine_ref, part), sine_ref)
             modes_ref[:, rows, :] = modes.reshape(NZ, 8, x_span)
 
-        def shift(group, moved_ref):
-            for c in range(3):
-                center = rows_ref[c, pl.ds(group * 8 + 1, 8)].reshape(8 * NZ, x_span)
-                moved = mm(jnp.concatenate(pieces(center), axis=1), shift_ref[...])
-                moved_ref[c] = moved.reshape(8, NZ, 2 * x_span)
-
-        shift(0, even_ref)
-
-        def two_groups(pair, _):
-            group = 2 * pair
-            transform(jnp.maximum(group - 1, 0))
-            shift(group + 1, odd_ref)
+        for r in range(8):
+            row(0, r)
+
+        def group_of_rows(group, _):
+            transform(group - 1)
             for r in range(8):
-                row(group, r, even_ref)
-            transform(group)
-            shift(jnp.minimum(group + 2, B // 8 - 1), even_ref)
-            for r in range(8):
-                row(group + 1, r, odd_ref)
+                row(group, r)
             return _
 
-        lax.fori_loop(0, B // 16, two_groups, 0)
+        lax.fori_loop(1, B // 8, group_of_rows, 0)
         transform(B // 8 - 1)
         gy_ref[...] = carry_ref[...]
 
@@ -338,20 +330,18 @@
                 pl.BlockSpec((3, NZ, x_span), lambda s, kinds: (0, 0, 0)),
                 pl.BlockSpec((8 * NZ, 24 * NZ), lambda s, kinds: (0, 0)),
                 pl.BlockSpec((None, 3 * x_span, x_span), lambda s, kinds: (kinds[1], 0, 0)),
-                pl.BlockSpec((2 * x_span, 2 * x_span), lambda s, kinds: (0, 0)),
             ],
             out_specs=[
                 pl.BlockSpec((3, B, NZ, x_span), lambda s, kinds: (0, s, 0, 0)),
                 pl.BlockSpec((NZ, B, x_span), lambda s, kinds: (0, s, 0)),
                 pl.BlockSpec((NZ, y_span), lambda s, kinds: (0, 0)),
                 pl.BlockSpec((NZ, x_span), lambda s, kinds: (0, 0)),
+                pl.BlockSpec((B, x_span), lambda s, kinds: (s, 0)),
             ],
             scratch_shapes=[
                 pltpu.VMEM((3, B + 2, NZ, x_span), f32),
                 pltpu.VMEM((B, NZ, x_span), f32),
                 pltpu.VMEM((NZ, x_span), f32),
-                pltpu.VMEM((3, 8, NZ, 2 * x_span), f32),
-                pltpu.VMEM((3, 8, NZ, 2 * x_span), f32),
             ],
         ),
         out_shape=[
@@ -359,23 +349,31 @@
             jax.ShapeDtypeStruct((NZ, y_span, x_span), f32),
             jax.ShapeDtypeStruct((NZ, y_span), f32),
             jax.ShapeDtypeStruct((NZ, x_span), f32),
+            jax.ShapeDtypeStruct((y_span, x_span), f32),
         ],
         compiler_params=params(),
-    )(kinds, tile, tile, tile, x_below, x_above, y_below, y_above, cosine, sine_x, shift)
-
-
-def first_solve(modes, sine_yt, sine_ytr, sine_xt, edge_y, edge_x, eigen, levels, flux_x, flux_y, cosine, kinds):
+    )(kinds, tile, tile, tile, x_below, x_above, y_below, y_above, cosine, sine_x)
+
+
+def first_solve(modes, sine_yt, sine_ytr, sine_xt, edge_y, edge_x, eigen, levels, flux_x, flux_y, cosine, mean, exact_yt, exact_x, kinds):
     layers, y_span, x_span = modes.shape
     batch = 4
     steps = layers // batch
     sides = 2 * layers
 
     def kernel(kinds_ref, modes_ref, yt_ref, ytr_ref, xt_ref, edge_y_ref, edge_x_ref, eigen_ref, levels_ref,
-               flux_x_ref, flux_y_ref, cosine_ref, spectrum_ref, bundle_ref, rows_ref, columns_ref):
+               flux_x_ref, flux_y_ref, cosine_ref, mean_ref, exact_yt_ref, exact_x_ref, spectrum_ref, bundle_ref, rows_ref, columns_ref, exact_ref):
         step = pl.program_id(0)
+        @pl.when(step == 0)
+        def _():
+            along_x = dot_full(mean_ref[...], exact_x_ref[...], ((1,), (0,)))
+            exact_ref[...] = dot_full(exact_yt_ref[...], along_x, ((1,), (0,)))
+
         for i in range(batch):
             k = step * batch + i
             spectrum = table_times(yt_ref, modes_ref[i])
+            if i == 0:
+                spectrum = jnp.where(step == 0, exact_ref[...], spectrum)
             spectrum_ref[i] = spectrum
             high, low = pieces(spectrum * inverse_of(eigen_ref[...] + levels_ref[k]))
             found = mm(edge_y_ref[...], high) + mm(edge_y_ref[...], low)
@@ -415,45 +413,56 @@
                 pl.BlockSpec((layers, y_span), lambda k, kinds: (0, 0)),
                 pl.BlockSpec((layers, x_span), lambda k, kinds: (0, 0)),
                 pl.BlockSpec((layers, layers), lambda k, kinds: (0, 0)),
+                pl.BlockSpec((y_span, x_span), lambda k, kinds: (0, 0)),
+                pl.BlockSpec((None, y_span, y_span), lambda k, kinds: (kinds[0], 0, 0)),
+                pl.BlockSpec((None, x_span, x_span), lambda k, kinds: (kinds[1], 0, 0)),
             ],
             out_specs=[
                 pl.BlockSpec((batch, y_span, x_span), lambda k, kinds: (k, 0, 0)),
                 pl.BlockSpec((3, layers, x_span + y_span), lambda k, kinds: (0, 0, 0)),
             ],
-            scratch_shapes=[pltpu.VMEM((sides, x_span), f32), pltpu.VMEM((sides, y_span), f32)],
+            scratch_shapes=[pltpu.VMEM((sides, x_span), f32), pltpu.VMEM((sides, y_span), f32), pltpu.VMEM((y_span, x_span), f32)],
         ),
         out_shape=[
             jax.ShapeDtypeStruct((layers, y_span, x_span), f32),
             jax.ShapeDtypeStruct((3, layers, x_span + y_span), f32),
         ],
         compiler_params=params(),
-    )(kinds, modes, sine_yt, sine_ytr, sine_xt, edge_y, edge_x, eigen, levels, flux_x, flux_y, cosine)
+    )(kinds, modes, sine_yt, sine_ytr, sine_xt, edge_y, edge_x, eigen, levels, flux_x, flux_y, cosine, mean, exact_yt, exact_x)
 
 
 def second_solve(spectrum, sums, sine_y, sine_yr, sine_x, sine_xt, edge_y, edge_x, eigen, levels, kinds):
     layers, y_span, x_span = spectrum.shape
-    batch = 4
+    batch = 8
     sides = 2 * layers
 
     def kernel(kinds_ref, spectrum_ref, sums_ref, y_ref, yr_ref, x_ref, xt_ref, edge_y_ref, edge_x_ref,
-               eigen_ref, levels_ref, out_ref, left_ref, right_ref):
+               eigen_ref, levels_ref, out_ref, along_x_ref, along_y_ref):
         step = pl.program_id(0)
 
         @pl.when(step == 0)
         def _():
-            right_ref[:sides] = edge_x_ref[...]
-            right_ref[sides:] = times_table(sums_ref[:, :x_span], x_ref)
-            left = jnp.concatenate([times_table(sums_ref[:, x_span:], yr_ref), edge_y_ref[...]], axis=0)
-            left_high, left_low = pieces(left.T)
-            left_ref[...] = jnp.concatenate([left_high, left_high, left_low], axis=1)
-
-        row_ids = lax.broadcasted_iota(jnp.int32, (2 * sides, x_span), 0) & (layers - 1)
-        for i in range(batch):
-            k = step * batch + i
-            high, low = pieces(jnp.where(row_ids == k, right_ref[...], 0.0))
-            added = mm(left_ref[...], jnp.concatenate([high, low, high], axis=0))
-            solved = (spectrum_ref[i] + added) * inverse_of(eigen_ref[...] + levels_ref[k])
-            out_ref[i] = times_table(table_times(y_ref, solved), xt_ref)
+            along_x_ref[...] = times_table(sums_ref[:, :x_span], x_ref)
+            along_y_ref[...] = times_table(sums_ref[:, x_span:], yr_ref)
+
+        low_side = pl.ds(pl.multiple_of(step * batch, batch), batch)
+        high_side = pl.ds(pl.multiple_of(layers + step * batch, batch), batch)
+        left = jnp.concatenate([along_y_ref[low_side], along_y_ref[high_side], edge_y_ref[...]], axis=0)
+        right = jnp.concatenate([edge_x_ref[...], along_x_ref[low_side], along_x_ref[high_side]], axis=0)
+        left_high = left.astype(jnp.bfloat16).astype(f32)
+        blank = jnp.zeros((LANES - 12 * batch, y_span), f32)
+        left = jnp.concatenate([left_high, left_high, left - left_high, blank], axis=0).T.astype(jnp.bfloat16)
+        blank = jnp.zeros((LANES - 12 * batch, x_span), jnp.bfloat16)
+        row_ids = lax.broadcasted_iota(jnp.int32, (4 * batch, x_span), 0) & (batch - 1)
+        for start in range(0, batch, 4):
+            along_y = []
+            for i in range(start, start + 4):
+                high, low = pieces(jnp.where(row_ids == i, right, 0.0))
+                added = mm(left, jnp.concatenate([high, low, high, blank], axis=0))
+                solved = (spectrum_ref[i] + added) * inverse_of(eigen_ref[...] + levels_ref[step * batch + i])
+                along_y.append(table_times(y_ref, solved))
+            found = times_table(jnp.concatenate(along_y, axis=0), xt_ref)
+            out_ref[start : start + 4] = found.reshape(4, y_span, x_span)
 
     return pl.pallas_call(
         kernel,
@@ -467,15 +476,15 @@
                 pl.BlockSpec((None, 3 * y_span, y_span), lambda k, kinds: (kinds[0], 0, 0)),
                 pl.BlockSpec((None, 3 * x_span, x_span), lambda k, kinds: (kinds[1], 0, 0)),
                 pl.BlockSpec((None, 3 * x_span, x_span), lambda k, kinds: (kinds[1], 0, 0)),
-                pl.BlockSpec((None, sides, y_span), lambda k, kinds: (kinds[0], 0, 0)),
-                pl.BlockSpec((None, sides, x_span), lambda k, kinds: (kinds[1], 0, 0)),
+                pl.BlockSpec((None, 2 * batch, y_span), lambda k, kinds: (kinds[0], 0, 0)),
+                pl.BlockSpec((None, 2 * batch, x_span), lambda k, kinds: (kinds[1], 0, 0)),
                 pl.BlockSpec((None, y_span, x_span), lambda k, kinds: (kinds[0] * 3 + kinds[1], 0, 0)),
                 pl.BlockSpec(memory_space=pltpu.SMEM),
             ],
             out_specs=pl.BlockSpec((batch, y_span, x_span), lambda k, kinds: (k, 0, 0)),
             scratch_shapes=[
-                pltpu.VMEM((y_span, 6 * sides), jnp.bfloat16),
-                pltpu.VMEM((2 * sides, x_span), f32),
+                pltpu.VMEM((sides, x_span), f32),
+                pltpu.VMEM((sides, y_span), f32),
             ],
         ),
         out_shape=jax.ShapeDtypeStruct((layers, y_span, x_span), f32),
@@ -516,23 +525,21 @@
         layers_at = lax.broadcasted_iota(jnp.int32, (NZ, LANES), 0)
         last_layer = layers_at == NZ - 1
         last_lane = lanes == LANES - 1
-        for q in range(B // 8):
-            part = modes_ref[:, 8 * q : 8 * q + 8, :].reshape(8 * NZ, x_span)
-            rows_ref[8 * q : 8 * q + 8] = table_times(cosine_ref, part).reshape(8, NZ, x_span)
-
-        @pl.when(step < rows_n - 1)
-        def _():
-            part = after_ref[...].reshape(8 * NZ, x_span)
-            rows_ref[B] = table_times(cosine_ref, part).reshape(8, NZ, x_span)[0]
-
-        @pl.when(step == rows_n - 1)
-        def _():
-            rows_ref[B] = jnp.where(kinds_ref[0] == 2, 0.0, beyond_ref[:, :x_span] - rows_ref[B - 1])
-
-        def four_rows(jq, _):
+        def layers_of(part):
+            return table_times(cosine_ref, part.reshape(8 * NZ, x_span)).reshape(8, NZ, x_span)
+
+        @pl.when(step == 0)
+        def _():
+            rows_ref[:8] = layers_of(modes_ref[:, :8, :])
+
+        @pl.when(step > 0)
+        def _():
+            rows_ref[:8] = rows_ref[B:]
+
+        def four_rows(jq):
             y = step * B + jq * 4
-            y_chunk = pl.ds(pl.multiple_of(x_span + y // LANES * LANES, LANES), LANES)
-            block = pl.ds(pl.multiple_of(jq * LANES, LANES), LANES)
+            y_chunk = pl.ds(pl.multiple_of(x_span + step * B // LANES * LANES, LANES), LANES)
+            block = slice(jq * LANES, (jq + 1) * LANES)
             to_left = [
                 [pltpu.roll(rows_ref[jq * 4 + t, :, h * LANES : (h + 1) * LANES], LANES - 1, 1) for t in range(4)]
                 for h in range(chunks)
@@ -559,9 +566,20 @@
                     swapped = swap_groups(found[channel], lanes)
                     for g in range(4):
                         blocks_ref[half, 4 * h + g, channel, :, block] = swapped[g]
-            return _
-
-        lax.fori_loop(0, B // 4, four_rows, 0)
+
+        groups = B // 8
+        rows_ref[8:16] = layers_of(modes_ref[:, 8:16, :])
+        for group in range(groups):
+            ahead = group + 2
+            if ahead < groups:
+                rows_ref[8 * ahead : 8 * ahead + 8] = layers_of(modes_ref[:, 8 * ahead : 8 * ahead + 8, :])
+            elif ahead == groups:
+                beyond = jnp.where(kinds_ref[0] == 2, 0.0, beyond_ref[:, :x_span] - rows_ref[B - 1])
+                found = layers_of(after_ref[...])
+                rows_ref[B] = jnp.where(step == rows_n - 1, beyond, found[0])
+                rows_ref[B + 1 :] = found[1:]
+            four_rows(2 * group)
+            four_rows(2 * group + 1)
 
         for copy in copies(step, half):
             copy.start()
@@ -586,7 +604,7 @@
             ],
             out_specs=[pl.BlockSpec(memory_space=pl.ANY), pl.BlockSpec(memory_space=pl.ANY)],
             scratch_shapes=[
-                pltpu.VMEM((B + 1, NZ, x_span), f32),
+                pltpu.VMEM((B + 8, NZ, x_span), f32),
                 pltpu.VMEM((2, cols_n, 4, NZ, B * B), f32),
                 pltpu.VMEM((NZ, x_span + y_span), f32),
                 pltpu.SemaphoreType.DMA((2, cols_n)),
@@ -682,15 +700,14 @@
 
     cosine = jnp.asarray(tables["cosine"])
     local = {name: jnp.asarray(tables[name]) for name in (
-        "y", "yr", "yt", "ytr", "x", "xt", "edge_y", "edge_x", "few_y", "few_x", "eigen", "levels", "picks_x", "picks_y", "fold_x", "line_y",
+        "y", "yr", "yt", "ytr", "x", "xt", "edge_y", "edge_x", "few_y", "few_x", "exact_yt", "exact_x", "eigen", "levels", "picks_x", "picks_y", "fold_x", "line_y",
         "eig_x", "eig_y")}
-    star, modes, flux_x, flux_y = advance(
-        tile, x_below, x_above, y_below, y_above, jnp.asarray(tables["cosine8"]), local["x"],
-        jnp.asarray(tables["shift"]), kinds
+    star, modes, flux_x, flux_y, mean = advance(
+        tile, x_below, x_above, y_below, y_above, jnp.asarray(tables["cosine8"]), local["x"], kinds
     )
     spectrum, bundle = first_solve(
         modes, local["yt"], local["ytr"], local["xt"], local["few_y"], local["few_x"], local["eigen"],
-        local["levels"], flux_x, flux_y, cosine, kinds
+        local["levels"], flux_x, flux_y, cosine, mean, local["exact_yt"], local["exact_x"], kinds
     )
     width = x_span + y_span
     bundle = jnp.repeat(bundle, repeats, axis=1) if repeats > 1 else bundle
@@ -744,21 +761,20 @@
         "cosine8": left_table(cosine8),
         "cosine8t": left_table(cosine8.T),
     }
-    below = np.eye(x_span, k=1)
-    shift = np.concatenate([below, below.T], axis=1)
-    tables["shift"] = np.concatenate([shift, shift], axis=0).astype(ml_dtypes.bfloat16)
     values = {}
     for name, length in (("y", y_span), ("x", x_span)):
         bases = tile_bases(length)
         if name == "x":
+            tables["exact_x"] = single(np.stack([b for b, _ in bases]))
             tables["x"] = np.stack([right_table(b) for b, _ in bases])
             tables["xt"] = np.stack([right_table(b.T) for b, _ in bases])
         else:
+            tables["exact_yt"] = single(np.stack([b.T for b, _ in bases]))
             tables["y"] = np.stack([left_table(b) for b, _ in bases])
             tables["yr"] = np.stack([right_table(b) for b, _ in bases])
             tables["yt"] = np.stack([left_table(b.T) for b, _ in bases])
             tables["ytr"] = np.stack([right_table(b.T) for b, _ in bases])
-        edges = np.stack([np.repeat(b[[0, -1]], NZ, axis=0) for b, _ in bases])
+        edges = np.stack([np.repeat(b[[0, -1]], 8, axis=0) for b, _ in bases])
         tables["edge_" + name] = single(edges)
         few = np.zeros((3, 16, length), ml_dtypes.bfloat16)
         for i, (b, _) in enumerate(bases):

time: 230 us -> 209 us (0.909)
  Pallas kernels: 176 us -> 154 us
    pallas_call x1, Pallas kernels: 59.4 us -> 46.3 us  [advance(): pl.pallas_call(kernel, grid_spec=pltpu.PrefetchScalarGridSpec(num_scalar_...]
    pallas_call x1, Pallas kernels: 22.7 us -> 17 us  [second_solve(): pl.pallas_call(kernel, grid_spec=pltpu.PrefetchScalarGridSpec(num_scalar_...]
    pallas_call x1, Pallas kernels: 34.8 us -> 31.2 us  [finish(): pl.pallas_call(kernel, grid_spec=pltpu.PrefetchScalarGridSpec(num_scalar_...]
where the time goes in v5:
time: 209 us; the launch traced here: 208 us
  Pallas kernels  154 us (74%)
  blocking collectives  29.6 us (14%)
  starting transfers between devices  10.5 us (5%)
  local copies, waits for them, and re-layouts  5.75 us (3%)
  other arithmetic  5.3 us (3%)
    pallas_call x1, Pallas kernels, advance(): pl.pallas_call(kernel, grid_spec=pltpu.PrefetchScalarGridSpec(num_scalar_...  46.3 us
    pallas_call x1, Pallas kernels, finish(): pl.pallas_call(kernel, grid_spec=pltpu.PrefetchScalarGridSpec(num_scalar_...  31.2 us
    pallas_call x1, Pallas kernels, gather_tile(): pl.pallas_call(kernel, grid_spec=pltpu.PrefetchScalarGridSpec(num_scalar_...  26.9 us
    all_to_all x1, blocking collectives, shards(): lax.all_to_all(bundle, ('pa', 'pb'), split_axis=1, concat_axis=1, tiled=T...  19.7 us
    pallas_call x1, Pallas kernels, second_solve(): pl.pallas_call(kernel, grid_spec=pltpu.PrefetchScalarGridSpec(num_scalar_...  17 us
    pallas_call x1, Pallas kernels, first_solve(): pl.pallas_call(kernel, grid_spec=pltpu.PrefetchScalarGridSpec(num_scalar_...  16.8 us
    pallas_call x1, Pallas kernels, solve_interfaces(): pl.pallas_call(kernel, grid_spec=pltpu.PrefetchScalarGridSpec(num_scalar_...  16.2 us
    all_to_all x1, blocking collectives, shards(): lax.all_to_all(reply, ('pa', 'pb'), split_axis=1, concat_axis=1, tiled=True)  9.91 us
  transfers between devices with their start and end apart: 4, of which 2 were waited for; matrix products, arithmetic and copies ran while one was open for 1% of the time, Pallas kernels for 0%

profile of v5, /device:TPU:0, one launch (start us, length us, event | category | flops | bytes accessed | tf_op | source)
XLA Modules:
  0.0 207.8 jit_solution(1328277694603352489)
XLA Ops:
  0.6 1.4 select_reduce_fusion.inverse_ref
  2.0 26.9 %shard_map.266 = (f32[4,256,32,256]{3,2,1,0:T(8,128)}, f32[3,32,512]{2,1,0:T(8,128)}, f32[3,32,512]{2,1,0:T(8,128)}) custom-call(s32[64]{0:T(128)} %select_reduce_fusion.inverse_ref, f32[3,64,32,1024]{3,2,1,0:T(8,128)} %refs_7_.1, f32[3,64,32,1024]{3,2,1,0:T(8,128)} %refs_7_.1, f32[3,64,32,1024]{3,2,1,0:T(8,128)} %refs_7_.1, f32[3,64,32,1024]{3,2,1,0:T(8,128)} %refs_7_.1, ...), custom_call_target="tpu_custom_call" | custom-call | tf_op jit(solution)/shard_map/pallas_call | solution.py:185
  28.9 4.9 %collective-permute-start = (f32[3,32,512]{2,1,0:T(8,128)}, f32[3,32,512]{2,1,0:T(8,128)S(1)}, u32[]{:S(2)}, u32[]{:S(2)}) collective-permute-start(f32[3,32,512]{2,1,0:T(8,128)} %get-tuple-element.15), channel_id=1, source_target_pairs={{0,1},{1,2},{2,3},{3,4},{4,5},{5,6},{6,7},{8,9},{9,10},{10,11},{11... | collective-permute-start | bytes 589832 | tf_op jit(solution)/shard_map/ppermute | solution.py:693
  33.8 1.3 collective-permute-start.1
  35.1 1.0 slice_bitcast_fusion
  36.0 1.3 collective-permute-start.3
  37.3 3.0 %collective-permute-start.2 = (f32[3,32,256]{2,1,0:T(8,128)S(1)}, f32[3,32,256]{2,1,0:T(8,128)S(1)}, u32[]{:S(2)}, u32[]{:S(2)}) collective-permute-start(f32[3,32,256]{2,1,0:T(8,128)S(1)} %get-tuple-element.27), channel_id=1, source_target_pairs={{0,8},{8,16},{16,24},{1,9},{9,17},{17,25},{2,10},{10,18},{18,26},{... | collective-permute-start | bytes 294920 | tf_op jit(solution)/shard_map/ppermute | solution.py:693
  40.4 0.7 pad_add_fusion.kinds_ref
  41.1 0.2 collective-permute-done.2.yb_ref
  41.3 0.9 collective-permute-done.1.xa_ref
  42.3 0.7 copy-done.1
  42.9 46.3 %shard_map.267 = (f32[3,256,32,256]{3,2,1,0:T(8,128)}, f32[32,256,256]{2,1,0:T(8,128)}, f32[32,256]{1,0:T(8,128)}, f32[32,256]{1,0:T(8,128)}, f32[256,256]{1,0:T(8,128)}) custom-call(s32[3]{0:T(128)} %pad_add_fusion.kinds_ref, f32[4,256,32,256]{3,2,1,0:T(8,128)} %get-tuple-element.14.main_ref.prev_ref.next_ref, ...), custom_call_target="tpu_custom_call" | custom-call | tf_op jit(solution)/shard_map/pallas_call | solution.py:318
  89.3 16.8 %shard_map.268 = (f32[32,256,256]{2,1,0:T(8,128)}, f32[3,32,512]{2,1,0:T(8,128)}) custom-call(s32[3]{0:T(128)} %pad_add_fusion.kinds_ref, f32[32,256,256]{2,1,0:T(8,128)} %get-tuple-element.17.modes_ref, bf16[3,256,768]{2,1,0:T(8,128)(2,1)} %constant.79.clone.yt_ref, bf16[3,768,256]{2,1,0:T(8,128)(2,1)} %constant.80.clone.ytr_ref.xt_ref, ...), custom_call_target="tpu_custom_call" | custom-call | tf_op jit(solution)/shard_map/pallas_call | solution.py:399
  106.1 1.1 copy.46
  107.2 19.7 %all_to_all.10 = f32[3,32,512]{2,0,1:T(4,128)S(1)} all-to-all(f32[3,32,512]{2,0,1:T(4,128)S(1)} %copy.46), channel_id=1, replica_groups=mesh['pa'=4,'pb'=8] {'pa','pb'}, dimensions={1} | all-to-all | bytes 393216 | tf_op jit(solution)/shard_map/all_to_all | solution.py:714
  126.9 0.1 fusion.3
  127.0 0.1 fusion.4
  127.2 0.6 pad.12.lines_x_ref
  127.9 0.6 rev.6
  128.5 0.7 pad_maximum_fusion.lines_y_ref
  129.2 16.2 %shard_map.269 = (f32[16,1024]{1,0:T(8,128)}, f32[2,16,1024]{2,1,0:T(8,128)}) custom-call(s32[3]{0:T(128)} %pad_add_fusion.kinds_ref, f32[16,1024]{1,0:T(8,128)} %pad.12.lines_x_ref, f32[2,16,1024]{2,1,0:T(8,128)} %pad_maximum_fusion.lines_y_ref, f32[2,16,2048]{2,1,0:T(8,128)} %constant.87.clone.picks_x_ref, f32[2,16,1024]{2,1,0:T(8,128)} %constant.88.clone.picks_y_ref, ...), custom_call_target="tpu_custom_call" | custom-call | tf_op jit(solution)/shard_map/pallas_call | solution.py:651
  145.4 0.8 add_bitcast_fusion.1
  146.2 0.8 slice_add_fusion
  146.9 0.8 slice_select_fusion
  147.9 0.7 rev.7
  148.6 0.1 concatenate.52
  148.7 0.1 concatenate.51
  148.8 0.1 maximum_maximum_fusion
  148.9 9.9 %all_to_all.11 = f32[2,32,512]{2,0,1:T(2,128)S(1)} all-to-all(f32[2,32,512]{2,0,1:T(2,128)S(1)} %maximum_maximum_fusion), channel_id=1, replica_groups=mesh['pa'=4,'pb'=8] {'pa','pb'}, dimensions={1} | all-to-all | bytes 262144 | tf_op jit(solution)/shard_map/all_to_all | solution.py:741
  158.8 0.7 copy.55
  159.5 17.0 %shard_map.270.modes_ref.after_ref = f32[32,256,256]{2,1,0:T(8,128)} custom-call(s32[3]{0:T(128)} %pad_add_fusion.kinds_ref, f32[32,256,256]{2,1,0:T(8,128)} %get-tuple-element.21.spectrum_ref, f32[64,512]{1,0:T(8,128)} %bitcast.41, bf16[3,256,768]{2,1,0:T(8,128)(2,1)} %constant.77.clone.y_ref, bf16[3,768,256]{2,1,0:T(8,128)(2,1)} %constant.78.clone.sine_ref.yr_ref.x_ref, ...), custom_call_target="tpu_custom_call" | custom-call | tf_op jit(solution)/shard_map/pallas_call | solution.py:467
  176.4 31.2 %shard_map.271 = (f32[3,64,32,1024]{3,2,1,0:T(8,128)}, f32[64,32,1024]{2,1,0:T(8,128)}) custom-call(s32[64]{0:T(128)} %select_reduce_fusion.inverse_ref, s32[3]{0:T(128)} %pad_add_fusion.kinds_ref, f32[32,256,256]{2,1,0:T(8,128)} %shard_map.270.modes_ref.after_ref, f32[32,256,256]{2,1,0:T(8,128)} %shard_map.270.modes_ref.after_ref, ...), custom_call_target="tpu_custom_call" | custom-call | tf_op jit(solution)/shard_map/pallas_call | solution.py:592
  (30 shorter events, 0.3 us)
Async XLA Ops:
  28.9 12.4 %collective-permute-start = (f32[3,32,512]{2,1,0:T(8,128)}, f32[3,32,512]{2,1,0:T(8,128)S(1)}, u32[]{:S(2)}, u32[]{:S(2)}) collective-permute-start(f32[3,32,512]{2,1,0:T(8,128)} %get-tuple-element.15), channel_id=1, source_target_pairs={{0,1},{1,2},{2,3},{3,4},{4,5},{5,6},{6,7},{8,9},{9,10},{10,11},{11... | collective-permute-start | bytes 589832 | tf_op jit(solution)/shard_map/ppermute | solution.py:693
  33.8 8.5 %collective-permute-start.1 = (f32[3,32,512]{2,1,0:T(8,128)}, f32[3,32,512]{2,1,0:T(8,128)S(1)}, u32[]{:S(2)}, u32[]{:S(2)}) collective-permute-start(f32[3,32,512]{2,1,0:T(8,128)} %get-tuple-element.16), channel_id=1, source_target_pairs={{1,0},{2,1},{3,2},{4,3},{5,4},{6,5},{7,6},{9,8},{10,9},{11,10},{12... | collective-permute-start | bytes 589832 | tf_op jit(solution)/shard_map/ppermute | solution.py:696
  36.0 5.0 %collective-permute-start.3 = (f32[3,32,256]{2,1,0:T(8,128)S(1)}, f32[3,32,256]{2,1,0:T(8,128)S(1)}, u32[]{:S(2)}, u32[]{:S(2)}) collective-permute-start(f32[3,32,256]{2,1,0:T(8,128)S(1)} %get-tuple-element.26), channel_id=1, source_target_pairs={{8,0},{16,8},{24,16},{9,1},{17,9},{25,17},{10,2},{18,10},{26,18},{... | collective-permute-start | bytes 294920 | tf_op jit(solution)/shard_map/ppermute | solution.py:696
  37.3 4.0 %collective-permute-start.2 = (f32[3,32,256]{2,1,0:T(8,128)S(1)}, f32[3,32,256]{2,1,0:T(8,128)S(1)}, u32[]{:S(2)}, u32[]{:S(2)}) collective-permute-start(f32[3,32,256]{2,1,0:T(8,128)S(1)} %get-tuple-element.27), channel_id=1, source_target_pairs={{0,8},{8,16},{16,24},{1,9},{9,17},{17,25},{2,10},{10,18},{18,26},{... | collective-permute-start | bytes 294920 | tf_op jit(solution)/shard_map/ppermute | solution.py:693
  41.1 1.2 copy-start.2
  41.3 0.9 copy-start.3
  41.3 0.9 copy-start
  42.3 0.7 copy-start.1
  126.9 20.0 %copy-start.4 = (pred[8]{0:T(512)(128)(4,1)S(1)}, pred[8]{0:T(512)(128)(4,1)}, u32[]{:S(2)}) copy-start(pred[8]{0:T(512)(128)(4,1)} %constant.75.clone.1) | copy-start | bytes 28

commit v6 on v5

--- a/solution.py
+++ b/solution.py
@@ -212,8 +212,6 @@
         first_layer, last_layer = layers == 0, layers == NZ - 1
         first_lane, last_lane = lanes == 0, lanes == LANES - 1
 
-        rows_ref[:, 1 : B + 1] = main_ref[:3]
-
         @pl.when(step == 0)
         def _():
             rows_ref[:, 0] = yb_ref[...]
@@ -225,15 +223,24 @@
 
         @pl.when(step == steps - 1)
         def _():
-            rows_ref[:, B + 1] = ya_ref[...]
+            rows_ref[:, 1] = ya_ref[...]
 
         @pl.when(step < steps - 1)
         def _():
-            rows_ref[:, B + 1] = next_ref[:3, 0]
+            rows_ref[:, 1] = next_ref[:3, 0]
 
         y_chunk = pl.ds(pl.multiple_of(step // 4 * LANES, LANES), LANES)
         halo_chunk = pl.ds(pl.multiple_of(step // 2 * LANES, LANES), LANES)
         even_lane = (lanes & 1) == 0
+
+        def neighbour_row(group, r, c, part):
+            if 0 <= r < 8:
+                return main_ref[c, group * 8 + r, :, part]
+            if r < 0:
+                inside = main_ref[c, jnp.maximum(group * 8 - 1, 0), :, part]
+                return jnp.where(group == 0, rows_ref[c, 0, :, part], inside)
+            inside = main_ref[c, jnp.minimum(group * 8 + 8, B - 1), :, part]
+            return jnp.where(group == B // 8 - 1, rows_ref[c, 1, :, part], inside)
 
         def row(group, r):
             j = group * 8 + r
@@ -243,7 +250,7 @@
             flow = {}
             for h in range(chunks):
                 for c in range(3):
-                    flow[c, h] = rows_ref[c, j + 1, :, h * LANES : (h + 1) * LANES]
+                    flow[c, h] = main_ref[c, j, :, h * LANES : (h + 1) * LANES]
             edge, to_right, to_left = {}, {}, {}
             for c in range(3):
                 both = jnp.where(even_lane, xb_ref[c, :, halo_chunk], xa_ref[c, :, halo_chunk])
@@ -265,8 +272,8 @@
                     after = edge[c] if h == chunks - 1 else to_left[c, h + 1]
                     x_low = jnp.where(first_lane, before, to_right[c, h])
                     x_up = jnp.where(last_lane, after, to_left[c, h])
-                    y_low = rows_ref[c, j, :, part]
-                    y_up = rows_ref[c, j + 2, :, part]
+                    y_low = neighbour_row(group, r - 1, c, part)
+                    y_up = neighbour_row(group, r + 1, c, part)
                     z_low = jnp.where(first_layer, 0.0, pltpu.roll(center, 1, 0))
                     z_up = jnp.where(last_layer, 0.0, pltpu.roll(center, NZ - 1, 0))
                     total = (
@@ -339,7 +346,7 @@
                 pl.BlockSpec((B, x_span), lambda s, kinds: (s, 0)),
             ],
             scratch_shapes=[
-                pltpu.VMEM((3, B + 2, NZ, x_span), f32),
+                pltpu.VMEM((3, 2, NZ, x_span), f32),
                 pltpu.VMEM((B, NZ, x_span), f32),
                 pltpu.VMEM((NZ, x_span), f32),
             ],

time: 209 us -> 207 us (level)
  no operation moved by 1% of the time
where the time goes in v6:
time: 207 us
  Pallas kernels  153 us (74%)
  blocking collectives  29.6 us (14%)
  starting transfers between devices  10.5 us (5%)
  local copies, waits for them, and re-layouts  5.75 us (3%)
  other arithmetic  5.3 us (3%)
    pallas_call x1, Pallas kernels, advance(): pl.pallas_call(kernel, grid_spec=pltpu.PrefetchScalarGridSpec(num_scalar_...  45.2 us
    pallas_call x1, Pallas kernels, finish(): pl.pallas_call(kernel, grid_spec=pltpu.PrefetchScalarGridSpec(num_scalar_...  31.2 us
    pallas_call x1, Pallas kernels, gather_tile(): pl.pallas_call(kernel, grid_spec=pltpu.PrefetchScalarGridSpec(num_scalar_...  26.9 us
    all_to_all x1, blocking collectives, shards(): lax.all_to_all(bundle, ('pa', 'pb'), split_axis=1, concat_axis=1, tiled=T...  19.7 us
    pallas_call x1, Pallas kernels, second_solve(): pl.pallas_call(kernel, grid_spec=pltpu.PrefetchScalarGridSpec(num_scalar_...  16.9 us
    pallas_call x1, Pallas kernels, first_solve(): pl.pallas_call(kernel, grid_spec=pltpu.PrefetchScalarGridSpec(num_scalar_...  16.8 us
    pallas_call x1, Pallas kernels, solve_interfaces(): pl.pallas_call(kernel, grid_spec=pltpu.PrefetchScalarGridSpec(num_scalar_...  16.2 us
    all_to_all x1, blocking collectives, shards(): lax.all_to_all(reply, ('pa', 'pb'), split_axis=1, concat_axis=1, tiled=True)  9.9 us
  transfers between devices with their start and end apart: 4, of which 2 were waited for; matrix products, arithmetic and copies ran while one was open for 1% of the time, Pallas kernels for 0%

profile of v6, /device:TPU:0, one launch (start us, length us, event | category | flops | bytes accessed | tf_op | source)
XLA Modules:
  0.0 206.6 jit_solution(2104714970801056138)
XLA Ops:
  0.6 1.4 select_reduce_fusion.inverse_ref
  2.0 26.9 %shard_map.266 = (f32[4,256,32,256]{3,2,1,0:T(8,128)}, f32[3,32,512]{2,1,0:T(8,128)}, f32[3,32,512]{2,1,0:T(8,128)}) custom-call(s32[64]{0:T(128)} %select_reduce_fusion.inverse_ref, f32[3,64,32,1024]{3,2,1,0:T(8,128)} %refs_7_.1, f32[3,64,32,1024]{3,2,1,0:T(8,128)} %refs_7_.1, f32[3,64,32,1024]{3,2,1,0:T(8,128)} %refs_7_.1, f32[3,64,32,1024]{3,2,1,0:T(8,128)} %refs_7_.1, ...), custom_call_target="tpu_custom_call" | custom-call | tf_op jit(solution)/shard_map/pallas_call | solution.py:185
  28.9 4.9 %collective-permute-start = (f32[3,32,512]{2,1,0:T(8,128)}, f32[3,32,512]{2,1,0:T(8,128)S(1)}, u32[]{:S(2)}, u32[]{:S(2)}) collective-permute-start(f32[3,32,512]{2,1,0:T(8,128)} %get-tuple-element.15), channel_id=1, source_target_pairs={{0,1},{1,2},{2,3},{3,4},{4,5},{5,6},{6,7},{8,9},{9,10},{10,11},{11... | collective-permute-start | bytes 589832 | tf_op jit(solution)/shard_map/ppermute | solution.py:700
  33.8 1.3 collective-permute-start.1
  35.1 1.0 slice_bitcast_fusion
  36.0 1.3 collective-permute-start.3
  37.3 3.0 %collective-permute-start.2 = (f32[3,32,256]{2,1,0:T(8,128)S(1)}, f32[3,32,256]{2,1,0:T(8,128)S(1)}, u32[]{:S(2)}, u32[]{:S(2)}) collective-permute-start(f32[3,32,256]{2,1,0:T(8,128)S(1)} %get-tuple-element.27), channel_id=1, source_target_pairs={{0,8},{8,16},{16,24},{1,9},{9,17},{17,25},{2,10},{10,18},{18,26},{... | collective-permute-start | bytes 294920 | tf_op jit(solution)/shard_map/ppermute | solution.py:700
  40.4 0.7 pad_add_fusion.kinds_ref
  41.1 0.2 collective-permute-done.2.yb_ref
  41.3 0.9 collective-permute-done.1.xa_ref
  42.3 0.7 copy-done.1
  42.9 45.2 %shard_map.267 = (f32[3,256,32,256]{3,2,1,0:T(8,128)}, f32[32,256,256]{2,1,0:T(8,128)}, f32[32,256]{1,0:T(8,128)}, f32[32,256]{1,0:T(8,128)}, f32[256,256]{1,0:T(8,128)}) custom-call(s32[3]{0:T(128)} %pad_add_fusion.kinds_ref, f32[4,256,32,256]{3,2,1,0:T(8,128)} %get-tuple-element.14.main_ref.prev_ref.next_ref, ...), custom_call_target="tpu_custom_call" | custom-call | tf_op jit(solution)/shard_map/pallas_call | solution.py:325
  88.1 16.8 %shard_map.268 = (f32[32,256,256]{2,1,0:T(8,128)}, f32[3,32,512]{2,1,0:T(8,128)}) custom-call(s32[3]{0:T(128)} %pad_add_fusion.kinds_ref, f32[32,256,256]{2,1,0:T(8,128)} %get-tuple-element.17.modes_ref, bf16[3,256,768]{2,1,0:T(8,128)(2,1)} %constant.79.clone.yt_ref, bf16[3,768,256]{2,1,0:T(8,128)(2,1)} %constant.80.clone.ytr_ref.xt_ref, ...), custom_call_target="tpu_custom_call" | custom-call | tf_op jit(solution)/shard_map/pallas_call | solution.py:406
  105.0 1.1 copy.46
  106.0 19.7 %all_to_all.10 = f32[3,32,512]{2,0,1:T(4,128)S(1)} all-to-all(f32[3,32,512]{2,0,1:T(4,128)S(1)} %copy.46), channel_id=1, replica_groups=mesh['pa'=4,'pb'=8] {'pa','pb'}, dimensions={1} | all-to-all | bytes 393216 | tf_op jit(solution)/shard_map/all_to_all | solution.py:721
  125.8 0.1 fusion.3
  125.8 0.1 fusion.4
  126.1 0.6 pad.12.lines_x_ref
  126.8 0.6 rev.6
  127.4 0.7 pad_maximum_fusion.lines_y_ref
  128.0 16.2 %shard_map.269 = (f32[16,1024]{1,0:T(8,128)}, f32[2,16,1024]{2,1,0:T(8,128)}) custom-call(s32[3]{0:T(128)} %pad_add_fusion.kinds_ref, f32[16,1024]{1,0:T(8,128)} %pad.12.lines_x_ref, f32[2,16,1024]{2,1,0:T(8,128)} %pad_maximum_fusion.lines_y_ref, f32[2,16,2048]{2,1,0:T(8,128)} %constant.87.clone.picks_x_ref, f32[2,16,1024]{2,1,0:T(8,128)} %constant.88.clone.picks_y_ref, ...), custom_call_target="tpu_custom_call" | custom-call | tf_op jit(solution)/shard_map/pallas_call | solution.py:658
  144.2 0.8 add_bitcast_fusion.1
  145.0 0.8 slice_add_fusion
  145.8 0.8 slice_select_fusion
  146.7 0.7 rev.7
  147.5 0.1 concatenate.52
  147.5 0.1 concatenate.51
  147.6 0.1 maximum_maximum_fusion
  147.7 9.9 %all_to_all.11 = f32[2,32,512]{2,0,1:T(2,128)S(1)} all-to-all(f32[2,32,512]{2,0,1:T(2,128)S(1)} %maximum_maximum_fusion), channel_id=1, replica_groups=mesh['pa'=4,'pb'=8] {'pa','pb'}, dimensions={1} | all-to-all | bytes 262144 | tf_op jit(solution)/shard_map/all_to_all | solution.py:748
  157.6 0.7 copy.55
  158.3 16.9 %shard_map.270.modes_ref.after_ref = f32[32,256,256]{2,1,0:T(8,128)} custom-call(s32[3]{0:T(128)} %pad_add_fusion.kinds_ref, f32[32,256,256]{2,1,0:T(8,128)} %get-tuple-element.21.spectrum_ref, f32[64,512]{1,0:T(8,128)} %bitcast.41, bf16[3,256,768]{2,1,0:T(8,128)(2,1)} %constant.77.clone.y_ref, bf16[3,768,256]{2,1,0:T(8,128)(2,1)} %constant.78.clone.sine_ref.yr_ref.x_ref, ...), custom_call_target="tpu_custom_call" | custom-call | tf_op jit(solution)/shard_map/pallas_call | solution.py:474
  175.3 31.2 %shard_map.271 = (f32[3,64,32,1024]{3,2,1,0:T(8,128)}, f32[64,32,1024]{2,1,0:T(8,128)}) custom-call(s32[64]{0:T(128)} %select_reduce_fusion.inverse_ref, s32[3]{0:T(128)} %pad_add_fusion.kinds_ref, f32[32,256,256]{2,1,0:T(8,128)} %shard_map.270.modes_ref.after_ref, f32[32,256,256]{2,1,0:T(8,128)} %shard_map.270.modes_ref.after_ref, ...), custom_call_target="tpu_custom_call" | custom-call | tf_op jit(solution)/shard_map/pallas_call | solution.py:599
  (30 shorter events, 0.3 us)
Async XLA Ops:
  28.9 12.4 %collective-permute-start = (f32[3,32,512]{2,1,0:T(8,128)}, f32[3,32,512]{2,1,0:T(8,128)S(1)}, u32[]{:S(2)}, u32[]{:S(2)}) collective-permute-start(f32[3,32,512]{2,1,0:T(8,128)} %get-tuple-element.15), channel_id=1, source_target_pairs={{0,1},{1,2},{2,3},{3,4},{4,5},{5,6},{6,7},{8,9},{9,10},{10,11},{11... | collective-permute-start | bytes 589832 | tf_op jit(solution)/shard_map/ppermute | solution.py:700
  33.8 8.5 %collective-permute-start.1 = (f32[3,32,512]{2,1,0:T(8,128)}, f32[3,32,512]{2,1,0:T(8,128)S(1)}, u32[]{:S(2)}, u32[]{:S(2)}) collective-permute-start(f32[3,32,512]{2,1,0:T(8,128)} %get-tuple-element.16), channel_id=1, source_target_pairs={{1,0},{2,1},{3,2},{4,3},{5,4},{6,5},{7,6},{9,8},{10,9},{11,10},{12... | collective-permute-start | bytes 589832 | tf_op jit(solution)/shard_map/ppermute | solution.py:703
  36.0 5.0 %collective-permute-start.3 = (f32[3,32,256]{2,1,0:T(8,128)S(1)}, f32[3,32,256]{2,1,0:T(8,128)S(1)}, u32[]{:S(2)}, u32[]{:S(2)}) collective-permute-start(f32[3,32,256]{2,1,0:T(8,128)S(1)} %get-tuple-element.26), channel_id=1, source_target_pairs={{8,0},{16,8},{24,16},{9,1},{17,9},{25,17},{10,2},{18,10},{26,18},{... | collective-permute-start | bytes 294920 | tf_op jit(solution)/shard_map/ppermute | solution.py:703
  37.3 4.0 %collective-permute-start.2 = (f32[3,32,256]{2,1,0:T(8,128)S(1)}, f32[3,32,256]{2,1,0:T(8,128)S(1)}, u32[]{:S(2)}, u32[]{:S(2)}) collective-permute-start(f32[3,32,256]{2,1,0:T(8,128)S(1)} %get-tuple-element.27), channel_id=1, source_target_pairs={{0,8},{8,16},{16,24},{1,9},{9,17},{17,25},{2,10},{10,18},{18,26},{... | collective-permute-start | bytes 294920 | tf_op jit(solution)/shard_map/ppermute | solution.py:700
  41.1 1.2 copy-start.2
  41.3 0.9 copy-start.3
  41.3 0.9 copy-start
  42.3 0.7 copy-start.1
  125.7 20.0 %copy-start.4 = (pred[8]{0:T(512)(128)(4,1)S(1)}, pred[8]{0:T(512)(128)(4,1)}, u32[]{:S(2)}) copy-start(pred[8]{0:T(512)(128)(4,1)} %constant.75.clone.1) | copy-start | bytes 28

commit v7 on v6

--- a/solution.py
+++ b/solution.py
@@ -16,7 +16,7 @@
 LANES = 128
 highest = lax.Precision.HIGHEST
 f32 = jnp.float32
-VMEM_LIMIT = 56 * 1024 * 1024
+VMEM_LIMIT = 34 * 1024 * 1024
 
 
 def cosine_basis():

time: 207 us -> 227 us (1.097)
  local copies, waits for them, and re-layouts: 5.75 us -> 39.2 us
  Pallas kernels: 153 us -> 139 us
    unnamed x17 -> x63, local copies, waits for them, and re-layouts: 0.77 us -> 23.6 us
    pallas_call x1, Pallas kernels: 16.2 us -> 10.8 us  [solve_interfaces(): pl.pallas_call(kernel, grid_spec=pltpu.PrefetchScalarGridSpec(num_scalar_...]
    rev x1, local copies, waits for them, and re-layouts: 0.72 us -> 4.19 us  [shards(): sum_y = jnp.concatenate([even + odd, (even - odd)[:, ::-1]], axis=1)]
    pallas_call x1, Pallas kernels: 26.9 us -> 23.9 us  [gather_tile(): pl.pallas_call(kernel, grid_spec=pltpu.PrefetchScalarGridSpec(num_scalar_...]
    pallas_call x1, Pallas kernels: 16.8 us -> 13.9 us  [first_solve(): pl.pallas_call(kernel, grid_spec=pltpu.PrefetchScalarGridSpec(num_scalar_...]
    concatenate x2, local copies, waits for them, and re-layouts: 0.09 us -> 2.81 us  [shards(): jnp.concatenate([low_y, low_x], axis=2)]
    concatenate x2, local copies, waits for them, and re-layouts: 0.09 us -> 2.8 us  [shards(): jnp.concatenate([high_y, high_x], axis=2)]
    pallas_call x1, Pallas kernels: 16.9 us -> 14.6 us  [second_solve(): pl.pallas_call(kernel, grid_spec=pltpu.PrefetchScalarGridSpec(num_scalar_...]
where the time goes in v7:
time: 227 us; the launch traced here: 226 us
  Pallas kernels  139 us (61%)
  local copies, waits for them, and re-layouts  39.2 us (17%)
  blocking collectives  29.7 us (13%)
  starting transfers between devices  10.4 us (5%)
  other arithmetic  4.56 us (2%)
    pallas_call x1, Pallas kernels, advance(): pl.pallas_call(kernel, grid_spec=pltpu.PrefetchScalarGridSpec(num_scalar_...  47 us
    pallas_call x1, Pallas kernels, finish(): pl.pallas_call(kernel, grid_spec=pltpu.PrefetchScalarGridSpec(num_scalar_...  29.1 us
    pallas_call x1, Pallas kernels, gather_tile(): pl.pallas_call(kernel, grid_spec=pltpu.PrefetchScalarGridSpec(num_scalar_...  23.9 us
    unnamed x63, local copies, waits for them, and re-layouts  23.6 us
    all_to_all x1, blocking collectives, shards(): lax.all_to_all(bundle, ('pa', 'pb'), split_axis=1, concat_axis=1, tiled=T...  19.8 us
    pallas_call x1, Pallas kernels, second_solve(): pl.pallas_call(kernel, grid_spec=pltpu.PrefetchScalarGridSpec(num_scalar_...  14.6 us
    pallas_call x1, Pallas kernels, first_solve(): pl.pallas_call(kernel, grid_spec=pltpu.PrefetchScalarGridSpec(num_scalar_...  13.9 us
    pallas_call x1, Pallas kernels, solve_interfaces(): pl.pallas_call(kernel, grid_spec=pltpu.PrefetchScalarGridSpec(num_scalar_...  10.8 us
  transfers between devices with their start and end apart: 4, of which 2 were waited for; matrix products, arithmetic and copies ran while one was open for 1% of the time, Pallas kernels for 0%

profile of v7, /device:TPU:0, one launch (start us, length us, event | category | flops | bytes accessed | tf_op | source)
XLA Modules:
  0.0 225.7 jit_solution(14751916277517277242)
XLA Ops:
  1.4 3.4 %copy-done = f32[64,32,1024]{2,1,0:T(8,128)S(1)} copy-done((f32[64,32,1024]{2,1,0:T(8,128)S(1)}, f32[64,32,1024]{2,1,0:T(8,128)}, u32[]{:S(2)}) %copy-start) | copy-done | bytes 8388632
  4.8 23.9 %shard_map.266 = (f32[4,256,32,256]{3,2,1,0:T(8,128)}, f32[3,32,512]{2,1,0:T(8,128)S(1)}, f32[3,32,512]{2,1,0:T(8,128)}) custom-call(s32[64]{0:T(128)S(1)} %select_reduce_fusion.inverse_ref, f32[3,64,32,1024]{3,2,1,0:T(8,128)} %refs_7_.1, f32[3,64,32,1024]{3,2,1,0:T(8,128)} %refs_7_.1, f32[3,64,32,1024]{3,2,1,0:T(8,128)} %refs_7_.1, ...), custom_call_target="tpu_custom_call" | custom-call | tf_op jit(solution)/shard_map/pallas_call | solution.py:185
  28.7 4.8 %collective-permute-start = (f32[3,32,512]{2,1,0:T(8,128)}, f32[3,32,512]{2,1,0:T(8,128)S(1)}, u32[]{:S(2)}, u32[]{:S(2)}) collective-permute-start(f32[3,32,512]{2,1,0:T(8,128)} %get-tuple-element.15), channel_id=1, source_target_pairs={{0,1},{1,2},{2,3},{3,4},{4,5},{5,6},{6,7},{8,9},{9,10},{10,11},{11... | collective-permute-start | bytes 589832 | tf_op jit(solution)/shard_map/ppermute | solution.py:700
  33.6 1.3 collective-permute-start.1
  34.9 1.6 slice_bitcast_fusion
  36.5 1.3 collective-permute-start.3
  37.8 3.0 %collective-permute-start.2 = (f32[3,32,256]{2,1,0:T(8,128)}, f32[3,32,256]{2,1,0:T(8,128)S(1)}, u32[]{:S(2)}, u32[]{:S(2)}) collective-permute-start(f32[3,32,256]{2,1,0:T(8,128)} %get-tuple-element.27), channel_id=1, source_target_pairs={{0,8},{8,16},{16,24},{1,9},{9,17},{17,25},{2,10},{10,18},{18,26},{... | collective-permute-start | bytes 294920 | tf_op jit(solution)/shard_map/ppermute | solution.py:700
  41.0 1.0 collective-permute-done.2.yb_ref
  42.3 47.0 %shard_map.267 = (f32[3,256,32,256]{3,2,1,0:T(8,128)}, f32[32,256,256]{2,1,0:T(8,128)S(1)}, f32[32,256]{1,0:T(8,128)S(1)}, f32[32,256]{1,0:T(8,128)S(1)}, f32[256,256]{1,0:T(8,128)S(1)}) custom-call(s32[3]{0:T(128)S(1)} %pad_add_fusion.kinds_ref, f32[4,256,32,256]{3,2,1,0:T(8,128)} %get-tuple-element.14.main_ref.prev_ref.next_ref, ...), custom_call_target="tpu_custom_call" | custom-call | tf_op jit(solution)/shard_map/pallas_call | solution.py:325
  89.3 3.4 %copy-done.7 = f32[32,256,256]{2,1,0:T(8,128)} copy-done((f32[32,256,256]{2,1,0:T(8,128)}, f32[32,256,256]{2,1,0:T(8,128)S(1)}, u32[]{:S(2)}) %copy-start.7) | copy-done | bytes 8388632
  92.8 13.9 %shard_map.268 = (f32[32,256,256]{2,1,0:T(8,128)S(1)}, f32[3,32,512]{2,1,0:T(8,128)S(1)}) custom-call(s32[3]{0:T(128)S(1)} %pad_add_fusion.kinds_ref, f32[32,256,256]{2,1,0:T(8,128)} %copy-done.7, bf16[3,256,768]{2,1,0:T(8,128)(2,1)S(1)} %copy-done.10, bf16[3,768,256]{2,1,0:T(8,128)(2,1)S(1)} %copy-done.1, bf16[3,768,256]{2,1,0:T(8,128)(2,1)S(1)} %copy-done.1, ...), custom_call_target="tpu_custom_call" | custom-call | tf_op jit(solution)/shard_map/pallas_call | solution.py:406
  106.7 3.4 %copy-done.5 = f32[32,256,256]{2,1,0:T(8,128)} copy-done((f32[32,256,256]{2,1,0:T(8,128)}, f32[32,256,256]{2,1,0:T(8,128)S(1)}, u32[]{:S(2)}) %copy-start.5) | copy-done | bytes 8388632
  110.2 19.8 %all_to_all.10 = f32[3,32,512]{2,0,1:T(4,128)S(1)} all-to-all(f32[3,32,512]{2,0,1:T(4,128)S(1)} %copy.46), channel_id=1, replica_groups=mesh['pa'=4,'pb'=8] {'pa','pb'}, dimensions={1} | all-to-all | bytes 393216 | tf_op jit(solution)/shard_map/all_to_all | solution.py:721
  132.3 3.4 %copy-done.6 = bf16[2,2,1024,1024]{3,2,1,0:T(8,128)(2,1)S(1)} copy-done((bf16[2,2,1024,1024]{3,2,1,0:T(8,128)(2,1)S(1)}, bf16[2,2,1024,1024]{3,2,1,0:T(8,128)(2,1)}, u32[]{:S(2)}) %copy-start.6) | copy-done | bytes 8388632
  135.6 2.2 copy-done.8
  137.8 1.2 copy-done.11
  139.1 0.9 copy-done.16
  140.0 0.8 copy-done.17
  140.8 0.9 copy-done.19
  142.5 10.8 %shard_map.269 = (f32[16,1024]{1,0:T(8,128)S(1)}, f32[2,16,1024]{2,1,0:T(8,128)S(1)}) custom-call(s32[3]{0:T(128)S(1)} %pad_add_fusion.kinds_ref, f32[16,1024]{1,0:T(8,128)S(1)} %copy-done.17, f32[2,16,1024]{2,1,0:T(8,128)S(1)} %pad_maximum_fusion.lines_y_ref, f32[2,16,2048]{2,1,0:T(8,128)S(1)} %copy-done.16, f32[2,16,1024]{2,1,0:T(8,128)S(1)} %copy-done.19, ...), custom_call_target="tpu_custom_call" | custom-call | tf_op jit(solution)/shard_map/pallas_call | solution.py:658
  155.2 1.4 concatenate.49
  156.6 1.4 concatenate.43
  158.0 1.4 concatenate.44
  159.4 4.2 %rev.7 = f32[3,1024]{1,0:T(4,128)} reverse(f32[3,1024]{1,0:T(4,128)} %get-tuple-element.37), dimensions={1} | reverse | bytes 24576 | tf_op jit(solution)/shard_map/rev | solution.py:739
  165.6 1.4 concatenate.52
  167.0 1.4 concatenate.51
  168.4 0.9 maximum_maximum_fusion
  169.4 9.9 %all_to_all.11 = f32[2,32,512]{2,0,1:T(2,128)S(1)} all-to-all(f32[2,32,512]{2,0,1:T(2,128)S(1)} %maximum_maximum_fusion), channel_id=1, replica_groups=mesh['pa'=4,'pb'=8] {'pa','pb'}, dimensions={1} | all-to-all | bytes 262144 | tf_op jit(solution)/shard_map/all_to_all | solution.py:748
  179.3 1.7 copy-done.4
  181.0 0.8 copy-done.18
  181.8 14.6 %shard_map.270.modes_ref.after_ref = f32[32,256,256]{2,1,0:T(8,128)S(1)} custom-call(s32[3]{0:T(128)S(1)} %pad_add_fusion.kinds_ref, f32[32,256,256]{2,1,0:T(8,128)} %copy-done.5, f32[64,512]{1,0:T(8,128)S(1)} %bitcast.41, bf16[3,256,768]{2,1,0:T(8,128)(2,1)S(1)} %copy-done.9, bf16[3,768,256]{2,1,0:T(8,128)(2,1)S(1)} %copy-done.2, ...), custom_call_target="tpu_custom_call" | custom-call | tf_op jit(solution)/shard_map/pallas_call | solution.py:474
  196.4 29.1 %shard_map.271 = (f32[3,64,32,1024]{3,2,1,0:T(8,128)}, f32[64,32,1024]{2,1,0:T(8,128)}) custom-call(s32[64]{0:T(128)S(1)} %select_reduce_fusion.inverse_ref, s32[3]{0:T(128)S(1)} %pad_add_fusion.kinds_ref, f32[32,256,256]{2,1,0:T(8,128)S(1)} %shard_map.270.modes_ref.after_ref, f32[32,256,256]{2,1,0:T(8,128)S(1)} %shard_map.270.modes_ref.after_ref, ...), custom_call_target="tpu_custom_call" | custom-call | tf_op jit(solution)/shard_map/pallas_call | solution.py:599
  (76 shorter events, 8.2 us)
Async XLA Ops:
  1.4 3.4 %copy-start = (f32[64,32,1024]{2,1,0:T(8,128)S(1)}, f32[64,32,1024]{2,1,0:T(8,128)}, u32[]{:S(2)}) copy-start(f32[64,32,1024]{2,1,0:T(8,128)} %refs_15_.1) | copy-start | bytes 25165828
  4.8 37.5 %copy-start.2 = (bf16[3,768,256]{2,1,0:T(8,128)(2,1)S(1)}, bf16[3,768,256]{2,1,0:T(8,128)(2,1)}, u32[]{:S(2)}) copy-start(bf16[3,768,256]{2,1,0:T(8,128)(2,1)} %constant.78.clone.sine_ref.yr_ref.x_ref) | copy-start | bytes 3538948
  4.8 37.5 %copy-start.15 = (bf16[256,768]{1,0:T(8,128)(2,1)S(1)}, bf16[256,768]{1,0:T(8,128)(2,1)}, u32[]{:S(2)}) copy-start(bf16[256,768]{1,0:T(8,128)(2,1)} %constant.93.clone.cosine_ref) | copy-start | bytes 1179652
  28.7 13.5 %collective-permute-start = (f32[3,32,512]{2,1,0:T(8,128)}, f32[3,32,512]{2,1,0:T(8,128)S(1)}, u32[]{:S(2)}, u32[]{:S(2)}) collective-permute-start(f32[3,32,512]{2,1,0:T(8,128)} %get-tuple-element.15), channel_id=1, source_target_pairs={{0,1},{1,2},{2,3},{3,4},{4,5},{5,6},{6,7},{8,9},{9,10},{10,11},{11... | collective-permute-start | bytes 589832 | tf_op jit(solution)/shard_map/ppermute | solution.py:700
  33.6 8.7 %collective-permute-start.1 = (f32[3,32,512]{2,1,0:T(8,128)S(1)}, f32[3,32,512]{2,1,0:T(8,128)S(1)}, u32[]{:S(2)}, u32[]{:S(2)}) collective-permute-start(f32[3,32,512]{2,1,0:T(8,128)S(1)} %get-tuple-element.16), channel_id=1, source_target_pairs={{1,0},{2,1},{3,2},{4,3},{5,4},{6,5},{7,6},{9,8},{10,9},{11,10},{12... | collective-permute-start | bytes 589832 | tf_op jit(solution)/shard_map/ppermute | solution.py:703
  36.5 4.5 %collective-permute-start.3 = (f32[3,32,256]{2,1,0:T(8,128)}, f32[3,32,256]{2,1,0:T(8,128)S(1)}, u32[]{:S(2)}, u32[]{:S(2)}) collective-permute-start(f32[3,32,256]{2,1,0:T(8,128)} %get-tuple-element.26), channel_id=1, source_target_pairs={{8,0},{16,8},{24,16},{9,1},{17,9},{25,17},{10,2},{18,10},{26,18},{... | collective-permute-start | bytes 294920 | tf_op jit(solution)/shard_map/ppermute | solution.py:703
  37.8 4.2 %collective-permute-start.2 = (f32[3,32,256]{2,1,0:T(8,128)}, f32[3,32,256]{2,1,0:T(8,128)S(1)}, u32[]{:S(2)}, u32[]{:S(2)}) collective-permute-start(f32[3,32,256]{2,1,0:T(8,128)} %get-tuple-element.27), channel_id=1, source_target_pairs={{0,8},{8,16},{16,24},{1,9},{9,17},{17,25},{2,10},{10,18},{18,26},{... | collective-permute-start | bytes 294920 | tf_op jit(solution)/shard_map/ppermute | solution.py:700
  40.9 51.8 %copy-start.1 = (bf16[3,768,256]{2,1,0:T(8,128)(2,1)S(1)}, bf16[3,768,256]{2,1,0:T(8,128)(2,1)}, u32[]{:S(2)}) copy-start(bf16[3,768,256]{2,1,0:T(8,128)(2,1)} %constant.80.clone.ytr_ref.xt_ref) | copy-start | bytes 3538948
  40.9 51.8 %copy-start.3 = (f32[9,256,256]{2,1,0:T(8,128)S(1)}, f32[9,256,256]{2,1,0:T(8,128)}, u32[]{:S(2)}) copy-start(f32[9,256,256]{2,1,0:T(8,128)} %constant.85.clone.eigen_ref) | copy-start | bytes 7077892
  40.9 51.8 %copy-start.10 = (bf16[3,256,768]{2,1,0:T(8,128)(2,1)S(1)}, bf16[3,256,768]{2,1,0:T(8,128)(2,1)}, u32[]{:S(2)}) copy-start(bf16[3,256,768]{2,1,0:T(8,128)(2,1)} %constant.79.clone.yt_ref) | copy-start | bytes 3538948
  40.9 51.8 %copy-start.12 = (f32[3,256,256]{2,1,0:T(8,128)S(1)}, f32[3,256,256]{2,1,0:T(8,128)}, u32[]{:S(2)}) copy-start(f32[3,256,256]{2,1,0:T(8,128)} %constant.84.clone.exact_x_ref) | copy-start | bytes 2359300
  41.0 51.8 %copy-start.13 = (f32[3,256,256]{2,1,0:T(8,128)S(1)}, f32[3,256,256]{2,1,0:T(8,128)}, u32[]{:S(2)}) copy-start(f32[3,256,256]{2,1,0:T(8,128)} %constant.83.clone.exact_yt_ref) | copy-start | bytes 2359300
  41.0 51.8 %copy-start.20 = (bf16[3,16,256]{2,1,0:T(8,128)(2,1)S(1)}, bf16[3,16,256]{2,1,0:T(8,128)(2,1)}, u32[]{:S(2)}) copy-start(bf16[3,16,256]{2,1,0:T(8,128)(2,1)} %constant.82.clone.edge_y_ref.edge_x_ref) | copy-start | bytes 73732
  41.0 51.8 %copy-start.23 = (f32[32,32]{1,0:T(8,128)S(1)}, f32[32,32]{1,0:T(8,128)}, u32[]{:S(2)}) copy-start(f32[32,32]{1,0:T(8,128)} %constant.76.clone.cosine_ref) | copy-start | bytes 12292
  41.0 51.8 %copy-start.24 = (f32[32]{0:T(128)S(1)}, f32[32]{0:T(128)}, u32[]{:S(2)}) copy-start(f32[32]{0:T(128)} %constant.86.clone.levels_ref) | copy-start | bytes 388
  89.3 3.4 %copy-start.7 = (f32[32,256,256]{2,1,0:T(8,128)}, f32[32,256,256]{2,1,0:T(8,128)S(1)}, u32[]{:S(2)}) copy-start(f32[32,256,256]{2,1,0:T(8,128)S(1)} %get-tuple-element.17.modes_ref) | copy-start | bytes 25165828
  106.7 3.4 %copy-start.5 = (f32[32,256,256]{2,1,0:T(8,128)}, f32[32,256,256]{2,1,0:T(8,128)S(1)}, u32[]{:S(2)}) copy-start(f32[32,256,256]{2,1,0:T(8,128)S(1)} %get-tuple-element.21.spectrum_ref) | copy-start | bytes 25165828
  130.0 24.5 %copy-start.27 = (pred[8]{0:T(512)(128)(4,1)S(1)}, pred[8]{0:T(512)(128)(4,1)}, u32[]{:S(2)}) copy-start(pred[8]{0:T(512)(128)(4,1)} %constant.75.clone.1) | copy-start | bytes 28
  130.2 1.4 copy-start.25
  132.2 21.7 %copy-start.26 = (f32[1,7,4,256]{3,1,2,0:T(8,128)S(1)}, f32[1,7,4,256]{3,1,2,0:T(8,128)}, u32[]{:S(2)}) copy-start(f32[1,7,4,256]{3,1,2,0:T(8,128)} %copy.65) | copy-start | bytes 86020
  132.3 3.4 %copy-start.6 = (bf16[2,2,1024,1024]{3,2,1,0:T(8,128)(2,1)S(1)}, bf16[2,2,1024,1024]{3,2,1,0:T(8,128)(2,1)}, u32[]{:S(2)}) copy-start(bf16[2,2,1024,1024]{3,2,1,0:T(8,128)(2,1)} %constant.89.clone.table_x_ref) | copy-start | bytes 25165828
  135.6 2.2 copy-start.8
  137.8 1.2 copy-start.11
  139.1 0.9 copy-start.16
  140.0 0.8 copy-start.17
  140.8 0.9 copy-start.19
  141.8 0.8 copy-start.21
  142.5 36.8 %copy-start.9 = (bf16[3,256,768]{2,1,0:T(8,128)(2,1)S(1)}, bf16[3,256,768]{2,1,0:T(8,128)(2,1)}, u32[]{:S(2)}) copy-start(bf16[3,256,768]{2,1,0:T(8,128)(2,1)} %constant.77.clone.y_ref) | copy-start | bytes 3538948
  179.3 1.7 copy-start.4
  181.0 0.8 copy-start.18
  181.8 14.6 %copy-start.14 = (bf16[256,768]{1,0:T(8,128)(2,1)S(1)}, bf16[256,768]{1,0:T(8,128)(2,1)}, u32[]{:S(2)}) copy-start(bf16[256,768]{1,0:T(8,128)(2,1)} %constant.95.clone.cosine_ref) | copy-start | bytes 1179652
  181.8 14.6 %copy-start.22 = (f32[32,32]{1,0:T(8,128)S(1)}, f32[32,32]{1,0:T(8,128)}, u32[]{:S(2)}) copy-start(f32[32,32]{1,0:T(8,128)} %constant.94.clone.inverse_cosine_ref) | copy-start | bytes 12292
